TPU v7x, 512 devices: a whole 4x8x8 slice. The times are simulated.
512 devices in a mesh: wide: 64 (over z, x, core), narrow: 8 (over y).
Axes of the slice: x: 4, y: 8, z: 8, core: 2. Of those that a mesh axis runs over, the one named last changes fastest.
Arguments:
- inputs: bfloat16 [5, 192, 8192], P(None, 'wide', 'narrow'), may hold values from -30 to 30
- pre_gain: float32 [8192], P('narrow'), may hold values from 0.1 to 1.9
- w_z: bfloat16 [8192, 16384], P('narrow', 'wide'), may hold values from -0.0625 to 0.0625
- w_x: bfloat16 [8192, 16384], P('narrow', 'wide'), may hold values from -0.0625 to 0.0625
- w_bc: bfloat16 [8192, 4096], P('narrow', 'wide'), may hold values from -0.0625 to 0.0625
- w_dt: bfloat16 [8192, 256], P('narrow', 'wide'), may hold values from -0.0625 to 0.0625
- conv_x_w: float32 [4, 16384], P(None, 'wide'), may hold values from -1 to 1
- conv_bc_w: float32 [4, 4096], P(None, 'wide'), may hold values from -1 to 1
- conv_x_state: bfloat16 [192, 3, 16384], P('narrow', None, 'wide'), may hold values from -5 to 5
- conv_bc_state: bfloat16 [192, 3, 4096], P('narrow', None, 'wide'), may hold values from -5 to 5
- a_log: float32 [256], P('wide'), may hold values from -0.7 to 2
- dt_bias: float32 [256], P('wide'), may hold values from -3 to 0
- skip_d: float32 [256], P('wide'), may hold values from 0.5 to 1.5
- ssm_state: bfloat16 [192, 256, 64, 256], P('narrow', 'wide'), may hold values from -2 to 2
- norm_gain: float32 [16384], P('wide'), may hold values from 0.1 to 1.9
- w_out: bfloat16 [16384, 8192], P('wide', 'narrow'), may hold values from -0.046875 to 0.046875
Outputs:
- mixed: bfloat16 [5, 192, 8192], P(None, 'wide', 'narrow')
All inputs are finite; a program needn't handle non-finite values.
Results may differ from a plain program's by a relative error of at most 0.018.
Values may be sent and summed in bfloat16 or wider, within the bound.
No kernel may reach another device: no remote copies, remote signals or barrier semaphores. Data moves between devices by JAX's collectives and lax.ppermute only.
A program may use at most 64 MiB of HBM per device.

v0:
```python
import jax
import jax.numpy as jnp
from jax import lax
from jax.sharding import PartitionSpec as P

D = 8192
GROUPS = 8
DI = 16384


EPS = 1e-05


def from_partner(x, axis, apart):
    return lax.ppermute(x, axis, [(i, i ^ 1 << apart) for i in range(lax.axis_size(axis))])


def conv_step(history, current, taps):
    window = jnp.concatenate([history, current[:, None, :]], axis=1)
    acc = taps[0] * window[:, 0].astype(jnp.float32)
    for k in range(1, window.shape[1]):
        acc = acc + taps[k] * window[:, k].astype(jnp.float32)
    return (jax.nn.silu(acc), window[:, 1:])


def per_device(
    inputs,
    pre_gain,
    w_z,
    w_x,
    w_bc,
    w_dt,
    conv_x_w,
    conv_bc_w,
    conv_x_state,
    conv_bc_state,
    a_log,
    dt_bias,
    skip_d,
    ssm_state,
    norm_gain,
    w_out,
):
    wide_count = lax.axis_size("wide")
    narrow_count = lax.axis_size("narrow")
    steps = inputs.shape[0]
    rows_dev = inputs.shape[1]
    rows_all = rows_dev * wide_count
    block = rows_all // narrow_count
    width_z = w_z.shape[1]
    width_x = w_x.shape[1]
    width_bc = w_bc.shape[1]
    heads_dev = ssm_state.shape[1]
    head_dim = ssm_state.shape[2]
    weights_in = jnp.concatenate([w_z, w_x, w_bc, w_dt], axis=1)
    per_group = wide_count // GROUPS
    levels = per_group.bit_length() - 1
    my_group = lax.axis_index("wide") // per_group
    group_mask = (jnp.arange(GROUPS)[None, :] == my_group).astype(jnp.float32)
    decay_rate = jnp.exp(a_log)
    state = ssm_state
    history_x = conv_x_state
    history_bc = conv_bc_state
    results = []
    for step in range(steps):
        tokens = inputs[step]
        local = tokens.astype(jnp.float32)
        squares = lax.psum(jnp.sum(local * local, axis=-1), "narrow")
        normed = (local * lax.rsqrt(squares[:, None] / D + EPS) * pre_gain).astype(jnp.bfloat16)
        partial_value = jnp.dot(
            lax.all_gather(normed, "wide", axis=0, tiled=True),
            weights_in,
            preferred_element_type=jnp.float32,
        ).astype(jnp.bfloat16)
        mine = (
            lax.psum_scatter(partial_value, "narrow", scatter_dimension=0, tiled=True)
            .astype(jnp.float32)
            .astype(jnp.bfloat16)
        )
        gate_raw = mine[:, :width_z]
        head_raw = mine[:, width_z : width_z + width_x]
        state_raw = mine[:, width_z + width_x : width_z + width_x + width_bc]
        step_raw = mine[:, width_z + width_x + width_bc :]
        head_conv, history_x = conv_step(history_x, head_raw, conv_x_w)
        state_conv, history_bc = conv_step(history_bc, state_raw, conv_bc_w)
        shared = state_conv.astype(jnp.bfloat16)
        for level in range(levels):
            other = from_partner(shared, "wide", level)
            upper = lax.axis_index("wide") // (1 << level) % 2 == 1
            shared = jnp.where(
                upper,
                jnp.concatenate([other, shared], axis=1),
                jnp.concatenate([shared, other], axis=1),
            )
        half = shared.shape[1] // 2
        b_vec = shared[:, :half].astype(jnp.float32)
        c_vec = shared[:, half:].astype(jnp.float32)
        step_size = jax.nn.softplus(step_raw.astype(jnp.float32) + dt_bias)
        decay = jnp.exp(-step_size * decay_rate)
        inner = head_conv.reshape(block, heads_dev, head_dim)
        wide_state = (
            decay[:, :, None, None] * state.astype(jnp.float32)
            + (step_size[:, :, None] * inner)[:, :, :, None] * b_vec[:, None, None, :]
        )
        head_out = jnp.sum(wide_state * c_vec[:, None, None, :], axis=-1)
        state = wide_state.astype(jnp.bfloat16)
        head_out = head_out + skip_d[None, :, None] * inner
        gated = head_out.reshape(block, width_x) * jax.nn.silu(gate_raw.astype(jnp.float32))
        local_sum = jnp.sum(gated * gated, axis=-1)
        totals = lax.psum(group_mask * local_sum[:, None], "wide")
        group_total = jnp.sum(totals * group_mask, axis=1)
        ynorm = (gated * lax.rsqrt(group_total[:, None] / (DI // GROUPS) + EPS) * norm_gain).astype(
            jnp.bfloat16
        )
        all_rows = lax.all_gather(ynorm, "narrow", axis=0, tiled=True)
        projected = lax.psum_scatter(
            jnp.dot(all_rows, w_out, preferred_element_type=jnp.float32),
            "wide",
            scatter_dimension=0,
            tiled=True,
        )
        results.append((tokens.astype(jnp.float32) + projected).astype(jnp.bfloat16))
    return jnp.stack(results, 0)


def solution(mesh):
    return jax.shard_map(
        per_device,
        mesh=mesh,
        in_specs=(
            P(None, "wide", "narrow"),
            P("narrow"),
            P("narrow", "wide"),
            P("narrow", "wide"),
            P("narrow", "wide"),
            P("narrow", "wide"),
            P(None, "wide"),
            P(None, "wide"),
            P("narrow", None, "wide"),
            P("narrow", None, "wide"),
            P("wide"),
            P("wide"),
            P("wide"),
            P("narrow", "wide", None, None),
            P("wide"),
            P("wide", "narrow"),
        ),
        out_specs=P(None, "wide", "narrow"),
        check_vma=False,
    )
```

profile of v0, /device:TPU:56, one launch (start us, length us, event | category | flops | bytes accessed | tf_op | source)
XLA Modules:
  0.0 1024.3 jit_solution(5651419099273867554)
XLA Ops:
  7.6 18.1 %all-reduce.12 = (f32[3]{0:T(128)S(1)}, f32[3]{0:T(128)S(1)}, f32[3]{0:T(128)S(1)}, f32[3]{0:T(128)S(1)}, f32[3]{0:T(128)S(1)}) all-reduce(f32[3]{0:T(128)S(1)} %get-tuple-element.12, f32[3]{0:T(128)S(1)} %get-tuple-element.13, f32[3]{0:T(128)S(1)} %get-tuple-element.10, ...), channel_id=1, replica_groups=mesh['wide'=64,'narrow'=8] {'narrow'}, use_global_device_ids=true, to_apply=%region_9.10 | all-reduce | flops 15 | bytes 120 | tf_op jit(solution)/shard_map/psum | solution.py:68
  28.6 53.2 %all-gather.2 = bf16[64,3,1024]{2,1,0:T(4,128)(2,1)S(1)} all-gather(bf16[1,3,1024]{2,1,0:T(4,128)(2,1)S(1)} %get-tuple-element.70), channel_id=1, replica_groups=mesh['wide'=64,'narrow'=8] {'wide'}, dimensions={0}, use_global_device_ids=true | all-gather | bytes 399360 | tf_op jit(solution)/shard_map/all_gather | solution.py:71
  82.2 49.4 %all-gather.1 = bf16[64,3,1024]{2,1,0:T(4,128)(2,1)S(1)} all-gather(bf16[1,3,1024]{2,1,0:T(4,128)(2,1)S(1)} %get-tuple-element.71), channel_id=1, replica_groups=mesh['wide'=64,'narrow'=8] {'wide'}, dimensions={0}, use_global_device_ids=true | all-gather | bytes 399360 | tf_op jit(solution)/shard_map/all_gather | solution.py:71
  134.3 47.7 %all-gather.3 = bf16[64,3,1024]{2,1,0:T(4,128)(2,1)S(1)} all-gather(bf16[1,3,1024]{2,1,0:T(4,128)(2,1)S(1)} %get-tuple-element.72), channel_id=1, replica_groups=mesh['wide'=64,'narrow'=8] {'wide'}, dimensions={0}, use_global_device_ids=true | all-gather | bytes 399360 | tf_op jit(solution)/shard_map/all_gather | solution.py:71
  183.6 49.5 %all-gather.4 = bf16[64,3,1024]{2,1,0:T(4,128)(2,1)S(1)} all-gather(bf16[1,3,1024]{2,1,0:T(4,128)(2,1)S(1)} %get-tuple-element.73), channel_id=1, replica_groups=mesh['wide'=64,'narrow'=8] {'wide'}, dimensions={0}, use_global_device_ids=true | all-gather | bytes 399360 | tf_op jit(solution)/shard_map/all_gather | solution.py:71
  234.6 47.7 %all-gather = bf16[64,3,1024]{2,1,0:T(4,128)(2,1)S(1)} all-gather(bf16[1,3,1024]{2,1,0:T(4,128)(2,1)S(1)} %get-tuple-element.74), channel_id=1, replica_groups=mesh['wide'=64,'narrow'=8] {'wide'}, dimensions={0}, use_global_device_ids=true | all-gather | bytes 399360 | tf_op jit(solution)/shard_map/all_gather | solution.py:71
  286.2 75.9 %all-reduce.19.cloned.1.call-done = (bf16[192,580]{1,0:T(8,128)(2,1)}, bf16[192,580]{1,0:T(8,128)(2,1)}, bf16[192,580]{1,0:T(8,128)(2,1)}, bf16[192,580]{1,0:T(8,128)(2,1)}, bf16[192,580]{1,0:T(8,128)(2,1)}) async-done(((bf16[192,580]{1,0:T(8,128)(2,1)}, bf16[192,580]{1,0:T(8,128)(2,1)}, bf16[192,580]{1,0:T(8,128)(2,1)}, bf16[192,580]{1,0:T(8,128)(2,1)}, bf16[192,580]{1,0:T(8,128)(2,1)}), ...) | async-done | bytes 1113616
  376.5 3.4 collective-permute-start.7
  382.6 3.4 collective-permute-start.13
  388.6 3.4 collective-permute-start.4
  392.0 4.6 collective-permute-start.2
  396.6 2.8 collective-permute-start.5
  399.4 4.6 collective-permute-start.14
  404.0 2.8 collective-permute-start.8
  406.8 4.6 collective-permute-start.11
  414.0 6.6 multiply_reduce_fusion.3
  420.8 10.3 %multiply_reduce_fusion = (f32[24,4,64]{2,1,0:T(4,128)S(1)}, f32[24,4,64]{2,1,0:T(4,128)S(1)}, f32[24,4,64]{2,1,0:T(4,128)S(1)}) fusion(f32[24,256]{1,0:T(8,128)S(1)} %get-tuple-element.80, f32[24,256]{1,0:T(8,128)S(1)} %get-tuple-element.79, f32[24,4,64]{2,1,0:T(4,128)S(1)} %broadcast_multiply_fusion, f32[24,4]{1,0:T(8,128)S(1)} %get-tuple-element.111, ...), kind=kLoop, calls=%fused_computation | loop fusion | flops 47167488 | bytes 3540864 | tf_op jit(solution)/shard_map/reduce_sum | solution.py:105
  432.5 248.0 %all-reduce.10 = (f32[24,8]{0,1:T(8,128)S(1)}, f32[24,8]{0,1:T(8,128)S(1)}, f32[24,8]{0,1:T(8,128)S(1)}, f32[24,8]{0,1:T(8,128)S(1)}, f32[24,8]{0,1:T(8,128)S(1)}) all-reduce(f32[24,8]{0,1:T(8,128)S(1)} %get-tuple-element.117, f32[24,8]{0,1:T(8,128)S(1)} %get-tuple-element.118, ...), channel_id=1, replica_groups=mesh['wide'=64,'narrow'=8] {'wide'}, use_global_device_ids=true, to_apply=%region_37.38 | all-reduce | flops 960 | bytes 7680 | tf_op jit(solution)/shard_map/psum | solution.py:110
  680.8 24.6 %all_gather.39 = bf16[192,256]{1,0:T(8,128)(2,1)S(1)} all-gather(bf16[24,256]{1,0:T(8,128)(2,1)S(1)} %get-tuple-element.93), channel_id=1, replica_groups=mesh['wide'=64,'narrow'=8] {'narrow'}, dimensions={0}, use_global_device_ids=true | all-gather | bytes 110592 | tf_op jit(solution)/shard_map/all_gather | solution.py:115
  705.4 24.6 %all_gather.33 = bf16[192,256]{1,0:T(8,128)(2,1)S(1)} all-gather(bf16[24,256]{1,0:T(8,128)(2,1)S(1)} %get-tuple-element.94), channel_id=1, replica_groups=mesh['wide'=64,'narrow'=8] {'narrow'}, dimensions={0}, use_global_device_ids=true | all-gather | bytes 110592 | tf_op jit(solution)/shard_map/all_gather | solution.py:115
  730.0 24.6 %all_gather.35 = bf16[192,256]{1,0:T(8,128)(2,1)S(1)} all-gather(bf16[24,256]{1,0:T(8,128)(2,1)S(1)} %get-tuple-element.95), channel_id=1, replica_groups=mesh['wide'=64,'narrow'=8] {'narrow'}, dimensions={0}, use_global_device_ids=true | all-gather | bytes 110592 | tf_op jit(solution)/shard_map/all_gather | solution.py:115
  754.6 24.6 %all_gather.37 = bf16[192,256]{1,0:T(8,128)(2,1)S(1)} all-gather(bf16[24,256]{1,0:T(8,128)(2,1)S(1)} %get-tuple-element.96), channel_id=1, replica_groups=mesh['wide'=64,'narrow'=8] {'narrow'}, dimensions={0}, use_global_device_ids=true | all-gather | bytes 110592 | tf_op jit(solution)/shard_map/all_gather | solution.py:115
  779.2 24.6 %all_gather.31 = bf16[192,256]{1,0:T(8,128)(2,1)S(1)} all-gather(bf16[24,256]{1,0:T(8,128)(2,1)S(1)} %get-tuple-element.97), channel_id=1, replica_groups=mesh['wide'=64,'narrow'=8] {'narrow'}, dimensions={0}, use_global_device_ids=true | all-gather | bytes 110592 | tf_op jit(solution)/shard_map/all_gather | solution.py:115
  811.6 200.4 %all-reduce.17.cloned.1.call-done = (f32[192,1024]{1,0:T(8,128)}, f32[192,1024]{1,0:T(8,128)}, f32[192,1024]{1,0:T(8,128)}, f32[192,1024]{1,0:T(8,128)}, f32[192,1024]{1,0:T(8,128)}) async-done(((f32[192,1024]{1,0:T(8,128)}, f32[192,1024]{1,0:T(8,128)}, f32[192,1024]{1,0:T(8,128)}, f32[192,1024]{1,0:T(8,128)}, f32[192,1024]{1,0:T(8,128)}), (f32[192,1024]{1,0:T(8,128)}, f32[192,1024]{1,0:T(8,128)}, ...) | async-done | bytes 3932176
  (134 shorter events, 49.6 us)
Async XLA Ops:
  6.5 797.3 %copy-start = (bf16[256,1024]{1,0:T(8,128)(2,1)S(1)}, bf16[256,1024]{1,0:T(8,128)(2,1)}, u32[]{:S(2)}) copy-start(bf16[256,1024]{1,0:T(8,128)(2,1)} %param.31) | copy-start | bytes 1572868
  6.5 125.3 %copy-start.10 = (bf16[1024,256]{1,0:T(8,128)(2,1)S(1)}, bf16[1024,256]{1,0:T(8,128)(2,1)}, u32[]{:S(2)}) copy-start(bf16[1024,256]{1,0:T(8,128)(2,1)} %param.19) | copy-start | bytes 1572868
  6.5 125.3 %copy-start.11 = (bf16[1024,256]{1,0:T(8,128)(2,1)S(1)}, bf16[1024,256]{1,0:T(8,128)(2,1)}, u32[]{:S(2)}) copy-start(bf16[1024,256]{1,0:T(8,128)(2,1)} %param.18) | copy-start | bytes 1572868
  6.5 355.6 %all-reduce.19.cloned.1.call-start = ((), (), s32[]{:S(2)}) async-start(), calls=%async_computation.1 | async-start | bytes 2457600
  282.7 91.0 %copy-start.2 = (bf16[24,3,256]{2,0,1:T(8,128)(2,1)S(1)}, bf16[24,3,256]{2,0,1:T(8,128)(2,1)}, u32[]{:S(2)}) copy-start(bf16[24,3,256]{2,0,1:T(8,128)(2,1)} %param.24) | copy-start | bytes 110596
  282.7 92.3 %copy-start.8 = (f32[4]{0:T(128)S(1)}, f32[4]{0:T(128)}, u32[]{:S(2)}) copy-start(f32[4]{0:T(128)} %param.27) | copy-start | bytes 52
  284.0 728.0 %all-reduce.17.cloned.1.call-start = ((), (), s32[]{:S(2)}) async-start(), calls=%async_computation | async-start | bytes 7864320
  363.0 13.4 %collective-permute-start.6 = (bf16[24,64]{1,0:T(8,128)(2,1)S(1)}, bf16[24,64]{1,0:T(8,128)(2,1)S(1)}, u32[]{:S(2)}, u32[]{:S(2)}) collective-permute-start(bf16[24,64]{1,0:T(8,128)(2,1)S(1)} %get-tuple-element.53), channel_id=1, source_target_pairs={{0,8},{8,0},{16,24},{24,16},{32,40},{40,32},{48,56},{56,48},{64,72... | collective-permute-start | bytes 9224 | tf_op jit(solution)/shard_map/ppermute | solution.py:15
  365.0 14.9 %collective-permute-start.9 = (bf16[24,64]{1,0:T(8,128)(2,1)S(1)}, bf16[24,64]{1,0:T(8,128)(2,1)S(1)}, u32[]{:S(2)}, u32[]{:S(2)}) collective-permute-start(bf16[24,64]{1,0:T(8,128)(2,1)S(1)} %get-tuple-element.54), channel_id=1, source_target_pairs={{0,8},{8,0},{16,24},{24,16},{32,40},{40,32},{48,56},{56,48},{64,72... | collective-permute-start | bytes 9224 | tf_op jit(solution)/shard_map/ppermute | solution.py:15
  367.4 15.1 %collective-permute-start.12 = (bf16[24,64]{1,0:T(8,128)(2,1)S(1)}, bf16[24,64]{1,0:T(8,128)(2,1)S(1)}, u32[]{:S(2)}, u32[]{:S(2)}) collective-permute-start(bf16[24,64]{1,0:T(8,128)(2,1)S(1)} %get-tuple-element.55), channel_id=1, source_target_pairs={{0,8},{8,0},{16,24},{24,16},{32,40},{40,32},{48,56},{56,48},{64,72... | collective-permute-start | bytes 9224 | tf_op jit(solution)/shard_map/ppermute | solution.py:15
  369.3 19.2 %collective-permute-start.3 = (bf16[24,64]{1,0:T(8,128)(2,1)S(1)}, bf16[24,64]{1,0:T(8,128)(2,1)S(1)}, u32[]{:S(2)}, u32[]{:S(2)}) collective-permute-start(bf16[24,64]{1,0:T(8,128)(2,1)S(1)} %get-tuple-element.57), channel_id=1, source_target_pairs={{0,8},{8,0},{16,24},{24,16},{32,40},{40,32},{48,56},{56,48},{64,72... | collective-permute-start | bytes 9224 | tf_op jit(solution)/shard_map/ppermute | solution.py:15
  371.7 14.2 %collective-permute-start = (bf16[24,64]{1,0:T(8,128)(2,1)S(1)}, bf16[24,64]{1,0:T(8,128)(2,1)S(1)}, u32[]{:S(2)}, u32[]{:S(2)}) collective-permute-start(bf16[24,64]{1,0:T(8,128)(2,1)S(1)} %get-tuple-element.59), channel_id=1, source_target_pairs={{0,8},{8,0},{16,24},{24,16},{32,40},{40,32},{48,56},{56,48},{64,72... | collective-permute-start | bytes 9224 | tf_op jit(solution)/shard_map/ppermute | solution.py:15
  376.5 27.5 %collective-permute-start.7 = (bf16[24,128]{1,0:T(8,128)(2,1)S(1)}, bf16[24,128]{1,0:T(8,128)(2,1)S(1)}, u32[]{:S(2)}, u32[]{:S(2)}) collective-permute-start(bf16[24,128]{1,0:T(8,128)(2,1)S(1)} %maximum_select_fusion.12), channel_id=1, source_target_pairs={{0,16},{8,24},{16,0},{24,8},{32,48},{40,56},{48,32},{56,40},{64,80... | collective-permute-start | bytes 18440 | tf_op jit(solution)/shard_map/ppermute | solution.py:15
  380.0 26.8 %collective-permute-start.10 = (bf16[24,128]{1,0:T(8,128)(2,1)S(1)}, bf16[24,128]{1,0:T(8,128)(2,1)S(1)}, u32[]{:S(2)}, u32[]{:S(2)}) collective-permute-start(bf16[24,128]{1,0:T(8,128)(2,1)S(1)} %maximum_select_fusion.13), channel_id=1, source_target_pairs={{0,16},{8,24},{16,0},{24,8},{32,48},{40,56},{48,32},{56,40},{64,80... | collective-permute-start | bytes 18440 | tf_op jit(solution)/shard_map/ppermute | solution.py:15
  382.6 16.8 %collective-permute-start.13 = (bf16[24,128]{1,0:T(8,128)(2,1)S(1)}, bf16[24,128]{1,0:T(8,128)(2,1)S(1)}, u32[]{:S(2)}, u32[]{:S(2)}) collective-permute-start(bf16[24,128]{1,0:T(8,128)(2,1)S(1)} %maximum_select_fusion.14), channel_id=1, source_target_pairs={{0,16},{8,24},{16,0},{24,8},{32,48},{40,56},{48,32},{56,40},{64,80... | collective-permute-start | bytes 18440 | tf_op jit(solution)/shard_map/ppermute | solution.py:15
  386.0 5.9 collective-permute-start.1
  388.6 8.0 collective-permute-start.4
  392.0 22.0 %collective-permute-start.2 = (bf16[24,256]{1,0:T(8,128)(2,1)S(1)}, bf16[24,256]{1,0:T(8,128)(2,1)S(1)}, u32[]{:S(2)}, u32[]{:S(2)}) collective-permute-start(bf16[24,256]{1,0:T(8,128)(2,1)S(1)} %maximum_select_fusion.5), channel_id=1, source_target_pairs={{0,32},{8,40},{16,48},{24,56},{32,0},{40,8},{48,16},{56,24},{64,96... | collective-permute-start | bytes 36872 | tf_op jit(solution)/shard_map/ppermute | solution.py:15
  396.6 17.4 %collective-permute-start.5 = (bf16[24,256]{1,0:T(8,128)(2,1)S(1)}, bf16[24,256]{1,0:T(8,128)(2,1)S(1)}, u32[]{:S(2)}, u32[]{:S(2)}) collective-permute-start(bf16[24,256]{1,0:T(8,128)(2,1)S(1)} %maximum_select_fusion.6), channel_id=1, source_target_pairs={{0,32},{8,40},{16,48},{24,56},{32,0},{40,8},{48,16},{56,24},{64,96... | collective-permute-start | bytes 36872 | tf_op jit(solution)/shard_map/ppermute | solution.py:15
  399.4 14.5 %collective-permute-start.14 = (bf16[24,256]{1,0:T(8,128)(2,1)S(1)}, bf16[24,256]{1,0:T(8,128)(2,1)S(1)}, u32[]{:S(2)}, u32[]{:S(2)}) collective-permute-start(bf16[24,256]{1,0:T(8,128)(2,1)S(1)} %maximum_select_fusion.9), channel_id=1, source_target_pairs={{0,32},{8,40},{16,48},{24,56},{32,0},{40,8},{48,16},{56,24},{64,96... | collective-permute-start | bytes 36872 | tf_op jit(solution)/shard_map/ppermute | solution.py:15
  404.0 7.4 collective-permute-start.8
  406.8 7.1 collective-permute-start.11
  420.7 260.1 %copy-start.7 = (f32[256]{0:T(256)S(1)}, f32[256]{0:T(256)}, u32[]{:S(2)}) copy-start(f32[256]{0:T(256)} %param.30) | copy-start | bytes 3076
  807.3 204.6 %copy-start.1 = (bf16[5,3,1024]{2,1,0:T(4,128)(2,1)S(1)}, bf16[5,3,1024]{2,1,0:T(4,128)(2,1)}, u32[]{:S(2)}) copy-start(bf16[5,3,1024]{2,1,0:T(4,128)(2,1)} %param.16) | copy-start | bytes 92164
  (6 other events, 90.1 us)
Sparse Core Ops, SparseCore 0:
  284.1 78.0 all-reduce.18
  809.8 202.1 all-reduce.16
where the time goes:
time: 1030 us; the launch traced here: 1020 us
  blocking collectives  637 us (62%)
  waiting for transfers between devices  279 us (27%)
  starting transfers between devices  44.9 us (4%)
  other arithmetic  28.7 us (3%)
  between operations  15.5 us (2%)
  matrix products  11.8 us (1%)
    unnamed x4, waiting for transfers between devices  276 us
    psum x1, blocking collectives, per_device(): totals = lax.psum(group_mask * local_sum[:, None], 'wide')  248 us
    all_gather x5, blocking collectives, per_device(): lax.all_gather(normed, 'wide', axis=0, tiled=True)  248 us
    all_gather x5, blocking collectives, per_device(): all_rows = lax.all_gather(ynorm, 'narrow', axis=0, tiled=True)  123 us
    ppermute x15, starting transfers between devices, from_partner(): lax.ppermute(x, axis, [(i, i ^ 1 << apart) for i in range(lax.axis_size(a...  44.9 us
  transfers between devices with their start and end apart: 17, of which 3 were waited for; matrix products, arithmetic and copies ran while one was open for 1% of the time, Pallas kernels for 0%

commit v1 on v0

v1 whole, which is shorter than its diff:
```python
import jax
import jax.numpy as jnp
from jax import lax
from jax.experimental import pallas as pl
from jax.experimental.pallas import tpu as pltpu
from jax.sharding import Mesh
from jax.sharding import PartitionSpec as P

D = 8192
GROUPS = 8
DI = 16384
STEPS = 5
CONVK = 4
EPS = 1e-05

NZ, NX, NC, NY = 8, 4, 2, 8
OWN = 3
SLOT = 16
HALF = NX * SLOT
BLOCK = 2 * HALF
RB = 24
BF = jnp.bfloat16
F32 = jnp.float32
WIDE = ("z", "x", "core")


def swap_core(v):
    return lax.ppermute(v, "core", [(0, 1), (1, 0)])


def to_all(v, axes, count):
    return lax.all_to_all(
        jnp.broadcast_to(v[None], (count,) + v.shape), axes, split_axis=0, concat_axis=0, tiled=True
    )


def call(kernel, out_shape, in_specs, vmem=48, **kw):
    return pl.pallas_call(
        kernel,
        out_shape=out_shape,
        in_specs=in_specs,
        compiler_params=pltpu.CompilerParams(vmem_limit_bytes=vmem * 2**20),
        **kw,
    )


VM = pl.BlockSpec(memory_space=pltpu.VMEM)
SM = pl.BlockSpec(memory_space=pltpu.SMEM)
ANY = pl.BlockSpec(memory_space=pl.ANY)


def project_kernel(g_ref, gain_ref, wz_ref, wx_ref, ws_ref, *rest):
    pz_ref, px_ref = rest[-2:]
    raw = g_ref[...].reshape(NZ * HALF, -1).astype(F32)
    ss = jnp.sum(raw * raw, axis=1, keepdims=True)
    lhs = (raw * gain_ref[...]).astype(BF)
    dot = lambda w: jnp.dot(lhs, w[...], preferred_element_type=F32)
    pz_ref[...] = dot(wz_ref).astype(pz_ref.dtype).reshape(NZ, HALF, -1)
    px_ref[:, :, :256] = dot(wx_ref).astype(BF).reshape(NZ, HALF, -1)
    small = dot(ws_ref)
    hi = ss.astype(BF).astype(F32)
    lo = ss - hi
    lane = lax.broadcasted_iota(jnp.int32, small.shape, 1)
    small = jnp.where(lane == 68, hi, jnp.where(lane == 69, lo, small))
    px_ref[:, :, 256:] = small.astype(BF).reshape(NZ, HALF, -1)


def project(g, gain, wz, wx, ws, which, held=()):
    shapes = (
        jax.ShapeDtypeStruct((NY, BLOCK, 256), BF),
        jax.ShapeDtypeStruct((NY, BLOCK, 384), BF),
    )
    specs = [
        pl.BlockSpec((NY, HALF, s.shape[2]), lambda i, w=which: (0, w, 0)) for s in shapes
    ]
    whole = lambda a: pl.BlockSpec(a.shape, lambda i, n=a.ndim: (0,) * n)
    args = (g, gain, wz, wx, ws)
    return pl.pallas_call(
        project_kernel,
        grid=(1,),
        out_shape=shapes,
        in_specs=[whole(a) for a in args] + [ANY] * len(held),
        out_specs=specs,
        input_output_aliases={len(args) + i: i for i in range(len(held))},
        compiler_params=pltpu.CompilerParams(vmem_limit_bytes=48 * 2**20),
    )(*args, *held)


def slot_of(m, core):
    half, x, j = m // HALF, m % HALF // SLOT, m % SLOT
    cc = jnp.where(half == 0, core, 1 - core)
    step = (j * 11) // 32
    q = x * 2 + cc
    return step * RB + q * OWN + (j - step * OWN), j, q


def step_from_slot(core):
    i = lax.broadcasted_iota(jnp.int32, (STEPS * RB, BLOCK), 0)
    at, j, _ = slot_of(lax.broadcasted_iota(jnp.int32, (STEPS * RB, BLOCK), 1), core)
    return jnp.where((at == i) & (j < SLOT - 1), 1.0, 0.0).astype(BF)


def slot_from_step(core):
    shape = (BLOCK, STEPS * RB)
    at, j, q = slot_of(lax.broadcasted_iota(jnp.int32, shape, 0), core)
    i = lax.broadcasted_iota(jnp.int32, shape, 1)
    row = i % RB
    last = j == SLOT - 1
    order = jnp.where((at == i) & ~last, 1.0, 0.0).astype(BF)
    collect = jnp.where((row // OWN == q) & last, 1.0, 0.0).astype(BF)
    return order, collect


def conv(hist_ref, current, taps_ref):
    seq = [hist_ref[k].astype(F32) for k in range(CONVK - 1)]
    seq += [current[t * RB : (t + 1) * RB] for t in range(STEPS)]
    out = []
    for t in range(STEPS):
        acc = taps_ref[0:1] * seq[t]
        for k in range(1, CONVK):
            acc = acc + taps_ref[k : k + 1] * seq[t + k]
        out.append(acc * jax.nn.sigmoid(acc))
    return out


def shared_kernel(core_ref, p_ref, hist_ref, taps_ref, cur_ref, rstd_ref, bcc_ref):
    total = p_ref[0].astype(F32)
    for n in range(1, NY):
        total = total + p_ref[n].astype(F32)
    ss = total[:, 256 + 68 : 256 + 69] + total[:, 256 + 69 : 256 + 70]
    rstd = lax.rsqrt(ss / D + EPS)
    raw = (total * rstd).astype(BF)
    cur = jnp.dot(step_from_slot(core_ref[0]), raw, preferred_element_type=F32)
    cur_ref[...] = cur.astype(BF)
    rstd_ref[...] = jnp.broadcast_to(rstd, rstd_ref.shape)
    for t, v in enumerate(conv(hist_ref, cur[:, 256:320], taps_ref)):
        bcc_ref[t * RB : (t + 1) * RB, :] = v.astype(BF)


def per_head(ref):
    head = lax.broadcasted_iota(jnp.int32, (1, 256), 1) // 64
    out = jnp.full((1, 256), ref[0], F32)
    for h in range(1, 4):
        out = jnp.where(head == h, ref[h], out)
    return out


def state_kernel(
    core_ref, a_log_ref, bias_ref, skip_ref, bc_ref, cur_ref, z_ref, rstd_ref, hist_ref, taps_ref,
    gain_ref, s_ref, u_ref, c_rows, y_rows,
):
    core = core_ref[0]
    at = lambda v, t: v[t * RB : (t + 1) * RB]
    b_all = jnp.concatenate([bc_ref[i] for i in range(4)], axis=1)
    c_all = jnp.concatenate([bc_ref[i] for i in range(4, 8)], axis=1)
    b_vec, c_vec = b_all.astype(F32), c_all.astype(F32)

    c_rows[...] = jnp.zeros_like(c_rows)
    for t in range(STEPS):
        for h in range(2):
            c_rows[h, pl.ds(t, RB, stride=8), :] = at(c_vec, t)[:, h * 128 : h * 128 + 128]
    for r in range(RB):
        c_row = jnp.concatenate([c_rows[h, r * 8 : r * 8 + 8, :] for h in range(2)], axis=1)
        y_row = lax.dot_general(
            c_row.astype(BF), s_ref[r], (((1,), (1,)), ((), ())), preferred_element_type=F32
        )
        for h in range(2):
            y_rows[h, r * 8 : r * 8 + 8, :] = y_row[:, h * 128 : h * 128 + 128]

    cur = cur_ref[...]
    lane = lax.broadcasted_iota(jnp.int32, (128, 256), 0)
    head = lax.broadcasted_iota(jnp.int32, (128, 256), 1) // 64
    spread = jnp.where(lane == head + 64, 1.0, 0.0).astype(BF)
    dt_raw = jnp.dot(cur[:, 256:], spread, preferred_element_type=F32)
    pre = dt_raw + per_head(bias_ref)
    dt = jnp.maximum(pre, 0.0) + jnp.log1p(jnp.exp(-jnp.abs(pre)))
    decay = jnp.exp(-dt * jnp.exp(per_head(a_log_ref)))
    skip = per_head(skip_ref)

    gate_raw = (z_ref[...].astype(F32) * rstd_ref[:, :1]).astype(BF)
    gate = jnp.dot(step_from_slot(core), gate_raw, preferred_element_type=F32)
    gate = gate * jax.nn.sigmoid(gate)

    inner = conv(hist_ref, cur[:, :256].astype(F32), taps_ref)
    carried, terms, gated = None, [], []
    for t in range(STEPS):
        d = at(decay, t)
        carried = d if carried is None else carried * d
        terms = [term * d for term in terms] + [at(dt, t) * inner[t]]
        held = [y_rows[h, pl.ds(t, RB, stride=8), :] for h in range(2)]
        y = carried * jnp.concatenate(held, axis=1) + skip * inner[t]
        for s in range(t + 1):
            y = y + jnp.sum(at(c_vec, t) * at(b_vec, s), axis=1, keepdims=True) * terms[s]
        gated.append(y * at(gate, t))
    gated = jnp.concatenate(gated, axis=0)
    ss = jnp.sum(gated * gated, axis=1, keepdims=True)
    hi = ss.astype(BF).astype(F32)
    lo = ss - hi
    row = lax.broadcasted_iota(jnp.int32, gated.shape, 0)
    lane = lax.broadcasted_iota(jnp.int32, gated.shape, 1)
    slot = row // RB * OWN + row % RB % OWN
    sums = jnp.where(lane == slot, hi, jnp.where(lane == slot + SLOT, lo, 0.0)).astype(BF)
    order, collect = slot_from_step(core)
    u = jnp.dot(order, (gated * gain_ref[...]).astype(BF), preferred_element_type=F32)
    u_ref[...] = (u + jnp.dot(collect, sums, preferred_element_type=F32)).astype(BF)


def out_kernel(u_ref, w_ref, w_other_ref, o_ref):
    mine = u_ref[:, 0].reshape(NY * HALF, 256)
    other = u_ref[:, 1].reshape(NY * HALF, 256)
    ss = mine[:, :128].astype(F32) + other[:, :128].astype(F32)
    lane = lax.broadcasted_iota(jnp.int32, ss.shape, 1)
    ss = ss + pltpu.roll(ss, 128 - SLOT, 1)
    hi = ss.astype(BF).astype(F32)
    lo = pltpu.roll(ss - hi, SLOT, 1)
    kept = jnp.where(lane < SLOT, hi, jnp.where(lane < 2 * SLOT, lo, 0.0))
    for c in range(4):
        cols = slice(c * 256, c * 256 + 256)
        part = jnp.dot(mine, w_ref[:, cols], preferred_element_type=F32)
        part = part + jnp.dot(other, w_other_ref[:, cols], preferred_element_type=F32)
        if c == 0:
            slot = lax.broadcasted_iota(jnp.int32, ss.shape, 0) % SLOT
            first = jnp.where(slot == SLOT - 1, kept, part[:, :128])
            part = jnp.concatenate([first, part[:, 128:]], axis=1)
        o_ref[:, :, cols] = part.astype(BF).reshape(NZ * NX, SLOT, 256)


def last_kernel(p_ref, x_ref, o_ref):
    lane = lax.broadcasted_iota(jnp.int32, (SLOT, 128), 1)
    slot = lax.broadcasted_iota(jnp.int32, (SLOT, 128), 0)
    mask = (lane == slot) | (lane == slot + SLOT)
    acc = x_ref[...].astype(F32)
    for z in range(NZ):
        part = p_ref[z * NX].astype(F32)
        for x in range(1, NX):
            part = part + p_ref[z * NX + x].astype(F32)
        ss = jnp.broadcast_to(part[SLOT - 1 :, :128], (SLOT, 128))
        ss = jnp.sum(jnp.where(mask, ss, 0.0), axis=1, keepdims=True)
        acc = acc + part * lax.rsqrt(ss / (DI // GROUPS) + EPS)
    o_ref[...] = acc.astype(BF)


def per_device(
    inputs, pre_gain, w_z, w_x, w_bc, w_dt, conv_x_w, conv_bc_w, conv_x_state, conv_bc_state,
    a_log, dt_bias, skip_d, ssm_state, norm_gain, w_out,
):
    core = lax.axis_index("core").astype(jnp.int32).reshape(1)
    w_out_other = swap_core(w_out)
    tokens = jnp.pad(inputs.reshape(STEPS * OWN, -1), ((0, 1), (0, 0)))
    gathered = to_all(tokens, ("z", "x"), NZ * NX)
    other = swap_core(gathered)
    w_small = jnp.concatenate([w_bc, w_dt, jnp.zeros((w_bc.shape[0], 60), BF)], axis=1)
    weights = (pre_gain[None], w_z, w_x, w_small)
    held = project(gathered, *weights, 0)
    pz, px = project(other, *weights, 1, held)

    both = lax.all_to_all(
        jnp.concatenate([pz, px], axis=2), "y", split_axis=0, concat_axis=0, tiled=True
    )
    gate = jnp.sum(both[:, :, :256].astype(F32), axis=0)
    px = both[:, :, 256:]

    cur, rstd, bcc = call(
        shared_kernel,
        (
            jax.ShapeDtypeStruct((STEPS * RB, 384), BF),
            jax.ShapeDtypeStruct((BLOCK, 128), F32),
            jax.ShapeDtypeStruct((STEPS * RB, 64), BF),
        ),
        [SM, VM, VM, VM],
    )(core, px, jnp.swapaxes(conv_bc_state, 0, 1), conv_bc_w)
    vectors = to_all(bcc, ("x", "core"), NX * NC)

    u = call(
        state_kernel,
        jax.ShapeDtypeStruct((BLOCK, 256), BF),
        [SM] * 4 + [VM] * 8,
        scratch_shapes=[pltpu.VMEM((2, RB * 8, 128), F32)] * 2,
    )(
        core, a_log, dt_bias, skip_d, vectors, cur, gate, rstd, jnp.swapaxes(conv_x_state, 0, 1),
        conv_x_w, norm_gain[None], ssm_state.reshape(RB, 256, 256),
    )
    mine = jnp.stack([u[:HALF], swap_core(u[HALF:])], 0)
    rows = to_all(mine, "y", NY)
    partial_sums = call(
        out_kernel, jax.ShapeDtypeStruct((NZ * NX, SLOT, w_out.shape[1]), BF), [VM] * 3
    )(rows, w_out, w_out_other)
    received = lax.all_to_all(partial_sums, ("z", "x"), split_axis=0, concat_axis=0, tiled=True)
    out = call(last_kernel, jax.ShapeDtypeStruct(tokens.shape, BF), [VM] * 2)(received, tokens)
    return out[: STEPS * OWN].reshape(inputs.shape)


def solution(mesh):
    fine = Mesh(mesh.devices.reshape(NZ, NX, NC, NY), (*WIDE, "y"))
    return jax.shard_map(
        per_device,
        mesh=fine,
        in_specs=(
            P(None, WIDE, "y"),
            P("y"),
            P("y", WIDE),
            P("y", WIDE),
            P("y", WIDE),
            P("y", WIDE),
            P(None, WIDE),
            P(None, WIDE),
            P("y", None, WIDE),
            P("y", None, WIDE),
            P(WIDE),
            P(WIDE),
            P(WIDE),
            P("y", WIDE, None, None),
            P(WIDE),
            P(WIDE, "y"),
        ),
        out_specs=P(None, WIDE, "y"),
        check_vma=False,
    )
```

time: 1030 us -> 177 us (0.17)
  the two profiles are of different devices: /device:TPU:56 before, /device:TPU:2 now
where the time goes in v1:
time: 177 us; the launch traced here: 176 us
  blocking collectives  75.1 us (42%)
  waiting for transfers between devices  55.9 us (32%)
  starting transfers between devices  21.4 us (12%)
  local copies, waits for them, and re-layouts  14.8 us (8%)
  Pallas kernels  5.31 us (3%)
  other arithmetic  3.43 us (2%)
    all_to_all x1, blocking collectives, to_all(): lax.all_to_all(jnp.broadcast_to(v[None], (count,) + v.shape), axes, split...  41.5 us
    all_to_all x1, waiting for transfers between devices, per_device(): lax.all_to_all(jnp.concatenate([pz, px], axis=2), 'y', split_axis=0, conc...  35.1 us
    all_to_all x1, blocking collectives, per_device(): lax.all_to_all(partial_sums, ('z', 'x'), split_axis=0, concat_axis=0, til...  33.7 us
    all_to_all x2, waiting for transfers between devices, to_all(): lax.all_to_all(jnp.broadcast_to(v[None], (count,) + v.shape), axes, split...  17.9 us
    unnamed x38, local copies, waits for them, and re-layouts  9.1 us
    all_to_all x2, starting transfers between devices, to_all(): lax.all_to_all(jnp.broadcast_to(v[None], (count,) + v.shape), axes, split...  8.29 us
    all_to_all x1, starting transfers between devices, per_device(): lax.all_to_all(jnp.concatenate([pz, px], axis=2), 'y', split_axis=0, conc...  7.1 us
    ppermute x3, starting transfers between devices, swap_core(): return lax.ppermute(v, 'core', [(0, 1), (1, 0)])  6.03 us
  transfers between devices with their start and end apart: 6, of which 5 were waited for; matrix products, arithmetic and copies ran while one was open for 2% of the time, Pallas kernels for 1%

profile of v1, /device:TPU:2, one launch (start us, length us, event | category | flops | bytes accessed | tf_op | source)
XLA Modules:
  0.0 176.3 jit_solution(14472307465627026298)
XLA Ops:
  1.0 41.5 %all_to_all.25.g_ref = bf16[32,16,1024]{2,1,0:T(8,128)(2,1)S(1)} all-to-all(bf16[32,16,1024]{2,1,0:T(8,128)(2,1)S(1)} %broadcast_in_dim.12), channel_id=1, replica_groups=mesh['z'=8,'x'=4,'core'=2,'y'=8] {'z','x'}, dimensions={0} | all-to-all | bytes 2097152 | tf_op jit(solution)/shard_map/all_to_all | solution.py:32
  42.5 1.9 %collective-permute-start = (bf16[32,16,1024]{2,1,0:T(8,128)(2,1)S(1)}, bf16[32,16,1024]{2,1,0:T(8,128)(2,1)S(1)}, u32[]{:S(2)}, u32[]{:S(2)}) collective-permute-start(bf16[32,16,1024]{2,1,0:T(8,128)(2,1)S(1)} %all_to_all.25.g_ref), channel_id=1, source_target_pairs={{0,8},{8,0},{1,9},{9,1},{2,10},{10,2},{3,11},{11,3},{4,12},{12,4},... | collective-permute-start | bytes 3145736 | tf_op jit(solution)/shard_map/ppermute | solution.py:28
  44.4 1.1 copy.21
  45.5 0.9 copy.22
  46.5 1.1 maximum_maximum_fusion.ws_ref
  47.6 1.0 shard_map.154
  48.7 1.0 shard_map.155
  49.7 1.2 pad_maximum_fusion
  50.9 7.1 %all-to-all-start.1 = ((bf16[8,128,640]{2,1,0:T(8,128)(2,1)}), bf16[8,128,640]{2,1,0:T(8,128)(2,1)}, u32[]{:S(2)}, u32[]{:S(2)}) async-start(bf16[8,128,640]{2,1,0:T(8,128)(2,1)} %pad_maximum_fusion), calls=%async_computation.1 | async-start | bytes 2621440 | tf_op jit(solution)/shard_map/all_to_all | solution.py:257
  58.0 35.1 %all-to-all-done.1 = bf16[8,128,640]{2,1,0:T(8,128)(2,1)} async-done(((bf16[8,128,640]{2,1,0:T(8,128)(2,1)}), bf16[8,128,640]{2,1,0:T(8,128)(2,1)}, u32[]{:S(2)}, u32[]{:S(2)}) %all-to-all-start.1) | async-done | bytes 1310752 | tf_op jit(solution)/shard_map/all_to_all | solution.py:257
  93.1 1.4 slice.20.p_ref
  96.9 4.8 %all-to-all-start.2 = ((bf16[8,120,64]{1,2,0:T(8,128)(2,1)}), bf16[8,120,64]{1,2,0:T(8,128)(2,1)}, u32[]{:S(2)}, u32[]{:S(2)}) async-start(bf16[8,120,64]{1,2,0:T(8,128)(2,1)} %broadcast_in_dim.30), calls=%async_computation.2 | async-start | bytes 262144 | tf_op jit(solution)/shard_map/all_to_all | solution.py:32
  101.7 1.1 convert_reduce_fusion.z_ref
  102.8 3.7 %all-to-all-done.2 = bf16[8,120,64]{1,2,0:T(8,128)(2,1)} async-done(((bf16[8,120,64]{1,2,0:T(8,128)(2,1)}), bf16[8,120,64]{1,2,0:T(8,128)(2,1)}, u32[]{:S(2)}, u32[]{:S(2)}) %all-to-all-start.2) | async-done | bytes 122912 | tf_op jit(solution)/shard_map/all_to_all | solution.py:32
  106.5 1.1 copy.24.bc_ref
  107.6 0.9 copy-done.5
  113.4 2.0 %shard_map.157 = bf16[128,256]{1,0:T(8,128)(2,1)S(1)} custom-call(s32[1]{0:T(128)} %bitcast.core_ref, f32[4]{0:T(128)S(1)} %copy-done.14, f32[4]{0:T(128)S(1)} %copy-done.15, f32[4]{0:T(128)S(1)} %copy-done.16, bf16[8,120,64]{2,1,0:T(8,128)(2,1)S(1)} %copy.24.bc_ref, bf16[120,384]{1,0:T(8,128)(2,1)S(1)} %copy-done.5, ...), custom_call_target="tpu_custom_call" | custom-call | tf_op jit(solution)/shard_map/pallas_call | solution.py:274
  115.4 2.1 %collective-permute-start.1 = (bf16[64,256]{1,0:T(8,128)(2,1)S(1)}, bf16[64,256]{1,0:T(8,128)(2,1)S(1)}, u32[]{:S(2)}, u32[]{:S(2)}) collective-permute-start(bf16[64,256]{1,0:T(8,128)(2,1)S(1)} %get-tuple-element.20), channel_id=1, source_target_pairs={{0,8},{8,0},{1,9},{9,1},{2,10},{10,2},{3,11},{11,3},{4,12},{12,4},... | collective-permute-start | bytes 98312 | tf_op jit(solution)/shard_map/ppermute | solution.py:28
  117.5 1.2 collective-permute-done.1
  119.5 3.5 %all-to-all-start.3 = ((bf16[8,2,64,256]{3,2,1,0:T(8,128)(2,1)}), bf16[8,2,64,256]{3,2,1,0:T(8,128)(2,1)S(1)}, u32[]{:S(2)}, u32[]{:S(2)}) async-start(bf16[8,2,64,256]{3,2,1,0:T(8,128)(2,1)} %broadcast_in_dim.32), calls=%async_computation.3 | async-start | bytes 1048576 | tf_op jit(solution)/shard_map/all_to_all | solution.py:32
  123.0 2.1 %collective-permute-start.2 = (bf16[256,1024]{1,0:T(8,128)(2,1)S(1)}, bf16[256,1024]{1,0:T(8,128)(2,1)S(1)}, u32[]{:S(2)}, u32[]{:S(2)}) collective-permute-start(bf16[256,1024]{1,0:T(8,128)(2,1)S(1)} %copy-done.3), channel_id=1, source_target_pairs={{0,8},{8,0},{1,9},{9,1},{2,10},{10,2},{3,11},{11,3},{4,12},{12,4},... | collective-permute-start | bytes 1572872 | tf_op jit(solution)/shard_map/ppermute | solution.py:28
  125.1 1.7 collective-permute-done.2.w_other_ref
  126.9 14.2 %all-to-all-done.3.u_ref = bf16[8,2,64,256]{3,2,1,0:T(8,128)(2,1)S(1)} async-done(((bf16[8,2,64,256]{3,2,1,0:T(8,128)(2,1)}), bf16[8,2,64,256]{3,2,1,0:T(8,128)(2,1)S(1)}, u32[]{:S(2)}, u32[]{:S(2)}) %all-to-all-start.3) | async-done | bytes 524320 | tf_op jit(solution)/shard_map/all_to_all | solution.py:32
  141.8 33.7 %all_to_all.26.p_ref = bf16[32,16,1024]{2,1,0:T(8,128)(2,1)S(1)} all-to-all(bf16[32,16,1024]{2,1,0:T(8,128)(2,1)S(1)} %shard_map.158), channel_id=1, replica_groups=mesh['z'=8,'x'=4,'core'=2,'y'=8] {'z','x'}, dimensions={0} | all-to-all | bytes 2097152 | tf_op jit(solution)/shard_map/all_to_all | solution.py:288
  (50 shorter events, 10.8 us)
Async XLA Ops:
  1.0 44.5 %copy-start.17 = (bf16[1024,4]{0,1:T(4,128)(2,1)S(1)}, bf16[1024,4]{0,1:T(4,128)(2,1)}, u32[]{:S(2)}) copy-start(bf16[1024,4]{0,1:T(4,128)(2,1)} %param.21) | copy-start | bytes 24580
  1.0 46.6 %copy-start.1 = (bf16[1024,256]{1,0:T(8,128)(2,1)S(1)}, bf16[1024,256]{1,0:T(8,128)(2,1)}, u32[]{:S(2)}) copy-start(bf16[1024,256]{1,0:T(8,128)(2,1)} %wz_ref.3) | copy-start | bytes 1572868
  1.0 46.6 %copy-start.2 = (bf16[1024,256]{1,0:T(8,128)(2,1)S(1)}, bf16[1024,256]{1,0:T(8,128)(2,1)}, u32[]{:S(2)}) copy-start(bf16[1024,256]{1,0:T(8,128)(2,1)} %wx_ref.3) | copy-start | bytes 1572868
  1.0 46.6 %copy-start.10 = (f32[1024]{0:T(1024)S(1)}, f32[1024]{0:T(1024)}, u32[]{:S(2)}) copy-start(f32[1024]{0:T(1024)} %param.17) | copy-start | bytes 12292
  42.5 6.2 %collective-permute-start = (bf16[32,16,1024]{2,1,0:T(8,128)(2,1)S(1)}, bf16[32,16,1024]{2,1,0:T(8,128)(2,1)S(1)}, u32[]{:S(2)}, u32[]{:S(2)}) collective-permute-start(bf16[32,16,1024]{2,1,0:T(8,128)(2,1)S(1)} %all_to_all.25.g_ref), channel_id=1, source_target_pairs={{0,8},{8,0},{1,9},{9,1},{2,10},{10,2},{3,11},{11,3},{4,12},{12,4},... | collective-permute-start | bytes 3145736 | tf_op jit(solution)/shard_map/ppermute | solution.py:28
  50.9 42.2 %all-to-all-start.1 = ((bf16[8,128,640]{2,1,0:T(8,128)(2,1)}), bf16[8,128,640]{2,1,0:T(8,128)(2,1)}, u32[]{:S(2)}, u32[]{:S(2)}) async-start(bf16[8,128,640]{2,1,0:T(8,128)(2,1)} %pad_maximum_fusion), calls=%async_computation.1 | async-start | bytes 2621440 | tf_op jit(solution)/shard_map/all_to_all | solution.py:257
  58.0 36.5 %copy-start.9 = (bf16[24,3,64]{2,0,1:T(8,128)(2,1)S(1)}, bf16[24,3,64]{2,0,1:T(8,128)(2,1)}, u32[]{:S(2)}) copy-start(bf16[24,3,64]{2,0,1:T(8,128)(2,1)} %param.25) | copy-start | bytes 27652
  58.0 36.5 %copy-start.12 = (f32[4,64]{1,0:T(4,128)S(1)}, f32[4,64]{1,0:T(4,128)}, u32[]{:S(2)}) copy-start(f32[4,64]{1,0:T(4,128)} %taps_ref.2) | copy-start | bytes 3076
  93.1 14.5 %copy-start = (bf16[24,4,64,256]{3,2,1,0:T(8,128)(2,1)S(1)}, bf16[24,4,64,256]{3,2,1,0:T(8,128)(2,1)}, u32[]{:S(2)}) copy-start(bf16[24,4,64,256]{3,2,1,0:T(8,128)(2,1)} %param.29) | copy-start | bytes 9437188
  94.8 0.6 copy-start.4
  95.5 0.6 copy-start.6
  96.9 9.6 %all-to-all-start.2 = ((bf16[8,120,64]{1,2,0:T(8,128)(2,1)}), bf16[8,120,64]{1,2,0:T(8,128)(2,1)}, u32[]{:S(2)}, u32[]{:S(2)}) async-start(bf16[8,120,64]{1,2,0:T(8,128)(2,1)} %broadcast_in_dim.30), calls=%async_computation.2 | async-start | bytes 262144 | tf_op jit(solution)/shard_map/all_to_all | solution.py:32
  107.6 0.9 copy-start.5
  108.5 0.8 copy-start.7
  109.3 0.8 copy-start.8
  110.1 0.7 copy-start.11
  110.8 0.7 copy-start.13
  111.4 0.7 copy-start.14
  112.1 0.7 copy-start.15
  112.7 0.7 copy-start.16
  115.4 7.6 %copy-start.3 = (bf16[256,1024]{1,0:T(8,128)(2,1)S(1)}, bf16[256,1024]{1,0:T(8,128)(2,1)}, u32[]{:S(2)}) copy-start(bf16[256,1024]{1,0:T(8,128)(2,1)} %w_ref.1) | copy-start | bytes 1572868
  115.4 3.2 %collective-permute-start.1 = (bf16[64,256]{1,0:T(8,128)(2,1)S(1)}, bf16[64,256]{1,0:T(8,128)(2,1)S(1)}, u32[]{:S(2)}, u32[]{:S(2)}) collective-permute-start(bf16[64,256]{1,0:T(8,128)(2,1)S(1)} %get-tuple-element.20), channel_id=1, source_target_pairs={{0,8},{8,0},{1,9},{9,1},{2,10},{10,2},{3,11},{11,3},{4,12},{12,4},... | collective-permute-start | bytes 98312 | tf_op jit(solution)/shard_map/ppermute | solution.py:28
  119.5 21.6 %all-to-all-start.3 = ((bf16[8,2,64,256]{3,2,1,0:T(8,128)(2,1)}), bf16[8,2,64,256]{3,2,1,0:T(8,128)(2,1)S(1)}, u32[]{:S(2)}, u32[]{:S(2)}) async-start(bf16[8,2,64,256]{3,2,1,0:T(8,128)(2,1)} %broadcast_in_dim.32), calls=%async_computation.3 | async-start | bytes 1048576 | tf_op jit(solution)/shard_map/all_to_all | solution.py:32
  123.0 3.8 %collective-permute-start.2 = (bf16[256,1024]{1,0:T(8,128)(2,1)S(1)}, bf16[256,1024]{1,0:T(8,128)(2,1)S(1)}, u32[]{:S(2)}, u32[]{:S(2)}) collective-permute-start(bf16[256,1024]{1,0:T(8,128)(2,1)S(1)} %copy-done.3), channel_id=1, source_target_pairs={{0,8},{8,0},{1,9},{9,1},{2,10},{10,2},{3,11},{11,3},{4,12},{12,4},... | collective-permute-start | bytes 1572872 | tf_op jit(solution)/shard_map/ppermute | solution.py:28

commit v2 on v1

v2 whole, which is shorter than its diff:
```python
import jax
import jax.numpy as jnp
from jax import lax
from jax.experimental import pallas as pl
from jax.experimental.pallas import tpu as pltpu
from jax.sharding import Mesh
from jax.sharding import PartitionSpec as P

D = 8192
GROUPS = 8
DI = 16384
STEPS = 5
CONVK = 4
EPS = 1e-05

NZ, NX, NC, NY = 8, 4, 2, 8
OWN = 3
SLOT = 16
HALF = NX * SLOT
BLOCK = NC * HALF
RB = 24
BF = jnp.bfloat16
F32 = jnp.float32
WIDE = ("z", "x", "core")


def swap_core(v):
    return lax.ppermute(v, "core", [(0, 1), (1, 0)])


def to_all(v, axes, count):
    return lax.all_to_all(
        jnp.broadcast_to(v[None], (count,) + v.shape), axes, split_axis=0, concat_axis=0, tiled=True
    )


def exchange(v, axes):
    return lax.all_to_all(v, axes, split_axis=0, concat_axis=0, tiled=True)


def call(kernel, out_shape, in_specs, vmem=48, **kw):
    return pl.pallas_call(
        kernel,
        out_shape=out_shape,
        in_specs=in_specs,
        compiler_params=pltpu.CompilerParams(vmem_limit_bytes=vmem * 2**20),
        **kw,
    )


VM = pl.BlockSpec(memory_space=pltpu.VMEM)
SM = pl.BlockSpec(memory_space=pltpu.SMEM)


def scaled_rows(g_ref, gain_ref, x):
    raw = g_ref[x].reshape(NZ * SLOT, -1).astype(F32)
    return raw, (raw * gain_ref[...]).astype(BF)


def over(lhs, w_ref, k):
    return lax.dot_general(lhs, w_ref[...], (((1,), (k,)), ((), ())), preferred_element_type=F32)


def small_kernel(pos_ref, g_ref, gain_ref, *refs):
    weights, out_ref = (refs[:2], refs[2:4]), refs[4]
    core = pos_ref[0]
    for x in range(NX):
        rows = slice(x * SLOT, x * SLOT + SLOT)
        raw, lhs = scaled_rows(g_ref, gain_ref, x)
        ss = jnp.sum(raw * raw, axis=1, keepdims=True)
        hi = ss.astype(BF).astype(F32)
        tail = [hi, ss - hi, jnp.zeros((NZ * SLOT, 58), F32)]
        for to, (wbc_ref, wdt_ref) in zip((core, 1 - core), weights):
            out = jnp.concatenate([over(lhs, wbc_ref, 1), over(lhs, wdt_ref, 1)] + tail, axis=1)
            out_ref[to, :, rows] = out.astype(BF).reshape(NZ, SLOT, 128)


def large_kernel(pos_ref, g_ref, gain_ref, *refs):
    weights, out_ref = (refs[:2], refs[2:4]), refs[4]
    core = pos_ref[0]
    for x in range(NX):
        rows = slice(x * SLOT, x * SLOT + SLOT)
        _, lhs = scaled_rows(g_ref, gain_ref, x)
        for to, pair in zip((core, 1 - core), weights):
            for i, w_ref in enumerate(pair):
                out = over(lhs, w_ref, 0).astype(BF).reshape(NZ, SLOT, 256)
                out_ref[to, :, rows, i * 256 : i * 256 + 256] = out


def slot_of(m):
    core, x, j = m // HALF, m % HALF // SLOT, m % SLOT
    step = (j * 11) // 32
    q = x * NC + core
    return step * RB + q * OWN + (j - step * OWN), j, q


def step_from_slot():
    i = lax.broadcasted_iota(jnp.int32, (STEPS * RB, BLOCK), 0)
    at, j, _ = slot_of(lax.broadcasted_iota(jnp.int32, (STEPS * RB, BLOCK), 1))
    return jnp.where((at == i) & (j < SLOT - 1), 1.0, 0.0).astype(BF)


def slot_from_step():
    shape = (BLOCK, STEPS * RB)
    at, j, q = slot_of(lax.broadcasted_iota(jnp.int32, shape, 0))
    i = lax.broadcasted_iota(jnp.int32, shape, 1)
    row = i % RB
    last = j == SLOT - 1
    order = jnp.where((at == i) & ~last, 1.0, 0.0).astype(BF)
    collect = jnp.where((row // OWN == q) & last, 1.0, 0.0).astype(BF)
    return order, collect


def conv(hist_ref, current, taps):
    seq = [hist_ref[k].astype(F32) for k in range(CONVK - 1)]
    seq += [current[t * RB : (t + 1) * RB] for t in range(STEPS)]
    out = []
    for t in range(STEPS):
        acc = taps[0:1] * seq[t]
        for k in range(1, CONVK):
            acc = acc + taps[k : k + 1] * seq[t + k]
        out.append(acc * jax.nn.sigmoid(acc))
    return out


def summed(p_ref):
    total = []
    for c in range(NC):
        part = p_ref[c * NY].astype(F32)
        for n in range(1, NY):
            part = part + p_ref[c * NY + n].astype(F32)
        total.append(part)
    return jnp.concatenate(total, axis=0)


def shared_kernel(p_ref, hist_ref, taps_ref, cur_ref, bcc_ref):
    total = summed(p_ref)
    rstd = lax.rsqrt((total[:, 68:69] + total[:, 69:70]) / D + EPS)
    lane = lax.broadcasted_iota(jnp.int32, (BLOCK, 128), 1)
    small, rest = total * rstd, rstd
    for k in range(3):
        piece = rest.astype(BF).astype(F32)
        small = jnp.where(lane == 70 + k, piece, small)
        rest = rest - piece
    cur = jnp.dot(step_from_slot(), small.astype(BF), preferred_element_type=F32)
    cur_ref[...] = cur.astype(BF)
    out = conv(hist_ref, cur[:, :64], taps_ref[...]) + [jnp.zeros((8, 64), F32)]
    out = jnp.concatenate(out, axis=0)
    bcc_ref[...] = jnp.concatenate([out[:64], out[64:]], axis=1).astype(BF)


def state_kernel(
    pos_ref, bc_0, bc_1, bc_2, bc_3, cur_ref, p_ref, params_ref, hist_ref, s_ref, u_ref,
    c_rows, y_rows, bc_ref,
):
    at = lambda v, t: v[t * RB : (t + 1) * RB]
    core, here = pos_ref[0], pos_ref[1]
    for shift, ref in enumerate((bc_0, bc_1, bc_2, bc_3)):
        frm = (here + NX - shift) % NX
        bc_ref[frm * NC + core] = ref[0].astype(F32)
        bc_ref[frm * NC + 1 - core] = ref[1].astype(F32)
    bc = [bc_ref[i] for i in range(NX * NC)]
    bc = [jnp.concatenate([v[:, :64], v[:, 64:]], axis=0) for v in bc]
    b_vec = jnp.concatenate(bc[:4], axis=1)
    c_vec = jnp.concatenate(bc[4:], axis=1)

    c_rows[...] = jnp.zeros_like(c_rows)
    for t in range(STEPS):
        for h in range(2):
            c_rows[h, pl.ds(t, RB, stride=8), :] = at(c_vec, t)[:, h * 128 : h * 128 + 128]
    for r in range(RB):
        c_row = jnp.concatenate([c_rows[h, r * 8 : r * 8 + 8, :] for h in range(2)], axis=1)
        y_row = lax.dot_general(
            c_row.astype(BF), s_ref[r], (((1,), (1,)), ((), ())), preferred_element_type=F32
        )
        for h in range(2):
            y_rows[h, r * 8 : r * 8 + 8, :] = y_row[:, h * 128 : h * 128 + 128]

    cur = cur_ref[...]
    taps, gain = params_ref[0:4], params_ref[4:5]
    a_log, bias, skip = params_ref[5:6], params_ref[6:7], params_ref[7:8]
    lane = lax.broadcasted_iota(jnp.int32, (128, 256), 0)
    head = lax.broadcasted_iota(jnp.int32, (128, 256), 1) // 64
    spread = jnp.where(lane == head + 64, 1.0, 0.0).astype(BF)
    dt_raw = jnp.dot(cur, spread, preferred_element_type=F32)
    pre = dt_raw + bias
    dt = jnp.maximum(pre, 0.0) + jnp.log1p(jnp.exp(-jnp.abs(pre)))
    decay = jnp.exp(-dt * jnp.exp(a_log))

    order, collect = slot_from_step()
    rstd = jnp.dot(order, cur, preferred_element_type=F32)
    rstd = rstd[:, 70:71] + rstd[:, 71:72] + rstd[:, 72:73]
    raw = (summed(p_ref) * rstd).astype(BF)
    raw = jnp.dot(step_from_slot(), raw, preferred_element_type=F32)
    gate = raw[:, 256:]
    gate = gate * jax.nn.sigmoid(gate)
    inner = conv(hist_ref, raw[:, :256], taps)
    carried, terms, gated = None, [], []
    for t in range(STEPS):
        d = at(decay, t)
        carried = d if carried is None else carried * d
        terms = [term * d for term in terms] + [at(dt, t) * inner[t]]
        held = [y_rows[h, pl.ds(t, RB, stride=8), :] for h in range(2)]
        y = carried * jnp.concatenate(held, axis=1) + skip * inner[t]
        for s in range(t + 1):
            y = y + jnp.sum(at(c_vec, t) * at(b_vec, s), axis=1, keepdims=True) * terms[s]
        gated.append(y * at(gate, t))
    gated = jnp.concatenate(gated, axis=0)
    ss = jnp.sum(gated * gated, axis=1, keepdims=True)
    hi = ss.astype(BF).astype(F32)
    lo = ss - hi
    row = lax.broadcasted_iota(jnp.int32, gated.shape, 0)
    lane = lax.broadcasted_iota(jnp.int32, gated.shape, 1)
    slot = row // RB * OWN + row % RB % OWN
    sums = jnp.where(lane == slot, hi, jnp.where(lane == slot + SLOT, lo, 0.0)).astype(BF)
    u = jnp.dot(order, (gated * gain).astype(BF), preferred_element_type=F32)
    u = (u + jnp.dot(collect, sums, preferred_element_type=F32)).astype(BF)
    for c in range(NC):
        for n in range(NY):
            u_ref[c * NY + n] = u[c * HALF : c * HALF + HALF]


def out_kernel(pos_ref, u_ref, w_ref, w_other_ref, o_ref):
    core = pos_ref[0]
    slot = lax.broadcasted_iota(jnp.int32, (NY * SLOT, 128), 0) % SLOT
    lane = lax.broadcasted_iota(jnp.int32, (NY * SLOT, 128), 1)
    for x in range(NX):
        rows = slice(x * SLOT, x * SLOT + SLOT)
        mine = u_ref[core, :, rows].reshape(NY * SLOT, 256)
        other = u_ref[1 - core, :, rows].reshape(NY * SLOT, 256)
        ss = mine[:, :128].astype(F32) + other[:, :128].astype(F32)
        ss = ss + pltpu.roll(ss, 128 - SLOT, 1)
        hi = ss.astype(BF).astype(F32)
        lo = pltpu.roll(ss - hi, SLOT, 1)
        kept = jnp.where(lane < SLOT, hi, jnp.where(lane < 2 * SLOT, lo, 0.0))
        for c in range(4):
            cols = slice(c * 256, c * 256 + 256)
            part = jnp.dot(mine, w_ref[:, cols], preferred_element_type=F32)
            part = part + jnp.dot(other, w_other_ref[:, cols], preferred_element_type=F32)
            if c == 0:
                first = jnp.where(slot == SLOT - 1, kept, part[:, :128])
                part = jnp.concatenate([first, part[:, 128:]], axis=1)
            o_ref[x, :, :, cols] = part.astype(BF).reshape(NZ, SLOT, 256)


def group_kernel(p_ref, o_ref):
    lane = lax.broadcasted_iota(jnp.int32, (SLOT, 128), 1)
    slot = lax.broadcasted_iota(jnp.int32, (SLOT, 128), 0)
    mask = (lane == slot) | (lane == slot + SLOT)
    for z in range(NZ):
        part = p_ref[0, z].astype(F32)
        for x in range(1, NX):
            part = part + p_ref[x, z].astype(F32)
        ss = jnp.broadcast_to(part[SLOT - 1 :, :128], (SLOT, 128))
        ss = jnp.sum(jnp.where(mask, ss, 0.0), axis=1, keepdims=True)
        o_ref[z] = (part * lax.rsqrt(ss / (DI // GROUPS) + EPS)).astype(BF)


def last_kernel(p_ref, x_ref, o_ref):
    acc = x_ref[...].astype(F32)
    for z in range(NZ):
        acc = acc + p_ref[z].astype(F32)
    for t in range(STEPS):
        o_ref[t] = acc[t * OWN : t * OWN + OWN].astype(BF)


def per_device(
    inputs, pre_gain, w_z, w_x, w_bc, w_dt, conv_x_w, conv_bc_w, conv_x_state, conv_bc_state,
    a_log, dt_bias, skip_d, ssm_state, norm_gain, w_out,
):
    shape = jax.ShapeDtypeStruct
    pos = jnp.stack([lax.axis_index("core"), lax.axis_index("x")]).astype(jnp.int32)
    narrow, broad = (w_bc.T, w_dt.T), (w_x, w_z)
    tokens = jnp.pad(inputs.reshape(STEPS * OWN, -1), ((0, 1), (0, 0)))
    gathered = to_all(to_all(tokens, "z", NZ), "x", NX)
    pair = lambda ws: (*ws, *(swap_core(w) for w in ws))
    small = call(small_kernel, shape((NC, NY, HALF, 128), BF), [SM] + [VM] * 6)(
        pos, gathered, pre_gain[None], *pair(narrow)
    )
    large = call(large_kernel, shape((NC, NY, HALF, 512), BF), [SM] + [VM] * 6)(
        pos, gathered, pre_gain[None], *pair(broad)
    )
    small, a_log, dt_bias, skip_d, norm_gain, conv_x_w = lax.optimization_barrier(
        (small, a_log, dt_bias, skip_d, norm_gain, conv_x_w)
    )
    heads = jnp.repeat(jnp.stack([a_log, dt_bias, skip_d]), 64, axis=1)
    params = jnp.concatenate([conv_x_w, norm_gain[None], heads], axis=0)

    small = exchange(small.reshape(NC * NY, HALF, 128), ("core", "y"))
    cur, bcc = call(
        shared_kernel, (shape((STEPS * RB, 128), BF), shape((64, 128), BF)), [VM] * 3
    )(small, jnp.swapaxes(conv_bc_state, 0, 1), conv_bc_w)
    large, bcc = lax.optimization_barrier((large, bcc))
    large = exchange(large.reshape(NC * NY, HALF, 512), ("core", "y"))
    vectors = jnp.stack([bcc, swap_core(bcc)])
    vectors = [vectors] + [
        lax.ppermute(vectors, "x", [(i, (i + k) % NX) for i in range(NX)]) for k in range(1, NX)
    ]
    u = call(
        state_kernel,
        shape((NC * NY, HALF, 256), BF),
        [SM] + [VM] * 9,
        scratch_shapes=[pltpu.VMEM((2, RB * 8, 128), F32)] * 2
        + [pltpu.VMEM((NX * NC, 64, 128), F32)],
    )(
        pos, *vectors, cur, large, params, jnp.swapaxes(conv_x_state, 0, 1),
        ssm_state.reshape(RB, 256, 256),
    )
    rows = exchange(u, ("core", "y")).reshape(NC, NY, HALF, 256)
    sums = call(out_kernel, shape((NX, NZ, SLOT, w_out.shape[1]), BF), [SM] + [VM] * 3)(
        pos, rows, w_out, swap_core(w_out)
    )
    sums = call(group_kernel, shape(sums.shape[1:], BF), [VM])(exchange(sums, "x"))
    return call(last_kernel, shape(inputs.shape, BF), [VM] * 2)(exchange(sums, "z"), tokens)


def solution(mesh):
    fine = Mesh(mesh.devices.reshape(NZ, NX, NC, NY), (*WIDE, "y"))
    return jax.shard_map(
        per_device,
        mesh=fine,
        in_specs=(
            P(None, WIDE, "y"),
            P("y"),
            P("y", WIDE),
            P("y", WIDE),
            P("y", WIDE),
            P("y", WIDE),
            P(None, WIDE),
            P(None, WIDE),
            P("y", None, WIDE),
            P("y", None, WIDE),
            P(WIDE),
            P(WIDE),
            P(WIDE),
            P("y", WIDE, None, None),
            P(WIDE),
            P(WIDE, "y"),
        ),
        out_specs=P(None, WIDE, "y"),
        check_vma=False,
    )
```

time: 177 us -> 153 us (0.86)
  the two profiles are of different devices: /device:TPU:2 before, /device:TPU:56 now
where the time goes in v2:
time: 153 us
  blocking collectives  55.7 us (36%)
  starting transfers between devices  44.7 us (29%)
  waiting for transfers between devices  36.6 us (24%)
  Pallas kernels  11.1 us (7%)
  local copies, waits for them, and re-layouts  4.15 us (3%)
    all_to_all x2, blocking collectives, exchange(): return lax.all_to_all(v, axes, split_axis=0, concat_axis=0, tiled=True)  33.7 us
    all_to_all x3, waiting for transfers between devices, exchange(): return lax.all_to_all(v, axes, split_axis=0, concat_axis=0, tiled=True)  26.3 us
    all_to_all x1, blocking collectives, to_all(): lax.all_to_all(jnp.broadcast_to(v[None], (count,) + v.shape), axes, split...  22 us
    all_to_all x3, starting transfers between devices, exchange(): return lax.all_to_all(v, axes, split_axis=0, concat_axis=0, tiled=True)  18.7 us
    ppermute x6, starting transfers between devices, swap_core(): return lax.ppermute(v, 'core', [(0, 1), (1, 0)])  12.7 us
    ppermute x3, starting transfers between devices, per_device(): lax.ppermute(vectors, 'x', [(i, (i + k) % NX) for i in range(NX)])  8.97 us
    all_to_all x1, starting transfers between devices, to_all(): lax.all_to_all(jnp.broadcast_to(v[None], (count,) + v.shape), axes, split...  4.29 us
    all_to_all x1, waiting for transfers between devices, to_all(): lax.all_to_all(jnp.broadcast_to(v[None], (count,) + v.shape), axes, split...  3.79 us
  transfers between devices with their start and end apart: 13, of which 9 were waited for; matrix products, arithmetic and copies ran while one was open for 0% of the time, Pallas kernels for 4%

profile of v2, /device:TPU:56, one launch (start us, length us, event | category | flops | bytes accessed | tf_op | source)
XLA Modules:
  0.0 152.6 jit_solution(852705205796694294)
XLA Ops:
  1.0 22.0 %all_to_all.35 = bf16[8,16,1024]{2,1,0:T(8,128)(2,1)S(1)} all-to-all(bf16[8,16,1024]{2,1,0:T(8,128)(2,1)S(1)} %broadcast_in_dim.10), channel_id=1, replica_groups=mesh['z'=8,'x'=4,'core'=2,'y'=8] {'z'}, dimensions={0} | all-to-all | bytes 524288 | tf_op jit(solution)/shard_map/all_to_all | solution.py:32
  24.1 4.3 %all-to-all-start.1 = ((bf16[4,8,16,1024]{3,2,1,0:T(8,128)(2,1)}), bf16[4,8,16,1024]{3,2,1,0:T(8,128)(2,1)S(1)}, u32[]{:S(2)}, u32[]{:S(2)}) async-start(bf16[4,8,16,1024]{3,2,1,0:T(8,128)(2,1)} %broadcast_in_dim.11), calls=%async_computation.1 | async-start | bytes 2097152 | tf_op jit(solution)/shard_map/all_to_all | solution.py:32
  28.4 1.9 %collective-permute-start.2 = (bf16[64,1024]{1,0:T(8,128)(2,1)S(1)}, bf16[64,1024]{1,0:T(8,128)(2,1)S(1)}, u32[]{:S(2)}, u32[]{:S(2)}) collective-permute-start(bf16[64,1024]{1,0:T(8,128)(2,1)S(1)} %bitcast.19), channel_id=1, source_target_pairs={{0,8},{8,0},{1,9},{9,1},{2,10},{10,2},{3,11},{11,3},{4,12},{12,4},... | collective-permute-start | bytes 393224 | tf_op jit(solution)/shard_map/ppermute | solution.py:28
  30.3 2.4 %collective-permute-start = (bf16[1024,256]{1,0:T(8,128)(2,1)S(1)}, bf16[1024,256]{1,0:T(8,128)(2,1)S(1)}, u32[]{:S(2)}, u32[]{:S(2)}) collective-permute-start(bf16[1024,256]{1,0:T(8,128)(2,1)S(1)} %copy-done.1), channel_id=1, source_target_pairs={{0,8},{8,0},{1,9},{9,1},{2,10},{10,2},{3,11},{11,3},{4,12},{12,4},... | collective-permute-start | bytes 1572872 | tf_op jit(solution)/shard_map/ppermute | solution.py:28
  32.7 1.9 %collective-permute-start.1 = (bf16[1024,256]{1,0:T(8,128)(2,1)S(1)}, bf16[1024,256]{1,0:T(8,128)(2,1)S(1)}, u32[]{:S(2)}, u32[]{:S(2)}) collective-permute-start(bf16[1024,256]{1,0:T(8,128)(2,1)S(1)} %copy-done.2), channel_id=1, source_target_pairs={{0,8},{8,0},{1,9},{9,1},{2,10},{10,2},{3,11},{11,3},{4,12},{12,4},... | collective-permute-start | bytes 1572872 | tf_op jit(solution)/shard_map/ppermute | solution.py:28
  34.7 2.4 %collective-permute-start.3 = (bf16[4,1024]{1,0:T(4,128)(2,1)S(1)}, bf16[4,1024]{1,0:T(4,128)(2,1)S(1)}, u32[]{:S(2)}, u32[]{:S(2)}) collective-permute-start(bf16[4,1024]{1,0:T(4,128)(2,1)S(1)} %bitcast.26), channel_id=1, source_target_pairs={{0,8},{8,0},{1,9},{9,1},{2,10},{10,2},{3,11},{11,3},{4,12},{12,4},... | collective-permute-start | bytes 24584 | tf_op jit(solution)/shard_map/ppermute | solution.py:28
  37.9 3.8 %all-to-all-done.1.g_ref = bf16[4,8,16,1024]{3,2,1,0:T(8,128)(2,1)S(1)} async-done(((bf16[4,8,16,1024]{3,2,1,0:T(8,128)(2,1)}), bf16[4,8,16,1024]{3,2,1,0:T(8,128)(2,1)S(1)}, u32[]{:S(2)}, u32[]{:S(2)}) %all-to-all-start.1) | async-done | bytes 1048608 | tf_op jit(solution)/shard_map/all_to_all | solution.py:32
  41.7 2.6 %shard_map.155 = bf16[2,8,64,128]{3,2,1,0:T(8,128)(2,1)} custom-call(s32[2]{0:T(128)S(1)} %pad_add_fusion.pos_ref, bf16[4,8,16,1024]{3,2,1,0:T(8,128)(2,1)S(1)} %all-to-all-done.1.g_ref, f32[1,1024]{1,0:T(1,128)S(1)} %bitcast.23, bf16[64,1024]{1,0:T(8,128)(2,1)S(1)} %bitcast.20, bf16[4,1024]{1,0:T(4,128)(2,1)S(1)} %bitcast.27, ...), custom_call_target="tpu_custom_call" | custom-call | tf_op jit(solution)/shard_map/pallas_call | solution.py:277
  44.3 6.9 %all-to-all-start.2 = ((bf16[16,64,128]{2,1,0:T(8,128)(2,1)}), bf16[16,64,128]{2,1,0:T(8,128)(2,1)S(1)}, u32[]{:S(2)}, u32[]{:S(2)}) async-start(bf16[16,64,128]{2,1,0:T(8,128)(2,1)} %bitcast.5), calls=%async_computation.2 | async-start | bytes 524288 | tf_op jit(solution)/shard_map/all_to_all | solution.py:38
  51.3 2.8 %shard_map.154 = bf16[2,8,64,512]{3,2,1,0:T(8,128)(2,1)} custom-call(s32[2]{0:T(128)S(1)} %pad_add_fusion.pos_ref, bf16[4,8,16,1024]{3,2,1,0:T(8,128)(2,1)S(1)} %all-to-all-done.1.g_ref, f32[1,1024]{1,0:T(1,128)S(1)} %bitcast.24, bf16[1024,256]{1,0:T(8,128)(2,1)S(1)} %copy-done.1, bf16[1024,256]{1,0:T(8,128)(2,1)S(1)} %copy-done.2, ...), custom_call_target="tpu_custom_call" | custom-call | tf_op jit(solution)/shard_map/pallas_call | solution.py:280
  54.0 6.0 %all-to-all-done.2.p_ref = bf16[16,64,128]{2,1,0:T(8,128)(2,1)S(1)} async-done(((bf16[16,64,128]{2,1,0:T(8,128)(2,1)}), bf16[16,64,128]{2,1,0:T(8,128)(2,1)S(1)}, u32[]{:S(2)}, u32[]{:S(2)}) %all-to-all-start.2) | async-done | bytes 262176 | tf_op jit(solution)/shard_map/all_to_all | solution.py:38
  60.5 5.8 %all-to-all-start.3 = ((bf16[16,64,512]{2,1,0:T(8,128)(2,1)}), bf16[16,64,512]{2,1,0:T(8,128)(2,1)S(1)}, u32[]{:S(2)}, u32[]{:S(2)}) async-start(bf16[16,64,512]{2,1,0:T(8,128)(2,1)} %bitcast.9), calls=%async_computation.3 | async-start | bytes 2097152 | tf_op jit(solution)/shard_map/all_to_all | solution.py:38
  66.3 2.0 %collective-permute-start.4 = (bf16[64,128]{1,0:T(8,128)(2,1)S(1)}, bf16[64,128]{1,0:T(8,128)(2,1)S(1)}, u32[]{:S(2)}, u32[]{:S(2)}) collective-permute-start(bf16[64,128]{1,0:T(8,128)(2,1)S(1)} %get-tuple-element.17), channel_id=1, source_target_pairs={{0,8},{8,0},{1,9},{9,1},{2,10},{10,2},{3,11},{11,3},{4,12},{12,4},... | collective-permute-start | bytes 49160 | tf_op jit(solution)/shard_map/ppermute | solution.py:28
  69.4 2.5 %collective-permute-start.5 = (bf16[2,64,128]{2,1,0:T(8,128)(2,1)S(1)}, bf16[2,64,128]{2,1,0:T(8,128)(2,1)S(1)}, u32[]{:S(2)}, u32[]{:S(2)}) collective-permute-start(bf16[2,64,128]{2,1,0:T(8,128)(2,1)S(1)} %pad_maximum_fusion.bc_0), channel_id=1, source_target_pairs={{0,16},{16,32},{32,48},{48,0},{1,17},{17,33},{33,49},{49,1},{2,18}... | collective-permute-start | bytes 98312 | tf_op jit(solution)/shard_map/ppermute | solution.py:297
  71.9 4.0 %collective-permute-start.6 = (bf16[2,64,128]{2,1,0:T(8,128)(2,1)S(1)}, bf16[2,64,128]{2,1,0:T(8,128)(2,1)S(1)}, u32[]{:S(2)}, u32[]{:S(2)}) collective-permute-start(bf16[2,64,128]{2,1,0:T(8,128)(2,1)S(1)} %pad_maximum_fusion.bc_0), channel_id=1, source_target_pairs={{0,32},{16,48},{32,0},{48,16},{1,33},{17,49},{33,1},{49,17},{2,34}... | collective-permute-start | bytes 98312 | tf_op jit(solution)/shard_map/ppermute | solution.py:297
  75.9 2.5 %collective-permute-start.7 = (bf16[2,64,128]{2,1,0:T(8,128)(2,1)S(1)}, bf16[2,64,128]{2,1,0:T(8,128)(2,1)S(1)}, u32[]{:S(2)}, u32[]{:S(2)}) collective-permute-start(bf16[2,64,128]{2,1,0:T(8,128)(2,1)S(1)} %pad_maximum_fusion.bc_0), channel_id=1, source_target_pairs={{0,48},{16,0},{32,16},{48,32},{1,49},{17,1},{33,17},{49,33},{2,50}... | collective-permute-start | bytes 98312 | tf_op jit(solution)/shard_map/ppermute | solution.py:297
  79.2 2.5 %collective-permute-done.7.bc_3 = bf16[2,64,128]{2,1,0:T(8,128)(2,1)S(1)} collective-permute-done((bf16[2,64,128]{2,1,0:T(8,128)(2,1)S(1)}, bf16[2,64,128]{2,1,0:T(8,128)(2,1)S(1)}, u32[]{:S(2)}, u32[]{:S(2)}) %collective-permute-start.7) | collective-permute-done | bytes 32800 | tf_op jit(solution)/shard_map/ppermute | solution.py:297
  81.7 10.2 %all-to-all-done.3.p_ref = bf16[16,64,512]{2,1,0:T(8,128)(2,1)S(1)} async-done(((bf16[16,64,512]{2,1,0:T(8,128)(2,1)}), bf16[16,64,512]{2,1,0:T(8,128)(2,1)S(1)}, u32[]{:S(2)}, u32[]{:S(2)}) %all-to-all-start.3) | async-done | bytes 1048608 | tf_op jit(solution)/shard_map/all_to_all | solution.py:38
  93.7 3.2 %shard_map.157 = bf16[16,64,256]{2,1,0:T(8,128)(2,1)} custom-call(s32[2]{0:T(128)S(1)} %pad_add_fusion.pos_ref, bf16[2,64,128]{2,1,0:T(8,128)(2,1)S(1)} %pad_maximum_fusion.bc_0, bf16[2,64,128]{2,1,0:T(8,128)(2,1)S(1)} %collective-permute-done.5.bc_1, bf16[2,64,128]{2,1,0:T(8,128)(2,1)S(1)} %collective-permute-done.6.bc_2, ...), custom_call_target="tpu_custom_call" | custom-call | tf_op jit(solution)/shard_map/pallas_call | solution.py:299
  96.9 5.9 %all-to-all-start.4 = ((bf16[16,64,256]{2,1,0:T(8,128)(2,1)}), bf16[16,64,256]{2,1,0:T(8,128)(2,1)S(1)}, u32[]{:S(2)}, u32[]{:S(2)}) async-start(bf16[16,64,256]{2,1,0:T(8,128)(2,1)} %shard_map.157), calls=%async_computation.4 | async-start | bytes 1048576 | tf_op jit(solution)/shard_map/all_to_all | solution.py:38
  102.9 2.1 %collective-permute-start.8 = (bf16[256,1024]{1,0:T(8,128)(2,1)S(1)}, bf16[256,1024]{1,0:T(8,128)(2,1)S(1)}, u32[]{:S(2)}, u32[]{:S(2)}) collective-permute-start(bf16[256,1024]{1,0:T(8,128)(2,1)S(1)} %copy-done.3), channel_id=1, source_target_pairs={{0,8},{8,0},{1,9},{9,1},{2,10},{10,2},{3,11},{11,3},{4,12},{12,4},... | collective-permute-start | bytes 1572872 | tf_op jit(solution)/shard_map/ppermute | solution.py:28
  106.7 10.1 %all-to-all-done.4 = bf16[16,64,256]{2,1,0:T(8,128)(2,1)S(1)} async-done(((bf16[16,64,256]{2,1,0:T(8,128)(2,1)}), bf16[16,64,256]{2,1,0:T(8,128)(2,1)S(1)}, u32[]{:S(2)}, u32[]{:S(2)}) %all-to-all-start.4) | async-done | bytes 524320 | tf_op jit(solution)/shard_map/all_to_all | solution.py:38
  118.1 18.7 %all_to_all.36.p_ref = bf16[4,8,16,1024]{3,2,1,0:T(8,128)(2,1)S(1)} all-to-all(bf16[4,8,16,1024]{3,2,1,0:T(8,128)(2,1)S(1)} %shard_map.158), channel_id=1, replica_groups=mesh['z'=8,'x'=4,'core'=2,'y'=8] {'x'}, dimensions={0} | all-to-all | bytes 2097152 | tf_op jit(solution)/shard_map/all_to_all | solution.py:38
  136.9 15.0 %all_to_all.37.p_ref = bf16[8,16,1024]{2,1,0:T(8,128)(2,1)S(1)} all-to-all(bf16[8,16,1024]{2,1,0:T(8,128)(2,1)S(1)} %shard_map.159), channel_id=1, replica_groups=mesh['z'=8,'x'=4,'core'=2,'y'=8] {'z'}, dimensions={0} | all-to-all | bytes 524288 | tf_op jit(solution)/shard_map/all_to_all | solution.py:38
  (52 shorter events, 10.8 us)
Async XLA Ops:
  0.0 28.4 %copy-start.4 = (bf16[1024,64]{0,1:T(8,128)(2,1)S(1)}, bf16[1024,64]{0,1:T(8,128)(2,1)}, u32[]{:S(2)}) copy-start(bf16[1024,64]{0,1:T(8,128)(2,1)} %param.20) | copy-start | bytes 393220
  0.0 30.3 %copy-start.1 = (bf16[1024,256]{1,0:T(8,128)(2,1)S(1)}, bf16[1024,256]{1,0:T(8,128)(2,1)}, u32[]{:S(2)}) copy-start(bf16[1024,256]{1,0:T(8,128)(2,1)} %refs_0_.1) | copy-start | bytes 1572868
  0.0 32.7 %copy-start.2 = (bf16[1024,256]{1,0:T(8,128)(2,1)S(1)}, bf16[1024,256]{1,0:T(8,128)(2,1)}, u32[]{:S(2)}) copy-start(bf16[1024,256]{1,0:T(8,128)(2,1)} %refs_1_.1) | copy-start | bytes 1572868
  0.0 34.6 %copy-start.8 = (bf16[1024,4]{0,1:T(4,128)(2,1)S(1)}, bf16[1024,4]{0,1:T(4,128)(2,1)}, u32[]{:S(2)}) copy-start(bf16[1024,4]{0,1:T(4,128)(2,1)} %param.21) | copy-start | bytes 24580
  0.0 41.7 %copy-start.7 = (f32[1024]{0:T(1024)S(1)}, f32[1024]{0:T(1024)}, u32[]{:S(2)}) copy-start(f32[1024]{0:T(1024)} %param.17) | copy-start | bytes 12292
  24.1 17.6 %all-to-all-start.1 = ((bf16[4,8,16,1024]{3,2,1,0:T(8,128)(2,1)}), bf16[4,8,16,1024]{3,2,1,0:T(8,128)(2,1)S(1)}, u32[]{:S(2)}, u32[]{:S(2)}) async-start(bf16[4,8,16,1024]{3,2,1,0:T(8,128)(2,1)} %broadcast_in_dim.11), calls=%async_computation.1 | async-start | bytes 2097152 | tf_op jit(solution)/shard_map/all_to_all | solution.py:32
  28.4 9.5 %collective-permute-start.2 = (bf16[64,1024]{1,0:T(8,128)(2,1)S(1)}, bf16[64,1024]{1,0:T(8,128)(2,1)S(1)}, u32[]{:S(2)}, u32[]{:S(2)}) collective-permute-start(bf16[64,1024]{1,0:T(8,128)(2,1)S(1)} %bitcast.19), channel_id=1, source_target_pairs={{0,8},{8,0},{1,9},{9,1},{2,10},{10,2},{3,11},{11,3},{4,12},{12,4},... | collective-permute-start | bytes 393224 | tf_op jit(solution)/shard_map/ppermute | solution.py:28
  30.3 20.9 %collective-permute-start = (bf16[1024,256]{1,0:T(8,128)(2,1)S(1)}, bf16[1024,256]{1,0:T(8,128)(2,1)S(1)}, u32[]{:S(2)}, u32[]{:S(2)}) collective-permute-start(bf16[1024,256]{1,0:T(8,128)(2,1)S(1)} %copy-done.1), channel_id=1, source_target_pairs={{0,8},{8,0},{1,9},{9,1},{2,10},{10,2},{3,11},{11,3},{4,12},{12,4},... | collective-permute-start | bytes 1572872 | tf_op jit(solution)/shard_map/ppermute | solution.py:28
  32.7 18.5 %collective-permute-start.1 = (bf16[1024,256]{1,0:T(8,128)(2,1)S(1)}, bf16[1024,256]{1,0:T(8,128)(2,1)S(1)}, u32[]{:S(2)}, u32[]{:S(2)}) collective-permute-start(bf16[1024,256]{1,0:T(8,128)(2,1)S(1)} %copy-done.2), channel_id=1, source_target_pairs={{0,8},{8,0},{1,9},{9,1},{2,10},{10,2},{3,11},{11,3},{4,12},{12,4},... | collective-permute-start | bytes 1572872 | tf_op jit(solution)/shard_map/ppermute | solution.py:28
  34.7 3.2 %collective-permute-start.3 = (bf16[4,1024]{1,0:T(4,128)(2,1)S(1)}, bf16[4,1024]{1,0:T(4,128)(2,1)S(1)}, u32[]{:S(2)}, u32[]{:S(2)}) collective-permute-start(bf16[4,1024]{1,0:T(4,128)(2,1)S(1)} %bitcast.26), channel_id=1, source_target_pairs={{0,8},{8,0},{1,9},{9,1},{2,10},{10,2},{3,11},{11,3},{4,12},{12,4},... | collective-permute-start | bytes 24584 | tf_op jit(solution)/shard_map/ppermute | solution.py:28
  41.7 18.4 %copy-start.6 = (bf16[24,3,64]{2,0,1:T(8,128)(2,1)S(1)}, bf16[24,3,64]{2,0,1:T(8,128)(2,1)}, u32[]{:S(2)}) copy-start(bf16[24,3,64]{2,0,1:T(8,128)(2,1)} %param.25) | copy-start | bytes 27652
  41.7 18.4 %copy-start.9 = (f32[4,64]{1,0:T(4,128)S(1)}, f32[4,64]{1,0:T(4,128)}, u32[]{:S(2)}) copy-start(f32[4,64]{1,0:T(4,128)} %taps_ref.1) | copy-start | bytes 3076
  44.3 15.8 %all-to-all-start.2 = ((bf16[16,64,128]{2,1,0:T(8,128)(2,1)}), bf16[16,64,128]{2,1,0:T(8,128)(2,1)S(1)}, u32[]{:S(2)}, u32[]{:S(2)}) async-start(bf16[16,64,128]{2,1,0:T(8,128)(2,1)} %bitcast.5), calls=%async_computation.2 | async-start | bytes 524288 | tf_op jit(solution)/shard_map/all_to_all | solution.py:38
  51.2 27.2 %copy-start.10 = (f32[4,256]{1,0:T(4,128)S(1)}, f32[4,256]{1,0:T(4,128)}, u32[]{:S(2)}) copy-start(f32[4,256]{1,0:T(4,128)} %param.22) | copy-start | bytes 12292
  51.2 27.2 %copy-start.11 = (f32[256]{0:T(256)S(1)}, f32[256]{0:T(256)}, u32[]{:S(2)}) copy-start(f32[256]{0:T(256)} %param.30) | copy-start | bytes 3076
  51.2 40.6 %copy-start.5 = (bf16[24,3,256]{2,0,1:T(8,128)(2,1)S(1)}, bf16[24,3,256]{2,0,1:T(8,128)(2,1)}, u32[]{:S(2)}) copy-start(bf16[24,3,256]{2,0,1:T(8,128)(2,1)} %param.24) | copy-start | bytes 110596
  60.5 42.4 %copy-start.3 = (bf16[256,1024]{1,0:T(8,128)(2,1)S(1)}, bf16[256,1024]{1,0:T(8,128)(2,1)}, u32[]{:S(2)}) copy-start(bf16[256,1024]{1,0:T(8,128)(2,1)} %w_ref.1) | copy-start | bytes 1572868
  60.5 31.4 %all-to-all-start.3 = ((bf16[16,64,512]{2,1,0:T(8,128)(2,1)}), bf16[16,64,512]{2,1,0:T(8,128)(2,1)S(1)}, u32[]{:S(2)}, u32[]{:S(2)}) async-start(bf16[16,64,512]{2,1,0:T(8,128)(2,1)} %bitcast.9), calls=%async_computation.3 | async-start | bytes 2097152 | tf_op jit(solution)/shard_map/all_to_all | solution.py:38
  66.3 3.1 %collective-permute-start.4 = (bf16[64,128]{1,0:T(8,128)(2,1)S(1)}, bf16[64,128]{1,0:T(8,128)(2,1)S(1)}, u32[]{:S(2)}, u32[]{:S(2)}) collective-permute-start(bf16[64,128]{1,0:T(8,128)(2,1)S(1)} %get-tuple-element.17), channel_id=1, source_target_pairs={{0,8},{8,0},{1,9},{9,1},{2,10},{10,2},{3,11},{11,3},{4,12},{12,4},... | collective-permute-start | bytes 49160 | tf_op jit(solution)/shard_map/ppermute | solution.py:28
  69.4 9.0 %collective-permute-start.5 = (bf16[2,64,128]{2,1,0:T(8,128)(2,1)S(1)}, bf16[2,64,128]{2,1,0:T(8,128)(2,1)S(1)}, u32[]{:S(2)}, u32[]{:S(2)}) collective-permute-start(bf16[2,64,128]{2,1,0:T(8,128)(2,1)S(1)} %pad_maximum_fusion.bc_0), channel_id=1, source_target_pairs={{0,16},{16,32},{32,48},{48,0},{1,17},{17,33},{33,49},{49,1},{2,18}... | collective-permute-start | bytes 98312 | tf_op jit(solution)/shard_map/ppermute | solution.py:297
  71.9 7.3 %collective-permute-start.6 = (bf16[2,64,128]{2,1,0:T(8,128)(2,1)S(1)}, bf16[2,64,128]{2,1,0:T(8,128)(2,1)S(1)}, u32[]{:S(2)}, u32[]{:S(2)}) collective-permute-start(bf16[2,64,128]{2,1,0:T(8,128)(2,1)S(1)} %pad_maximum_fusion.bc_0), channel_id=1, source_target_pairs={{0,32},{16,48},{32,0},{48,16},{1,33},{17,49},{33,1},{49,17},{2,34}... | collective-permute-start | bytes 98312 | tf_op jit(solution)/shard_map/ppermute | solution.py:297
  75.9 5.8 %collective-permute-start.7 = (bf16[2,64,128]{2,1,0:T(8,128)(2,1)S(1)}, bf16[2,64,128]{2,1,0:T(8,128)(2,1)S(1)}, u32[]{:S(2)}, u32[]{:S(2)}) collective-permute-start(bf16[2,64,128]{2,1,0:T(8,128)(2,1)S(1)} %pad_maximum_fusion.bc_0), channel_id=1, source_target_pairs={{0,48},{16,0},{32,16},{48,32},{1,49},{17,1},{33,17},{49,33},{2,50}... | collective-permute-start | bytes 98312 | tf_op jit(solution)/shard_map/ppermute | solution.py:297
  96.9 19.9 %all-to-all-start.4 = ((bf16[16,64,256]{2,1,0:T(8,128)(2,1)}), bf16[16,64,256]{2,1,0:T(8,128)(2,1)S(1)}, u32[]{:S(2)}, u32[]{:S(2)}) async-start(bf16[16,64,256]{2,1,0:T(8,128)(2,1)} %shard_map.157), calls=%async_computation.4 | async-start | bytes 1048576 | tf_op jit(solution)/shard_map/all_to_all | solution.py:38
  102.9 3.8 %collective-permute-start.8 = (bf16[256,1024]{1,0:T(8,128)(2,1)S(1)}, bf16[256,1024]{1,0:T(8,128)(2,1)S(1)}, u32[]{:S(2)}, u32[]{:S(2)}) collective-permute-start(bf16[256,1024]{1,0:T(8,128)(2,1)S(1)} %copy-done.3), channel_id=1, source_target_pairs={{0,8},{8,0},{1,9},{9,1},{2,10},{10,2},{3,11},{11,3},{4,12},{12,4},... | collective-permute-start | bytes 1572872 | tf_op jit(solution)/shard_map/ppermute | solution.py:28
  (4 other events, 53.6 us)

commit v3 on v2

--- a/solution.py
+++ b/solution.py
@@ -34,11 +34,16 @@
     )
 
 
+def around_x(v):
+    ways = [[(i, (i + k) % NX) for i in range(NX)] for k in range(1, NX)]
+    return [v] + [lax.ppermute(v, "x", way) for way in ways]
+
+
 def exchange(v, axes):
     return lax.all_to_all(v, axes, split_axis=0, concat_axis=0, tiled=True)
 
 
-def call(kernel, out_shape, in_specs, vmem=48, **kw):
+def call(kernel, out_shape, in_specs, vmem=32, **kw):
     return pl.pallas_call(
         kernel,
         out_shape=out_shape,
@@ -52,39 +57,62 @@
 SM = pl.BlockSpec(memory_space=pltpu.SMEM)
 
 
-def scaled_rows(g_ref, gain_ref, x):
-    raw = g_ref[x].reshape(NZ * SLOT, -1).astype(F32)
-    return raw, (raw * gain_ref[...]).astype(BF)
-
-
-def over(lhs, w_ref, k):
-    return lax.dot_general(lhs, w_ref[...], (((1,), (k,)), ((), ())), preferred_element_type=F32)
-
-
-def small_kernel(pos_ref, g_ref, gain_ref, *refs):
-    weights, out_ref = (refs[:2], refs[2:4]), refs[4]
+def over(lhs, w, k):
+    return lax.dot_general(lhs, w, (((1,), (k,)), ((), ())), preferred_element_type=F32)
+
+
+def into_empty(values, lanes, rows):
+    slot = lax.broadcasted_iota(jnp.int32, rows.shape, 0) % SLOT
+    total = jnp.sum(values.reshape(-1, SLOT, 128), axis=1, keepdims=True)
+    total = jnp.broadcast_to(total, (rows.shape[0] // SLOT, SLOT, 128)).reshape(rows.shape)
+    return jnp.where((slot == SLOT - 1) & lanes, total, rows)
+
+
+def small_kernel(pos_ref, g_ref, gain_ref, w_ref, w_other_ref, out_ref):
+    raw = g_ref[...].reshape(NX * NZ * SLOT, -1).astype(F32)
+    lhs = (raw * gain_ref[...]).astype(BF)
+    out = over(lhs, jnp.concatenate([w_ref[...], w_other_ref[...]], axis=0), 1)
+    ss = jnp.sum(raw * raw, axis=1, keepdims=True)
+    hi = ss.astype(BF).astype(F32)
+    lane = lax.broadcasted_iota(jnp.int32, out.shape, 1) % 64
+    slot = lax.broadcasted_iota(jnp.int32, out.shape, 0) % SLOT
+    ss = jnp.where(lane == slot, hi, jnp.where(lane == slot + SLOT, ss - hi, 0.0))
+    out = into_empty(ss, lane < 2 * SLOT, out).reshape(NX, NZ, SLOT, 128)
+    for x in range(2):
+        low, high = out[x], out[x + 2]
+        rows = slice(x * SLOT, x * SLOT + SLOT)
+        own = jnp.concatenate([low[:, :, :64], high[:, :, :64]], axis=2)
+        other = jnp.concatenate([low[:, :, 64:], high[:, :, 64:]], axis=2)
+        out_ref[pos_ref[0], :, rows] = own.astype(BF)
+        out_ref[1 - pos_ref[0], :, rows] = other.astype(BF)
+
+
+def large_kernel(pos_ref, g_ref, gain_ref, *refs):
+    weights, out_ref = refs[:6], refs[6]
+    size = NZ * SLOT
+    lhs = (g_ref[...].reshape(NX * size, -1).astype(F32) * gain_ref[...]).astype(BF)
+    heads = [
+        jnp.broadcast_to(ref[h : h + 1, :].astype(F32), (SLOT, D // NY))
+        for ref in weights[4:]
+        for h in range(4)
+    ]
+    sizes = over(lhs, jnp.concatenate(heads, axis=0).astype(BF), 1)
+    lane = lax.broadcasted_iota(jnp.int32, sizes.shape, 1)
+    slot = lax.broadcasted_iota(jnp.int32, sizes.shape, 0) % SLOT
+    sizes = jnp.where(lane % SLOT == slot, sizes, 0.0)
+    sizes = (sizes, pltpu.roll(sizes, 64, 1))
     core = pos_ref[0]
-    for x in range(NX):
-        rows = slice(x * SLOT, x * SLOT + SLOT)
-        raw, lhs = scaled_rows(g_ref, gain_ref, x)
-        ss = jnp.sum(raw * raw, axis=1, keepdims=True)
-        hi = ss.astype(BF).astype(F32)
-        tail = [hi, ss - hi, jnp.zeros((NZ * SLOT, 58), F32)]
-        for to, (wbc_ref, wdt_ref) in zip((core, 1 - core), weights):
-            out = jnp.concatenate([over(lhs, wbc_ref, 1), over(lhs, wdt_ref, 1)] + tail, axis=1)
-            out_ref[to, :, rows] = out.astype(BF).reshape(NZ, SLOT, 128)
-
-
-def large_kernel(pos_ref, g_ref, gain_ref, *refs):
-    weights, out_ref = (refs[:2], refs[2:4]), refs[4]
-    core = pos_ref[0]
-    for x in range(NX):
-        rows = slice(x * SLOT, x * SLOT + SLOT)
-        _, lhs = scaled_rows(g_ref, gain_ref, x)
-        for to, pair in zip((core, 1 - core), weights):
-            for i, w_ref in enumerate(pair):
-                out = over(lhs, w_ref, 0).astype(BF).reshape(NZ, SLOT, 256)
-                out_ref[to, :, rows, i * 256 : i * 256 + 256] = out
+    for i, w_ref in enumerate(weights[:4]):
+        to, cols = (core, 1 - core)[i // 2], slice(i % 2 * 256, i % 2 * 256 + 256)
+        out = jnp.dot(lhs, w_ref[...], preferred_element_type=F32)
+        if i % 2 == 0:
+            first = into_empty(sizes[i // 2], lane < 64, out[:, :128])
+            out = jnp.concatenate([first, out[:, 128:]], axis=1)
+        out = out.astype(BF)
+        for x in range(NX):
+            out_ref[to, :, x * SLOT : x * SLOT + SLOT, cols] = out[
+                x * size : x * size + size
+            ].reshape(NZ, SLOT, 256)
 
 
 def slot_of(m):
@@ -123,46 +151,56 @@
     return out
 
 
-def summed(p_ref):
+def empty_sums(rows):
+    slot = lax.broadcasted_iota(jnp.int32, rows.shape, 0) % SLOT
+    lane = lax.broadcasted_iota(jnp.int32, rows.shape, 1)
+    mask = (lane == slot) | (lane == slot + SLOT)
+    shape = (rows.shape[0] // SLOT, SLOT, rows.shape[1])
+    ss = jnp.broadcast_to(rows.reshape(shape)[:, SLOT - 1 :], shape).reshape(rows.shape)
+    return jnp.sum(jnp.where(mask, ss, 0.0), axis=1, keepdims=True)
+
+
+def shared_kernel(p_ref, hist_ref, taps_ref, rstd_ref, bcc_ref):
     total = []
     for c in range(NC):
         part = p_ref[c * NY].astype(F32)
         for n in range(1, NY):
             part = part + p_ref[c * NY + n].astype(F32)
-        total.append(part)
-    return jnp.concatenate(total, axis=0)
-
-
-def shared_kernel(p_ref, hist_ref, taps_ref, cur_ref, bcc_ref):
-    total = summed(p_ref)
-    rstd = lax.rsqrt((total[:, 68:69] + total[:, 69:70]) / D + EPS)
-    lane = lax.broadcasted_iota(jnp.int32, (BLOCK, 128), 1)
-    small, rest = total * rstd, rstd
+        total += [part[:, :64], part[:, 64:]]
+    total = jnp.concatenate(total, axis=0)
+    rest = rstd = lax.rsqrt(empty_sums(total) / D + EPS)
+    lane = lax.broadcasted_iota(jnp.int32, total.shape, 1)
+    factor = jnp.zeros(total.shape, F32)
     for k in range(3):
         piece = rest.astype(BF).astype(F32)
-        small = jnp.where(lane == 70 + k, piece, small)
+        factor = jnp.where(lane == k, piece, factor)
         rest = rest - piece
-    cur = jnp.dot(step_from_slot(), small.astype(BF), preferred_element_type=F32)
-    cur_ref[...] = cur.astype(BF)
+    raw = jnp.concatenate([total * rstd, factor], axis=1).astype(BF)
+    cur = jnp.dot(step_from_slot(), raw, preferred_element_type=F32)
+    rstd = cur[:, 64:65] + cur[:, 65:66] + cur[:, 66:67]
+    rstd_ref[...] = jnp.broadcast_to(rstd, rstd_ref.shape)
     out = conv(hist_ref, cur[:, :64], taps_ref[...]) + [jnp.zeros((8, 64), F32)]
     out = jnp.concatenate(out, axis=0)
     bcc_ref[...] = jnp.concatenate([out[:64], out[64:]], axis=1).astype(BF)
 
 
-def state_kernel(
-    pos_ref, bc_0, bc_1, bc_2, bc_3, cur_ref, p_ref, params_ref, hist_ref, s_ref, u_ref,
-    c_rows, y_rows, bc_ref,
+def at(v, t):
+    return v[t * RB : (t + 1) * RB]
+
+
+def carried_kernel(
+    pos_ref, bc_0, bc_1, bc_2, bc_3, rstd_ref, s_ref, y_ref, pairs_ref, sum_ref, empty_ref,
+    c_rows, y_rows, held,
 ):
-    at = lambda v, t: v[t * RB : (t + 1) * RB]
     core, here = pos_ref[0], pos_ref[1]
-    for shift, ref in enumerate((bc_0, bc_1, bc_2, bc_3)):
-        frm = (here + NX - shift) % NX
-        bc_ref[frm * NC + core] = ref[0].astype(F32)
-        bc_ref[frm * NC + 1 - core] = ref[1].astype(F32)
-    bc = [bc_ref[i] for i in range(NX * NC)]
-    bc = [jnp.concatenate([v[:, :64], v[:, 64:]], axis=0) for v in bc]
-    b_vec = jnp.concatenate(bc[:4], axis=1)
-    c_vec = jnp.concatenate(bc[4:], axis=1)
+    for k, ref in enumerate((bc_0, bc_1, bc_2, bc_3)):
+        frm = (here + NX - k) % NX
+        held[frm * NC + core] = ref[0].astype(F32)
+        held[frm * NC + 1 - core] = ref[1].astype(F32)
+    vectors = [held[i] for i in range(NX * NC)]
+    vectors = [jnp.concatenate([v[:, :64], v[:, 64:]], axis=0) for v in vectors]
+    b_vec = jnp.concatenate(vectors[:4], axis=1)
+    c_vec = jnp.concatenate(vectors[4:], axis=1)
 
     c_rows[...] = jnp.zeros_like(c_rows)
     for t in range(STEPS):
@@ -176,22 +214,48 @@
         for h in range(2):
             y_rows[h, r * 8 : r * 8 + 8, :] = y_row[:, h * 128 : h * 128 + 128]
 
-    cur = cur_ref[...]
+    for t in range(STEPS):
+        for h in range(2):
+            y_ref[t * RB : t * RB + RB, h * 128 : h * 128 + 128] = y_rows[h, pl.ds(t, RB, stride=8), :]
+    rstd = rstd_ref[...]
+    lane = lax.broadcasted_iota(jnp.int32, (RB, 128), 1)
+    for t in range(STEPS):
+        out = at(rstd, t)
+        for s in range(t + 1):
+            pair = jnp.sum(at(c_vec, t) * at(b_vec, s), axis=1, keepdims=True)
+            out = jnp.where(lane == s, pair, out)
+        pairs_ref[t * RB : t * RB + RB, :] = out
+    m = lax.broadcasted_iota(jnp.int32, (1, NC * NY * HALF), 1)
+    x, j = m % HALF // SLOT, m % SLOT
+    q = x * NC + m // (NY * HALF)
+    step = (j * 11) // 32
+    row = jnp.where(j < SLOT - 1, step * RB + q * OWN + j - step * OWN, -1)
+    i = lax.broadcasted_iota(jnp.int32, (STEPS * RB, 1), 0)
+    sum_ref[...] = jnp.where(row == i, 1.0, 0.0).astype(BF)
+    q = jnp.where(j == SLOT - 1, q, -1)
+    empty_ref[...] = jnp.where(q == i % RB // OWN, 1.0, 0.0).astype(BF)
+
+
+def state_kernel(y0_ref, pairs_ref, sum_ref, empty_ref, p_ref, params_ref, hist_ref, u_ref):
     taps, gain = params_ref[0:4], params_ref[4:5]
     a_log, bias, skip = params_ref[5:6], params_ref[6:7], params_ref[7:8]
+    pairs = pairs_ref[...]
+    rstd = pairs[:, 127:]
+    large = p_ref[...].reshape(NC * NY * HALF, 512)
+    sizes = jnp.dot(empty_ref[...], large[:, :128], preferred_element_type=F32) * rstd
+    row = lax.broadcasted_iota(jnp.int32, sizes.shape, 0)
+    lane = lax.broadcasted_iota(jnp.int32, sizes.shape, 1)
+    slot = row // RB * OWN + row % RB % OWN
+    sizes = jnp.where((lane % SLOT == slot) & (lane < 64), sizes, 0.0).astype(BF)
     lane = lax.broadcasted_iota(jnp.int32, (128, 256), 0)
     head = lax.broadcasted_iota(jnp.int32, (128, 256), 1) // 64
-    spread = jnp.where(lane == head + 64, 1.0, 0.0).astype(BF)
-    dt_raw = jnp.dot(cur, spread, preferred_element_type=F32)
-    pre = dt_raw + bias
+    spread = jnp.where(lane // SLOT == head, 1.0, 0.0).astype(BF)
+    pre = jnp.dot(sizes, spread, preferred_element_type=F32) + bias
     dt = jnp.maximum(pre, 0.0) + jnp.log1p(jnp.exp(-jnp.abs(pre)))
     decay = jnp.exp(-dt * jnp.exp(a_log))
-
     order, collect = slot_from_step()
-    rstd = jnp.dot(order, cur, preferred_element_type=F32)
-    rstd = rstd[:, 70:71] + rstd[:, 71:72] + rstd[:, 72:73]
-    raw = (summed(p_ref) * rstd).astype(BF)
-    raw = jnp.dot(step_from_slot(), raw, preferred_element_type=F32)
+    raw = jnp.dot(sum_ref[...], large, preferred_element_type=F32) * rstd
+    raw = raw.astype(BF).astype(F32)
     gate = raw[:, 256:]
     gate = gate * jax.nn.sigmoid(gate)
     inner = conv(hist_ref, raw[:, :256], taps)
@@ -200,10 +264,9 @@
         d = at(decay, t)
         carried = d if carried is None else carried * d
         terms = [term * d for term in terms] + [at(dt, t) * inner[t]]
-        held = [y_rows[h, pl.ds(t, RB, stride=8), :] for h in range(2)]
-        y = carried * jnp.concatenate(held, axis=1) + skip * inner[t]
+        y = carried * at(y0_ref, t) + skip * inner[t]
         for s in range(t + 1):
-            y = y + jnp.sum(at(c_vec, t) * at(b_vec, s), axis=1, keepdims=True) * terms[s]
+            y = y + at(pairs, t)[:, s : s + 1] * terms[s]
         gated.append(y * at(gate, t))
     gated = jnp.concatenate(gated, axis=0)
     ss = jnp.sum(gated * gated, axis=1, keepdims=True)
@@ -244,16 +307,12 @@
 
 
 def group_kernel(p_ref, o_ref):
-    lane = lax.broadcasted_iota(jnp.int32, (SLOT, 128), 1)
-    slot = lax.broadcasted_iota(jnp.int32, (SLOT, 128), 0)
-    mask = (lane == slot) | (lane == slot + SLOT)
     for z in range(NZ):
         part = p_ref[0, z].astype(F32)
         for x in range(1, NX):
             part = part + p_ref[x, z].astype(F32)
-        ss = jnp.broadcast_to(part[SLOT - 1 :, :128], (SLOT, 128))
-        ss = jnp.sum(jnp.where(mask, ss, 0.0), axis=1, keepdims=True)
-        o_ref[z] = (part * lax.rsqrt(ss / (DI // GROUPS) + EPS)).astype(BF)
+        scale = lax.rsqrt(empty_sums(part[:, :128]) / (DI // GROUPS) + EPS)
+        o_ref[z] = (part * scale).astype(BF)
 
 
 def last_kernel(p_ref, x_ref, o_ref):
@@ -270,15 +329,15 @@
 ):
     shape = jax.ShapeDtypeStruct
     pos = jnp.stack([lax.axis_index("core"), lax.axis_index("x")]).astype(jnp.int32)
-    narrow, broad = (w_bc.T, w_dt.T), (w_x, w_z)
     tokens = jnp.pad(inputs.reshape(STEPS * OWN, -1), ((0, 1), (0, 0)))
     gathered = to_all(to_all(tokens, "z", NZ), "x", NX)
-    pair = lambda ws: (*ws, *(swap_core(w) for w in ws))
-    small = call(small_kernel, shape((NC, NY, HALF, 128), BF), [SM] + [VM] * 6)(
-        pos, gathered, pre_gain[None], *pair(narrow)
-    )
-    large = call(large_kernel, shape((NC, NY, HALF, 512), BF), [SM] + [VM] * 6)(
-        pos, gathered, pre_gain[None], *pair(broad)
+    gain, w_bc, w_dt = pre_gain[None], w_bc.T, w_dt.T
+    small = call(small_kernel, shape((NC, NY, HALF // 2, 128), BF), [SM] + [VM] * 4)(
+        pos, gathered, gain, w_bc, swap_core(w_bc)
+    )
+    weights = (w_x, w_z, swap_core(w_x), swap_core(w_z), w_dt, swap_core(w_dt))
+    large = call(large_kernel, shape((NC, NY, HALF, 512), BF), [SM] + [VM] * 8)(
+        pos, gathered, gain, *weights
     )
     small, a_log, dt_bias, skip_d, norm_gain, conv_x_w = lax.optimization_barrier(
         (small, a_log, dt_bias, skip_d, norm_gain, conv_x_w)
@@ -286,25 +345,28 @@
     heads = jnp.repeat(jnp.stack([a_log, dt_bias, skip_d]), 64, axis=1)
     params = jnp.concatenate([conv_x_w, norm_gain[None], heads], axis=0)
 
-    small = exchange(small.reshape(NC * NY, HALF, 128), ("core", "y"))
-    cur, bcc = call(
-        shared_kernel, (shape((STEPS * RB, 128), BF), shape((64, 128), BF)), [VM] * 3
+    small = exchange(small.reshape(NC * NY, HALF // 2, 128), ("core", "y"))
+    rstd, bcc = call(
+        shared_kernel, (shape((STEPS * RB, 128), F32), shape((64, 128), BF)), [VM] * 3
     )(small, jnp.swapaxes(conv_bc_state, 0, 1), conv_bc_w)
     large, bcc = lax.optimization_barrier((large, bcc))
     large = exchange(large.reshape(NC * NY, HALF, 512), ("core", "y"))
-    vectors = jnp.stack([bcc, swap_core(bcc)])
-    vectors = [vectors] + [
-        lax.ppermute(vectors, "x", [(i, (i + k) % NX) for i in range(NX)]) for k in range(1, NX)
-    ]
-    u = call(
-        state_kernel,
-        shape((NC * NY, HALF, 256), BF),
-        [SM] + [VM] * 9,
+    ready = call(
+        carried_kernel,
+        (
+            shape((STEPS * RB, 256), F32),
+            shape((STEPS * RB, 128), F32),
+            shape((STEPS * RB, NC * NY * HALF), BF),
+            shape((STEPS * RB, NC * NY * HALF), BF),
+        ),
+        [SM] + [VM] * 6,
         scratch_shapes=[pltpu.VMEM((2, RB * 8, 128), F32)] * 2
         + [pltpu.VMEM((NX * NC, 64, 128), F32)],
     )(
-        pos, *vectors, cur, large, params, jnp.swapaxes(conv_x_state, 0, 1),
-        ssm_state.reshape(RB, 256, 256),
+        pos, *around_x(jnp.stack([bcc, swap_core(bcc)])), rstd, ssm_state.reshape(RB, 256, 256)
+    )
+    u = call(state_kernel, shape((NC * NY, HALF, 256), BF), [VM] * 7)(
+        *ready, large, params, jnp.swapaxes(conv_x_state, 0, 1)
     )
     rows = exchange(u, ("core", "y")).reshape(NC, NY, HALF, 256)
     sums = call(out_kernel, shape((NX, NZ, SLOT, w_out.shape[1]), BF), [SM] + [VM] * 3)(

time: 153 us -> 148 us (0.967)
  waiting for transfers between devices: 36.6 us -> 30.8 us
    all_to_all x3, waiting for transfers between devices: 26.3 us -> 17.3 us  [exchange(): return lax.all_to_all(v, axes, split_axis=0, concat_axis=0, tiled=True)]
    all_to_all x1, waiting for transfers between devices: 3.79 us -> 5.56 us  [to_all(): lax.all_to_all(jnp.broadcast_to(v[None], (count,) + v.shape), axes, split...]
    pallas_call x4 -> x5, Pallas kernels: 8.97 us -> 8.71 us  [the longest x1 3.06 us: per_device(): call(large_kernel, shape((NC, NY, HALF, 512), BF), [SM] + [VM] * 8)]
  transfers between devices with their start and end apart: 13 -> 13, of which waited for: 9 -> 10; matrix products, arithmetic and copies ran while one was open for 0% -> 0% of each run, Pallas kernels for 4% -> 4%
where the time goes in v3:
time: 148 us; the launch traced here: 147 us
  blocking collectives  55.7 us (38%)
  starting transfers between devices  45.4 us (31%)
  waiting for transfers between devices  30.8 us (21%)
  Pallas kernels  10.8 us (7%)
  local copies, waits for them, and re-layouts  4.15 us (3%)
    all_to_all x2, blocking collectives, exchange(): return lax.all_to_all(v, axes, split_axis=0, concat_axis=0, tiled=True)  33.7 us
    all_to_all x1, blocking collectives, to_all(): lax.all_to_all(jnp.broadcast_to(v[None], (count,) + v.shape), axes, split...  22 us
    all_to_all x3, starting transfers between devices, exchange(): return lax.all_to_all(v, axes, split_axis=0, concat_axis=0, tiled=True)  19.5 us
    all_to_all x3, waiting for transfers between devices, exchange(): return lax.all_to_all(v, axes, split_axis=0, concat_axis=0, tiled=True)  17.3 us
    ppermute x6, starting transfers between devices, swap_core(): return lax.ppermute(v, 'core', [(0, 1), (1, 0)])  12.7 us
    ppermute x3, starting transfers between devices, around_x(): return [v] + [lax.ppermute(v, 'x', way) for way in ways]  8.96 us
    all_to_all x1, waiting for transfers between devices, to_all(): lax.all_to_all(jnp.broadcast_to(v[None], (count,) + v.shape), axes, split...  5.56 us
    ppermute x6, waiting for transfers between devices, swap_core(): return lax.ppermute(v, 'core', [(0, 1), (1, 0)])  4.79 us
  transfers between devices with their start and end apart: 13, of which 10 were waited for; matrix products, arithmetic and copies ran while one was open for 0% of the time, Pallas kernels for 4%

profile of v3, /device:TPU:56, one launch (start us, length us, event | category | flops | bytes accessed | tf_op | source)
XLA Modules:
  0.0 147.3 jit_solution(11622059052973850099)
XLA Ops:
  1.0 22.0 %all_to_all.35 = bf16[8,16,1024]{2,1,0:T(8,128)(2,1)S(1)} all-to-all(bf16[8,16,1024]{2,1,0:T(8,128)(2,1)S(1)} %broadcast_in_dim.10), channel_id=1, replica_groups=mesh['z'=8,'x'=4,'core'=2,'y'=8] {'z'}, dimensions={0} | all-to-all | bytes 524288 | tf_op jit(solution)/shard_map/all_to_all | solution.py:32
  24.1 4.3 %all-to-all-start.1 = ((bf16[4,8,16,1024]{3,2,1,0:T(8,128)(2,1)}), bf16[4,8,16,1024]{3,2,1,0:T(8,128)(2,1)S(1)}, u32[]{:S(2)}, u32[]{:S(2)}) async-start(bf16[4,8,16,1024]{3,2,1,0:T(8,128)(2,1)} %broadcast_in_dim.22), calls=%async_computation.1 | async-start | bytes 2097152 | tf_op jit(solution)/shard_map/all_to_all | solution.py:32
  28.4 2.1 %collective-permute-start = (bf16[1024,256]{1,0:T(8,128)(2,1)S(1)}, bf16[1024,256]{1,0:T(8,128)(2,1)S(1)}, u32[]{:S(2)}, u32[]{:S(2)}) collective-permute-start(bf16[1024,256]{1,0:T(8,128)(2,1)S(1)} %copy-done.1), channel_id=1, source_target_pairs={{0,8},{8,0},{1,9},{9,1},{2,10},{10,2},{3,11},{11,3},{4,12},{12,4},... | collective-permute-start | bytes 1572872 | tf_op jit(solution)/shard_map/ppermute | solution.py:28
  30.4 2.4 %collective-permute-start.1 = (bf16[1024,256]{1,0:T(8,128)(2,1)S(1)}, bf16[1024,256]{1,0:T(8,128)(2,1)S(1)}, u32[]{:S(2)}, u32[]{:S(2)}) collective-permute-start(bf16[1024,256]{1,0:T(8,128)(2,1)S(1)} %copy-done.2), channel_id=1, source_target_pairs={{0,8},{8,0},{1,9},{9,1},{2,10},{10,2},{3,11},{11,3},{4,12},{12,4},... | collective-permute-start | bytes 1572872 | tf_op jit(solution)/shard_map/ppermute | solution.py:28
  32.9 1.9 %collective-permute-start.3 = (bf16[64,1024]{1,0:T(8,128)(2,1)S(1)}, bf16[64,1024]{1,0:T(8,128)(2,1)S(1)}, u32[]{:S(2)}, u32[]{:S(2)}) collective-permute-start(bf16[64,1024]{1,0:T(8,128)(2,1)S(1)} %bitcast.19), channel_id=1, source_target_pairs={{0,8},{8,0},{1,9},{9,1},{2,10},{10,2},{3,11},{11,3},{4,12},{12,4},... | collective-permute-start | bytes 393224 | tf_op jit(solution)/shard_map/ppermute | solution.py:28
  36.1 5.6 %all-to-all-done.1.g_ref = bf16[4,8,16,1024]{3,2,1,0:T(8,128)(2,1)S(1)} async-done(((bf16[4,8,16,1024]{3,2,1,0:T(8,128)(2,1)}), bf16[4,8,16,1024]{3,2,1,0:T(8,128)(2,1)S(1)}, u32[]{:S(2)}, u32[]{:S(2)}) %all-to-all-start.1) | async-done | bytes 1048608 | tf_op jit(solution)/shard_map/all_to_all | solution.py:32
  41.7 1.8 %shard_map.155 = bf16[2,8,32,128]{3,2,1,0:T(8,128)(2,1)} custom-call(s32[2]{0:T(128)S(1)} %pad_add_fusion.pos_ref, bf16[4,8,16,1024]{3,2,1,0:T(8,128)(2,1)S(1)} %all-to-all-done.1.g_ref, f32[1,1024]{1,0:T(1,128)S(1)} %bitcast.23, bf16[64,1024]{1,0:T(8,128)(2,1)S(1)} %bitcast.20, bf16[64,1024]{1,0:T(8,128)(2,1)S(1)} %collective-permute-done.3.w_other_ref), custom_call_target="tpu_custom_call" | custom-call | tf_op jit(solution)/shard_map/pallas_call | solution.py:335
  43.4 6.9 %all-to-all-start.2 = ((bf16[16,32,128]{2,1,0:T(8,128)(2,1)}), bf16[16,32,128]{2,1,0:T(8,128)(2,1)S(1)}, u32[]{:S(2)}, u32[]{:S(2)}) async-start(bf16[16,32,128]{2,1,0:T(8,128)(2,1)} %bitcast.5), calls=%async_computation.2 | async-start | bytes 262144 | tf_op jit(solution)/shard_map/all_to_all | solution.py:43
  50.4 2.2 %collective-permute-start.2 = (bf16[4,1024]{1,0:T(4,128)(2,1)S(1)}, bf16[4,1024]{1,0:T(4,128)(2,1)S(1)}, u32[]{:S(2)}, u32[]{:S(2)}) collective-permute-start(bf16[4,1024]{1,0:T(4,128)(2,1)S(1)} %bitcast.26), channel_id=1, source_target_pairs={{0,8},{8,0},{1,9},{9,1},{2,10},{10,2},{3,11},{11,3},{4,12},{12,4},... | collective-permute-start | bytes 24584 | tf_op jit(solution)/shard_map/ppermute | solution.py:28
  53.6 3.1 %shard_map.154 = bf16[2,8,64,512]{3,2,1,0:T(8,128)(2,1)} custom-call(s32[2]{0:T(128)S(1)} %pad_add_fusion.pos_ref, bf16[4,8,16,1024]{3,2,1,0:T(8,128)(2,1)S(1)} %all-to-all-done.1.g_ref, f32[1,1024]{1,0:T(1,128)S(1)} %bitcast.24, bf16[1024,256]{1,0:T(8,128)(2,1)S(1)} %copy-done.1, bf16[1024,256]{1,0:T(8,128)(2,1)S(1)} %copy-done.2, ...), custom_call_target="tpu_custom_call" | custom-call | tf_op jit(solution)/shard_map/pallas_call | solution.py:339
  57.8 6.7 %all-to-all-start.3 = ((bf16[16,64,512]{2,1,0:T(8,128)(2,1)}), bf16[16,64,512]{2,1,0:T(8,128)(2,1)S(1)}, u32[]{:S(2)}, u32[]{:S(2)}) async-start(bf16[16,64,512]{2,1,0:T(8,128)(2,1)} %bitcast.10), calls=%async_computation.3 | async-start | bytes 2097152 | tf_op jit(solution)/shard_map/all_to_all | solution.py:43
  64.4 2.0 %collective-permute-start.4 = (bf16[64,128]{1,0:T(8,128)(2,1)S(1)}, bf16[64,128]{1,0:T(8,128)(2,1)S(1)}, u32[]{:S(2)}, u32[]{:S(2)}) collective-permute-start(bf16[64,128]{1,0:T(8,128)(2,1)S(1)} %get-tuple-element.21), channel_id=1, source_target_pairs={{0,8},{8,0},{1,9},{9,1},{2,10},{10,2},{3,11},{11,3},{4,12},{12,4},... | collective-permute-start | bytes 49160 | tf_op jit(solution)/shard_map/ppermute | solution.py:28
  67.5 2.5 %collective-permute-start.5 = (bf16[2,64,128]{2,1,0:T(8,128)(2,1)S(1)}, bf16[2,64,128]{2,1,0:T(8,128)(2,1)S(1)}, u32[]{:S(2)}, u32[]{:S(2)}) collective-permute-start(bf16[2,64,128]{2,1,0:T(8,128)(2,1)S(1)} %pad_maximum_fusion.bc_0), channel_id=1, source_target_pairs={{0,16},{16,32},{32,48},{48,0},{1,17},{17,33},{33,49},{49,1},{2,18}... | collective-permute-start | bytes 98312 | tf_op jit(solution)/shard_map/ppermute | solution.py:39
  70.0 4.0 %collective-permute-start.6 = (bf16[2,64,128]{2,1,0:T(8,128)(2,1)S(1)}, bf16[2,64,128]{2,1,0:T(8,128)(2,1)S(1)}, u32[]{:S(2)}, u32[]{:S(2)}) collective-permute-start(bf16[2,64,128]{2,1,0:T(8,128)(2,1)S(1)} %pad_maximum_fusion.bc_0), channel_id=1, source_target_pairs={{0,32},{16,48},{32,0},{48,16},{1,33},{17,49},{33,1},{49,17},{2,34}... | collective-permute-start | bytes 98312 | tf_op jit(solution)/shard_map/ppermute | solution.py:39
  74.0 2.5 %collective-permute-start.7 = (bf16[2,64,128]{2,1,0:T(8,128)(2,1)S(1)}, bf16[2,64,128]{2,1,0:T(8,128)(2,1)S(1)}, u32[]{:S(2)}, u32[]{:S(2)}) collective-permute-start(bf16[2,64,128]{2,1,0:T(8,128)(2,1)S(1)} %pad_maximum_fusion.bc_0), channel_id=1, source_target_pairs={{0,48},{16,0},{32,16},{48,32},{1,49},{17,1},{33,17},{49,33},{2,50}... | collective-permute-start | bytes 98312 | tf_op jit(solution)/shard_map/ppermute | solution.py:39
  77.3 2.5 %collective-permute-done.7.bc_3 = bf16[2,64,128]{2,1,0:T(8,128)(2,1)S(1)} collective-permute-done((bf16[2,64,128]{2,1,0:T(8,128)(2,1)S(1)}, bf16[2,64,128]{2,1,0:T(8,128)(2,1)S(1)}, u32[]{:S(2)}, u32[]{:S(2)}) %collective-permute-start.7) | collective-permute-done | bytes 32800 | tf_op jit(solution)/shard_map/ppermute | solution.py:39
  79.8 1.9 %copy-done = bf16[24,4,64,256]{3,2,1,0:T(8,128)(2,1)S(1)} copy-done((bf16[24,4,64,256]{3,2,1,0:T(8,128)(2,1)S(1)}, bf16[24,4,64,256]{3,2,1,0:T(8,128)(2,1)}, u32[]{:S(2)}) %copy-start) | copy-done | bytes 3145752
  83.4 6.5 %all-to-all-done.3.p_ref = bf16[16,64,512]{2,1,0:T(8,128)(2,1)S(1)} async-done(((bf16[16,64,512]{2,1,0:T(8,128)(2,1)}), bf16[16,64,512]{2,1,0:T(8,128)(2,1)S(1)}, u32[]{:S(2)}, u32[]{:S(2)}) %all-to-all-start.3) | async-done | bytes 1048608 | tf_op jit(solution)/shard_map/all_to_all | solution.py:43
  91.6 5.9 %all-to-all-start.4 = ((bf16[16,64,256]{2,1,0:T(8,128)(2,1)}), bf16[16,64,256]{2,1,0:T(8,128)(2,1)S(1)}, u32[]{:S(2)}, u32[]{:S(2)}) async-start(bf16[16,64,256]{2,1,0:T(8,128)(2,1)} %shard_map.158), calls=%async_computation.4 | async-start | bytes 1048576 | tf_op jit(solution)/shard_map/all_to_all | solution.py:43
  97.5 2.1 %collective-permute-start.8 = (bf16[256,1024]{1,0:T(8,128)(2,1)S(1)}, bf16[256,1024]{1,0:T(8,128)(2,1)S(1)}, u32[]{:S(2)}, u32[]{:S(2)}) collective-permute-start(bf16[256,1024]{1,0:T(8,128)(2,1)S(1)} %copy-done.3), channel_id=1, source_target_pairs={{0,8},{8,0},{1,9},{9,1},{2,10},{10,2},{3,11},{11,3},{4,12},{12,4},... | collective-permute-start | bytes 1572872 | tf_op jit(solution)/shard_map/ppermute | solution.py:28
  99.6 1.7 %collective-permute-done.8.w_other_ref = bf16[256,1024]{1,0:T(8,128)(2,1)S(1)} collective-permute-done((bf16[256,1024]{1,0:T(8,128)(2,1)S(1)}, bf16[256,1024]{1,0:T(8,128)(2,1)S(1)}, u32[]{:S(2)}, u32[]{:S(2)}) %collective-permute-start.8) | collective-permute-done | bytes 524320 | tf_op jit(solution)/shard_map/ppermute | solution.py:28
  101.3 10.1 %all-to-all-done.4 = bf16[16,64,256]{2,1,0:T(8,128)(2,1)S(1)} async-done(((bf16[16,64,256]{2,1,0:T(8,128)(2,1)}), bf16[16,64,256]{2,1,0:T(8,128)(2,1)S(1)}, u32[]{:S(2)}, u32[]{:S(2)}) %all-to-all-start.4) | async-done | bytes 524320 | tf_op jit(solution)/shard_map/all_to_all | solution.py:43
  112.7 18.7 %all_to_all.36.p_ref = bf16[4,8,16,1024]{3,2,1,0:T(8,128)(2,1)S(1)} all-to-all(bf16[4,8,16,1024]{3,2,1,0:T(8,128)(2,1)S(1)} %shard_map.159), channel_id=1, replica_groups=mesh['z'=8,'x'=4,'core'=2,'y'=8] {'x'}, dimensions={0} | all-to-all | bytes 2097152 | tf_op jit(solution)/shard_map/all_to_all | solution.py:43
  131.6 15.0 %all_to_all.37.p_ref = bf16[8,16,1024]{2,1,0:T(8,128)(2,1)S(1)} all-to-all(bf16[8,16,1024]{2,1,0:T(8,128)(2,1)S(1)} %shard_map.160), channel_id=1, replica_groups=mesh['z'=8,'x'=4,'core'=2,'y'=8] {'z'}, dimensions={0} | all-to-all | bytes 524288 | tf_op jit(solution)/shard_map/all_to_all | solution.py:43
  (53 shorter events, 12.7 us)
Async XLA Ops:
  0.0 28.4 %copy-start.1 = (bf16[1024,256]{1,0:T(8,128)(2,1)S(1)}, bf16[1024,256]{1,0:T(8,128)(2,1)}, u32[]{:S(2)}) copy-start(bf16[1024,256]{1,0:T(8,128)(2,1)} %refs_0_.1) | copy-start | bytes 1572868
  0.0 30.4 %copy-start.2 = (bf16[1024,256]{1,0:T(8,128)(2,1)S(1)}, bf16[1024,256]{1,0:T(8,128)(2,1)}, u32[]{:S(2)}) copy-start(bf16[1024,256]{1,0:T(8,128)(2,1)} %refs_1_.1) | copy-start | bytes 1572868
  0.0 32.9 %copy-start.4 = (bf16[1024,64]{0,1:T(8,128)(2,1)S(1)}, bf16[1024,64]{0,1:T(8,128)(2,1)}, u32[]{:S(2)}) copy-start(bf16[1024,64]{0,1:T(8,128)(2,1)} %param.20) | copy-start | bytes 393220
  0.0 41.7 %copy-start.7 = (f32[1024]{0:T(1024)S(1)}, f32[1024]{0:T(1024)}, u32[]{:S(2)}) copy-start(f32[1024]{0:T(1024)} %param.17) | copy-start | bytes 12292
  0.0 50.3 %copy-start.8 = (bf16[1024,4]{0,1:T(4,128)(2,1)S(1)}, bf16[1024,4]{0,1:T(4,128)(2,1)}, u32[]{:S(2)}) copy-start(bf16[1024,4]{0,1:T(4,128)(2,1)} %param.21) | copy-start | bytes 24580
  24.1 17.6 %all-to-all-start.1 = ((bf16[4,8,16,1024]{3,2,1,0:T(8,128)(2,1)}), bf16[4,8,16,1024]{3,2,1,0:T(8,128)(2,1)S(1)}, u32[]{:S(2)}, u32[]{:S(2)}) async-start(bf16[4,8,16,1024]{3,2,1,0:T(8,128)(2,1)} %broadcast_in_dim.22), calls=%async_computation.1 | async-start | bytes 2097152 | tf_op jit(solution)/shard_map/all_to_all | solution.py:32
  28.4 28.9 %copy-start.6 = (bf16[24,3,64]{2,0,1:T(8,128)(2,1)S(1)}, bf16[24,3,64]{2,0,1:T(8,128)(2,1)}, u32[]{:S(2)}) copy-start(bf16[24,3,64]{2,0,1:T(8,128)(2,1)} %param.25) | copy-start | bytes 27652
  28.4 28.9 %copy-start.9 = (f32[4,64]{1,0:T(4,128)S(1)}, f32[4,64]{1,0:T(4,128)}, u32[]{:S(2)}) copy-start(f32[4,64]{1,0:T(4,128)} %taps_ref.1) | copy-start | bytes 3076
  28.4 25.2 %collective-permute-start = (bf16[1024,256]{1,0:T(8,128)(2,1)S(1)}, bf16[1024,256]{1,0:T(8,128)(2,1)S(1)}, u32[]{:S(2)}, u32[]{:S(2)}) collective-permute-start(bf16[1024,256]{1,0:T(8,128)(2,1)S(1)} %copy-done.1), channel_id=1, source_target_pairs={{0,8},{8,0},{1,9},{9,1},{2,10},{10,2},{3,11},{11,3},{4,12},{12,4},... | collective-permute-start | bytes 1572872 | tf_op jit(solution)/shard_map/ppermute | solution.py:28
  30.4 23.1 %collective-permute-start.1 = (bf16[1024,256]{1,0:T(8,128)(2,1)S(1)}, bf16[1024,256]{1,0:T(8,128)(2,1)S(1)}, u32[]{:S(2)}, u32[]{:S(2)}) collective-permute-start(bf16[1024,256]{1,0:T(8,128)(2,1)S(1)} %copy-done.2), channel_id=1, source_target_pairs={{0,8},{8,0},{1,9},{9,1},{2,10},{10,2},{3,11},{11,3},{4,12},{12,4},... | collective-permute-start | bytes 1572872 | tf_op jit(solution)/shard_map/ppermute | solution.py:28
  32.9 3.2 %collective-permute-start.3 = (bf16[64,1024]{1,0:T(8,128)(2,1)S(1)}, bf16[64,1024]{1,0:T(8,128)(2,1)S(1)}, u32[]{:S(2)}, u32[]{:S(2)}) collective-permute-start(bf16[64,1024]{1,0:T(8,128)(2,1)S(1)} %bitcast.19), channel_id=1, source_target_pairs={{0,8},{8,0},{1,9},{9,1},{2,10},{10,2},{3,11},{11,3},{4,12},{12,4},... | collective-permute-start | bytes 393224 | tf_op jit(solution)/shard_map/ppermute | solution.py:28
  43.4 13.8 %all-to-all-start.2 = ((bf16[16,32,128]{2,1,0:T(8,128)(2,1)}), bf16[16,32,128]{2,1,0:T(8,128)(2,1)S(1)}, u32[]{:S(2)}, u32[]{:S(2)}) async-start(bf16[16,32,128]{2,1,0:T(8,128)(2,1)} %bitcast.5), calls=%async_computation.2 | async-start | bytes 262144 | tf_op jit(solution)/shard_map/all_to_all | solution.py:43
  50.3 16.2 %copy-start.12 = (f32[4]{0:T(128)S(1)}, f32[4]{0:T(128)}, u32[]{:S(2)}) copy-start(f32[4]{0:T(128)} %param.28) | copy-start | bytes 52
  50.4 26.1 %copy-start.10 = (f32[4,256]{1,0:T(4,128)S(1)}, f32[4,256]{1,0:T(4,128)}, u32[]{:S(2)}) copy-start(f32[4,256]{1,0:T(4,128)} %param.22) | copy-start | bytes 12292
  50.4 26.1 %copy-start.11 = (f32[256]{0:T(256)S(1)}, f32[256]{0:T(256)}, u32[]{:S(2)}) copy-start(f32[256]{0:T(256)} %param.30) | copy-start | bytes 3076
  50.4 3.2 %collective-permute-start.2 = (bf16[4,1024]{1,0:T(4,128)(2,1)S(1)}, bf16[4,1024]{1,0:T(4,128)(2,1)S(1)}, u32[]{:S(2)}, u32[]{:S(2)}) collective-permute-start(bf16[4,1024]{1,0:T(4,128)(2,1)S(1)} %bitcast.26), channel_id=1, source_target_pairs={{0,8},{8,0},{1,9},{9,1},{2,10},{10,2},{3,11},{11,3},{4,12},{12,4},... | collective-permute-start | bytes 24584 | tf_op jit(solution)/shard_map/ppermute | solution.py:28
  56.7 33.3 %copy-start.5 = (bf16[24,3,256]{2,0,1:T(8,128)(2,1)S(1)}, bf16[24,3,256]{2,0,1:T(8,128)(2,1)}, u32[]{:S(2)}) copy-start(bf16[24,3,256]{2,0,1:T(8,128)(2,1)} %param.24) | copy-start | bytes 110596
  57.8 32.2 %all-to-all-start.3 = ((bf16[16,64,512]{2,1,0:T(8,128)(2,1)}), bf16[16,64,512]{2,1,0:T(8,128)(2,1)S(1)}, u32[]{:S(2)}, u32[]{:S(2)}) async-start(bf16[16,64,512]{2,1,0:T(8,128)(2,1)} %bitcast.10), calls=%async_computation.3 | async-start | bytes 2097152 | tf_op jit(solution)/shard_map/all_to_all | solution.py:43
  64.4 3.1 %collective-permute-start.4 = (bf16[64,128]{1,0:T(8,128)(2,1)S(1)}, bf16[64,128]{1,0:T(8,128)(2,1)S(1)}, u32[]{:S(2)}, u32[]{:S(2)}) collective-permute-start(bf16[64,128]{1,0:T(8,128)(2,1)S(1)} %get-tuple-element.21), channel_id=1, source_target_pairs={{0,8},{8,0},{1,9},{9,1},{2,10},{10,2},{3,11},{11,3},{4,12},{12,4},... | collective-permute-start | bytes 49160 | tf_op jit(solution)/shard_map/ppermute | solution.py:28
  67.5 9.0 %collective-permute-start.5 = (bf16[2,64,128]{2,1,0:T(8,128)(2,1)S(1)}, bf16[2,64,128]{2,1,0:T(8,128)(2,1)S(1)}, u32[]{:S(2)}, u32[]{:S(2)}) collective-permute-start(bf16[2,64,128]{2,1,0:T(8,128)(2,1)S(1)} %pad_maximum_fusion.bc_0), channel_id=1, source_target_pairs={{0,16},{16,32},{32,48},{48,0},{1,17},{17,33},{33,49},{49,1},{2,18}... | collective-permute-start | bytes 98312 | tf_op jit(solution)/shard_map/ppermute | solution.py:39
  70.0 7.3 %collective-permute-start.6 = (bf16[2,64,128]{2,1,0:T(8,128)(2,1)S(1)}, bf16[2,64,128]{2,1,0:T(8,128)(2,1)S(1)}, u32[]{:S(2)}, u32[]{:S(2)}) collective-permute-start(bf16[2,64,128]{2,1,0:T(8,128)(2,1)S(1)} %pad_maximum_fusion.bc_0), channel_id=1, source_target_pairs={{0,32},{16,48},{32,0},{48,16},{1,33},{17,49},{33,1},{49,17},{2,34}... | collective-permute-start | bytes 98312 | tf_op jit(solution)/shard_map/ppermute | solution.py:39
  74.0 5.8 %collective-permute-start.7 = (bf16[2,64,128]{2,1,0:T(8,128)(2,1)S(1)}, bf16[2,64,128]{2,1,0:T(8,128)(2,1)S(1)}, u32[]{:S(2)}, u32[]{:S(2)}) collective-permute-start(bf16[2,64,128]{2,1,0:T(8,128)(2,1)S(1)} %pad_maximum_fusion.bc_0), channel_id=1, source_target_pairs={{0,48},{16,0},{32,16},{48,32},{1,49},{17,1},{33,17},{49,33},{2,50}... | collective-permute-start | bytes 98312 | tf_op jit(solution)/shard_map/ppermute | solution.py:39
  91.6 19.9 %all-to-all-start.4 = ((bf16[16,64,256]{2,1,0:T(8,128)(2,1)}), bf16[16,64,256]{2,1,0:T(8,128)(2,1)S(1)}, u32[]{:S(2)}, u32[]{:S(2)}) async-start(bf16[16,64,256]{2,1,0:T(8,128)(2,1)} %shard_map.158), calls=%async_computation.4 | async-start | bytes 1048576 | tf_op jit(solution)/shard_map/all_to_all | solution.py:43
  97.5 3.8 %collective-permute-start.8 = (bf16[256,1024]{1,0:T(8,128)(2,1)S(1)}, bf16[256,1024]{1,0:T(8,128)(2,1)S(1)}, u32[]{:S(2)}, u32[]{:S(2)}) collective-permute-start(bf16[256,1024]{1,0:T(8,128)(2,1)S(1)} %copy-done.3), channel_id=1, source_target_pairs={{0,8},{8,0},{1,9},{9,1},{2,10},{10,2},{3,11},{11,3},{4,12},{12,4},... | collective-permute-start | bytes 1572872 | tf_op jit(solution)/shard_map/ppermute | solution.py:28
  (4 other events, 50.1 us)

commit v4 on v3

--- a/solution.py
+++ b/solution.py
@@ -1,3 +1,5 @@
+import functools
+
 import jax
 import jax.numpy as jnp
 from jax import lax
@@ -34,9 +36,11 @@
     )
 
 
+NEXT, ACROSS, PREVIOUS = ([(i, (i + k) % NX) for i in range(NX)] for k in (1, 2, 3))
+
+
 def around_x(v):
-    ways = [[(i, (i + k) % NX) for i in range(NX)] for k in range(1, NX)]
-    return [v] + [lax.ppermute(v, "x", way) for way in ways]
+    return [v] + [lax.ppermute(v, "x", way) for way in (NEXT, ACROSS, PREVIOUS)]
 
 
 def exchange(v, axes):
@@ -189,8 +193,7 @@
 
 
 def carried_kernel(
-    pos_ref, bc_0, bc_1, bc_2, bc_3, rstd_ref, s_ref, y_ref, pairs_ref, sum_ref, empty_ref,
-    c_rows, y_rows, held,
+    pos_ref, bc_0, bc_1, bc_2, bc_3, rstd_ref, s_ref, out_ref, c_rows, y_rows, held
 ):
     core, here = pos_ref[0], pos_ref[1]
     for k, ref in enumerate((bc_0, bc_1, bc_2, bc_3)):
@@ -216,7 +219,7 @@
 
     for t in range(STEPS):
         for h in range(2):
-            y_ref[t * RB : t * RB + RB, h * 128 : h * 128 + 128] = y_rows[h, pl.ds(t, RB, stride=8), :]
+            out_ref[t * RB : t * RB + RB, h * 128 : h * 128 + 128] = y_rows[h, pl.ds(t, RB, stride=8), :]
     rstd = rstd_ref[...]
     lane = lax.broadcasted_iota(jnp.int32, (RB, 128), 1)
     for t in range(STEPS):
@@ -224,25 +227,25 @@
         for s in range(t + 1):
             pair = jnp.sum(at(c_vec, t) * at(b_vec, s), axis=1, keepdims=True)
             out = jnp.where(lane == s, pair, out)
-        pairs_ref[t * RB : t * RB + RB, :] = out
+        out_ref[t * RB : t * RB + RB, 256:] = out
+
+
+def state_kernel(ready_ref, p_ref, params_ref, hist_ref, u_ref):
     m = lax.broadcasted_iota(jnp.int32, (1, NC * NY * HALF), 1)
     x, j = m % HALF // SLOT, m % SLOT
     q = x * NC + m // (NY * HALF)
     step = (j * 11) // 32
     row = jnp.where(j < SLOT - 1, step * RB + q * OWN + j - step * OWN, -1)
     i = lax.broadcasted_iota(jnp.int32, (STEPS * RB, 1), 0)
-    sum_ref[...] = jnp.where(row == i, 1.0, 0.0).astype(BF)
+    gather = jnp.where(row == i, 1.0, 0.0).astype(BF)
     q = jnp.where(j == SLOT - 1, q, -1)
-    empty_ref[...] = jnp.where(q == i % RB // OWN, 1.0, 0.0).astype(BF)
-
-
-def state_kernel(y0_ref, pairs_ref, sum_ref, empty_ref, p_ref, params_ref, hist_ref, u_ref):
+    empty = jnp.where(q == i % RB // OWN, 1.0, 0.0).astype(BF)
     taps, gain = params_ref[0:4], params_ref[4:5]
     a_log, bias, skip = params_ref[5:6], params_ref[6:7], params_ref[7:8]
-    pairs = pairs_ref[...]
+    y0, pairs = ready_ref[:, :256], ready_ref[:, 256:]
     rstd = pairs[:, 127:]
     large = p_ref[...].reshape(NC * NY * HALF, 512)
-    sizes = jnp.dot(empty_ref[...], large[:, :128], preferred_element_type=F32) * rstd
+    sizes = jnp.dot(empty, large[:, :128], preferred_element_type=F32) * rstd
     row = lax.broadcasted_iota(jnp.int32, sizes.shape, 0)
     lane = lax.broadcasted_iota(jnp.int32, sizes.shape, 1)
     slot = row // RB * OWN + row % RB % OWN
@@ -254,7 +257,7 @@
     dt = jnp.maximum(pre, 0.0) + jnp.log1p(jnp.exp(-jnp.abs(pre)))
     decay = jnp.exp(-dt * jnp.exp(a_log))
     order, collect = slot_from_step()
-    raw = jnp.dot(sum_ref[...], large, preferred_element_type=F32) * rstd
+    raw = jnp.dot(gather, large, preferred_element_type=F32) * rstd
     raw = raw.astype(BF).astype(F32)
     gate = raw[:, 256:]
     gate = gate * jax.nn.sigmoid(gate)
@@ -264,7 +267,7 @@
         d = at(decay, t)
         carried = d if carried is None else carried * d
         terms = [term * d for term in terms] + [at(dt, t) * inner[t]]
-        y = carried * at(y0_ref, t) + skip * inner[t]
+        y = carried * at(y0, t) + skip * inner[t]
         for s in range(t + 1):
             y = y + at(pairs, t)[:, s : s + 1] * terms[s]
         gated.append(y * at(gate, t))
@@ -278,41 +281,41 @@
     sums = jnp.where(lane == slot, hi, jnp.where(lane == slot + SLOT, lo, 0.0)).astype(BF)
     u = jnp.dot(order, (gated * gain).astype(BF), preferred_element_type=F32)
     u = (u + jnp.dot(collect, sums, preferred_element_type=F32)).astype(BF)
-    for c in range(NC):
-        for n in range(NY):
-            u_ref[c * NY + n] = u[c * HALF : c * HALF + HALF]
-
-
-def out_kernel(pos_ref, u_ref, w_ref, w_other_ref, o_ref):
-    core = pos_ref[0]
-    slot = lax.broadcasted_iota(jnp.int32, (NY * SLOT, 128), 0) % SLOT
-    lane = lax.broadcasted_iota(jnp.int32, (NY * SLOT, 128), 1)
     for x in range(NX):
-        rows = slice(x * SLOT, x * SLOT + SLOT)
-        mine = u_ref[core, :, rows].reshape(NY * SLOT, 256)
-        other = u_ref[1 - core, :, rows].reshape(NY * SLOT, 256)
-        ss = mine[:, :128].astype(F32) + other[:, :128].astype(F32)
+        for c in range(NC):
+            first = c * HALF + x * SLOT
+            for n in range(NY):
+                u_ref[x, n, c] = u[first : first + SLOT]
+
+
+def out_kernel(own, pos_ref, u_ref, w_ref, left_ref, low_ref, high_ref, right_ref, o_ref):
+    core, here = pos_ref[0], pos_ref[1]
+    which = core if own else 1 - core
+    rows = [
+        u_ref[(here + NX - k) % NX, :, which].reshape(NY * SLOT, 256) for k in range(NX)
+    ]
+    ss = rows[0][:, :128].astype(F32)
+    for r in rows[1:]:
+        ss = ss + r[:, :128].astype(F32)
+    if not own:
+        lane = lax.broadcasted_iota(jnp.int32, ss.shape, 1)
         ss = ss + pltpu.roll(ss, 128 - SLOT, 1)
         hi = ss.astype(BF).astype(F32)
         lo = pltpu.roll(ss - hi, SLOT, 1)
-        kept = jnp.where(lane < SLOT, hi, jnp.where(lane < 2 * SLOT, lo, 0.0))
-        for c in range(4):
-            cols = slice(c * 256, c * 256 + 256)
-            part = jnp.dot(mine, w_ref[:, cols], preferred_element_type=F32)
-            part = part + jnp.dot(other, w_other_ref[:, cols], preferred_element_type=F32)
-            if c == 0:
-                first = jnp.where(slot == SLOT - 1, kept, part[:, :128])
-                part = jnp.concatenate([first, part[:, 128:]], axis=1)
-            o_ref[x, :, :, cols] = part.astype(BF).reshape(NZ, SLOT, 256)
-
-
-def group_kernel(p_ref, o_ref):
-    for z in range(NZ):
-        part = p_ref[0, z].astype(F32)
-        for x in range(1, NX):
-            part = part + p_ref[x, z].astype(F32)
-        scale = lax.rsqrt(empty_sums(part[:, :128]) / (DI // GROUPS) + EPS)
-        o_ref[z] = (part * scale).astype(BF)
+        ss = jnp.where(lane < SLOT, hi, jnp.where(lane < 2 * SLOT, lo, 0.0))
+    dot = lambda v, w: jnp.dot(v, w[...], preferred_element_type=F32)
+    total = dot(rows[0], w_ref) + dot(rows[1], left_ref) + dot(rows[3], right_ref)
+    total = total + dot(rows[2][:, :128], low_ref) + dot(rows[2][:, 128:], high_ref)
+    slot = lax.broadcasted_iota(jnp.int32, ss.shape, 0) % SLOT
+    first = jnp.where(slot == SLOT - 1, ss, total[:, :128])
+    total = jnp.concatenate([first, total[:, 128:]], axis=1)
+    o_ref[...] = total.astype(o_ref.dtype).reshape(o_ref.shape)
+
+
+def group_kernel(own_ref, other_ref, o_ref):
+    total = own_ref[...] + other_ref[...].reshape(NZ * SLOT, -1).astype(F32)
+    total = total * lax.rsqrt(empty_sums(total[:, :128]) / (DI // GROUPS) + EPS)
+    o_ref[...] = total.astype(BF).reshape(o_ref.shape)
 
 
 def last_kernel(p_ref, x_ref, o_ref):
@@ -349,30 +352,34 @@
     rstd, bcc = call(
         shared_kernel, (shape((STEPS * RB, 128), F32), shape((64, 128), BF)), [VM] * 3
     )(small, jnp.swapaxes(conv_bc_state, 0, 1), conv_bc_w)
-    large, bcc = lax.optimization_barrier((large, bcc))
+    large, bcc, w_out = lax.optimization_barrier((large, bcc, w_out))
+    left, right = (lax.ppermute(w_out, "x", way) for way in (NEXT, PREVIOUS))
     large = exchange(large.reshape(NC * NY, HALF, 512), ("core", "y"))
     ready = call(
         carried_kernel,
-        (
-            shape((STEPS * RB, 256), F32),
-            shape((STEPS * RB, 128), F32),
-            shape((STEPS * RB, NC * NY * HALF), BF),
-            shape((STEPS * RB, NC * NY * HALF), BF),
-        ),
+        shape((STEPS * RB, 384), F32),
         [SM] + [VM] * 6,
         scratch_shapes=[pltpu.VMEM((2, RB * 8, 128), F32)] * 2
         + [pltpu.VMEM((NX * NC, 64, 128), F32)],
     )(
         pos, *around_x(jnp.stack([bcc, swap_core(bcc)])), rstd, ssm_state.reshape(RB, 256, 256)
     )
-    u = call(state_kernel, shape((NC * NY, HALF, 256), BF), [VM] * 7)(
-        *ready, large, params, jnp.swapaxes(conv_x_state, 0, 1)
-    )
-    rows = exchange(u, ("core", "y")).reshape(NC, NY, HALF, 256)
-    sums = call(out_kernel, shape((NX, NZ, SLOT, w_out.shape[1]), BF), [SM] + [VM] * 3)(
-        pos, rows, w_out, swap_core(w_out)
-    )
-    sums = call(group_kernel, shape(sums.shape[1:], BF), [VM])(exchange(sums, "x"))
+    ready, left, right = lax.optimization_barrier((ready, left, right))
+    u = call(state_kernel, shape((NX, NY, NC, SLOT, 256), BF), [VM] * 4)(
+        ready, large, params, jnp.swapaxes(conv_x_state, 0, 1)
+    )
+    u = exchange(u.reshape(NX * NY, NC, SLOT, 256), ("x", "y")).reshape(u.shape)
+    half = w_out.shape[0] // 2
+    low = lax.ppermute(left[:half], "x", NEXT)
+    high = lax.ppermute(right[half:], "x", PREVIOUS)
+    width = w_out.shape[1]
+    out = lambda own, result: call(
+        functools.partial(out_kernel, own), result, [SM] + [VM] * 6
+    )(pos, u, w_out, left, low, high, right)
+    other = swap_core(out(False, shape((NZ, SLOT, width), BF)))
+    sums = call(group_kernel, shape((NZ, SLOT, width), BF), [VM] * 2)(
+        out(True, shape((NZ * SLOT, width), F32)), other
+    )
     return call(last_kernel, shape(inputs.shape, BF), [VM] * 2)(exchange(sums, "z"), tokens)
 
 

time: 148 us -> 140 us (0.946)
  blocking collectives: 55.7 us -> 37 us
  starting transfers between devices: 45.4 us -> 61.1 us
  waiting for transfers between devices: 30.8 us -> 23.3 us
    all_to_all x2 -> x1, blocking collectives: 33.7 us -> 15 us  [exchange(): return lax.all_to_all(v, axes, split_axis=0, concat_axis=0, tiled=True)]
    all_to_all x3, waiting for transfers between devices: 17.3 us -> 0.04 us  [exchange(): return lax.all_to_all(v, axes, split_axis=0, concat_axis=0, tiled=True)]
    ppermute x3 -> x7, starting transfers between devices: 8.96 us -> 21.4 us  [the longest x3 8.96 us: around_x(): return [v] + [lax.ppermute(v, 'x', way) for way in (NEXT, ACROSS, PREVIOUS)]]
    ppermute x3 -> x7, waiting for transfers between devices: 3.23 us -> 14.1 us  [the longest x1 6.52 us: per_device(): high = lax.ppermute(right[half:], 'x', PREVIOUS)]
    all_to_all x3, starting transfers between devices: 19.5 us -> 23 us  [exchange(): return lax.all_to_all(v, axes, split_axis=0, concat_axis=0, tiled=True)]
    pallas_call x4 -> x5, Pallas kernels: 4.78 us -> 5.56 us  [the longest x2 2.15 us: per_device(): call(functools.partial(out_kernel, own), result, [SM] + [VM] * 6)]
  transfers between devices with their start and end apart: 13 -> 17, of which waited for: 10 -> 9; matrix products, arithmetic and copies ran while one was open for 0% -> 0% of each run, Pallas kernels for 4% -> 6%
where the time goes in v4:
time: 140 us; the launch traced here: 138 us
  starting transfers between devices  61.1 us (44%)
  blocking collectives  37 us (26%)
  waiting for transfers between devices  23.3 us (17%)
  Pallas kernels  12.1 us (9%)
  local copies, waits for them, and re-layouts  4.19 us (3%)
    all_to_all x3, starting transfers between devices, exchange(): return lax.all_to_all(v, axes, split_axis=0, concat_axis=0, tiled=True)  23 us
    all_to_all x1, blocking collectives, to_all(): lax.all_to_all(jnp.broadcast_to(v[None], (count,) + v.shape), axes, split...  22 us
    all_to_all x1, blocking collectives, exchange(): return lax.all_to_all(v, axes, split_axis=0, concat_axis=0, tiled=True)  15 us
    ppermute x6, starting transfers between devices, swap_core(): return lax.ppermute(v, 'core', [(0, 1), (1, 0)])  12.4 us
    ppermute x3, starting transfers between devices, around_x(): return [v] + [lax.ppermute(v, 'x', way) for way in (NEXT, ACROSS, PREVIOUS)]  8.96 us
    ppermute x1, waiting for transfers between devices, per_device(): high = lax.ppermute(right[half:], 'x', PREVIOUS)  6.52 us
    ppermute x2, starting transfers between devices, per_device(): left, right = (lax.ppermute(w_out, 'x', way) for way in (NEXT, PREVIOUS))  5.84 us
    all_to_all x1, waiting for transfers between devices, to_all(): lax.all_to_all(jnp.broadcast_to(v[None], (count,) + v.shape), axes, split...  5.56 us
  transfers between devices with their start and end apart: 17, of which 9 were waited for; matrix products, arithmetic and copies ran while one was open for 0% of the time, Pallas kernels for 6%

profile of v4, /device:TPU:56, one launch (start us, length us, event | category | flops | bytes accessed | tf_op | source)
XLA Modules:
  0.0 138.2 jit_solution(6579381327696479401)
XLA Ops:
  1.0 22.0 %all_to_all.30 = bf16[8,16,1024]{2,1,0:T(8,128)(2,1)S(1)} all-to-all(bf16[8,16,1024]{2,1,0:T(8,128)(2,1)S(1)} %broadcast_in_dim.10), channel_id=1, replica_groups=mesh['z'=8,'x'=4,'core'=2,'y'=8] {'z'}, dimensions={0} | all-to-all | bytes 524288 | tf_op jit(solution)/shard_map/all_to_all | solution.py:34
  24.1 4.3 %all-to-all-start.1 = ((bf16[4,8,16,1024]{3,2,1,0:T(8,128)(2,1)}), bf16[4,8,16,1024]{3,2,1,0:T(8,128)(2,1)S(1)}, u32[]{:S(2)}, u32[]{:S(2)}) async-start(bf16[4,8,16,1024]{3,2,1,0:T(8,128)(2,1)} %broadcast_in_dim.22), calls=%async_computation.1 | async-start | bytes 2097152 | tf_op jit(solution)/shard_map/all_to_all | solution.py:34
  28.4 2.1 %collective-permute-start.1 = (bf16[1024,256]{1,0:T(8,128)(2,1)S(1)}, bf16[1024,256]{1,0:T(8,128)(2,1)S(1)}, u32[]{:S(2)}, u32[]{:S(2)}) collective-permute-start(bf16[1024,256]{1,0:T(8,128)(2,1)S(1)} %copy-done.3), channel_id=1, source_target_pairs={{0,8},{8,0},{1,9},{9,1},{2,10},{10,2},{3,11},{11,3},{4,12},{12,4},... | collective-permute-start | bytes 1572872 | tf_op jit(solution)/shard_map/ppermute | solution.py:30
  30.5 2.4 %collective-permute-start = (bf16[1024,256]{1,0:T(8,128)(2,1)S(1)}, bf16[1024,256]{1,0:T(8,128)(2,1)}, u32[]{:S(2)}, u32[]{:S(2)}) collective-permute-start(bf16[1024,256]{1,0:T(8,128)(2,1)S(1)} %copy-done.2), channel_id=1, source_target_pairs={{0,8},{8,0},{1,9},{9,1},{2,10},{10,2},{3,11},{11,3},{4,12},{12,4},... | collective-permute-start | bytes 1572872 | tf_op jit(solution)/shard_map/ppermute | solution.py:30
  32.9 1.9 %collective-permute-start.3 = (bf16[64,1024]{1,0:T(8,128)(2,1)S(1)}, bf16[64,1024]{1,0:T(8,128)(2,1)S(1)}, u32[]{:S(2)}, u32[]{:S(2)}) collective-permute-start(bf16[64,1024]{1,0:T(8,128)(2,1)S(1)} %bitcast.21), channel_id=1, source_target_pairs={{0,8},{8,0},{1,9},{9,1},{2,10},{10,2},{3,11},{11,3},{4,12},{12,4},... | collective-permute-start | bytes 393224 | tf_op jit(solution)/shard_map/ppermute | solution.py:30
  36.1 5.6 %all-to-all-done.1.g_ref = bf16[4,8,16,1024]{3,2,1,0:T(8,128)(2,1)S(1)} async-done(((bf16[4,8,16,1024]{3,2,1,0:T(8,128)(2,1)}), bf16[4,8,16,1024]{3,2,1,0:T(8,128)(2,1)S(1)}, u32[]{:S(2)}, u32[]{:S(2)}) %all-to-all-start.1) | async-done | bytes 1048608 | tf_op jit(solution)/shard_map/all_to_all | solution.py:34
  43.4 6.9 %all-to-all-start.2 = ((bf16[16,32,128]{2,1,0:T(8,128)(2,1)}), bf16[16,32,128]{2,1,0:T(8,128)(2,1)S(1)}, u32[]{:S(2)}, u32[]{:S(2)}) async-start(bf16[16,32,128]{2,1,0:T(8,128)(2,1)} %bitcast.5), calls=%async_computation.2 | async-start | bytes 262144 | tf_op jit(solution)/shard_map/all_to_all | solution.py:47
  50.4 2.2 %collective-permute-start.2 = (bf16[4,1024]{1,0:T(4,128)(2,1)S(1)}, bf16[4,1024]{1,0:T(4,128)(2,1)S(1)}, u32[]{:S(2)}, u32[]{:S(2)}) collective-permute-start(bf16[4,1024]{1,0:T(4,128)(2,1)S(1)} %bitcast.28), channel_id=1, source_target_pairs={{0,8},{8,0},{1,9},{9,1},{2,10},{10,2},{3,11},{11,3},{4,12},{12,4},... | collective-permute-start | bytes 24584 | tf_op jit(solution)/shard_map/ppermute | solution.py:30
  53.6 3.6 %shard_map.154 = bf16[2,8,64,512]{3,2,1,0:T(8,128)(2,1)} custom-call(s32[2]{0:T(128)S(1)} %pad_add_fusion.pos_ref, bf16[4,8,16,1024]{3,2,1,0:T(8,128)(2,1)S(1)} %all-to-all-done.1.g_ref, f32[1,1024]{1,0:T(1,128)S(1)} %bitcast.26, bf16[1024,256]{1,0:T(8,128)(2,1)S(1)} %copy-done.2, bf16[1024,256]{1,0:T(8,128)(2,1)S(1)} %copy-done.3, ...), custom_call_target="tpu_custom_call" | custom-call | tf_op jit(solution)/shard_map/pallas_call | solution.py:342
  57.8 7.2 %all-to-all-start.3 = ((bf16[16,64,512]{2,1,0:T(8,128)(2,1)}), bf16[16,64,512]{2,1,0:T(8,128)(2,1)S(1)}, u32[]{:S(2)}, u32[]{:S(2)}) async-start(bf16[16,64,512]{2,1,0:T(8,128)(2,1)} %bitcast.10), calls=%async_computation.3 | async-start | bytes 2097152 | tf_op jit(solution)/shard_map/all_to_all | solution.py:47
  65.0 3.1 %collective-permute-start.9 = (bf16[256,1024]{1,0:T(8,128)(2,1)S(1)}, bf16[256,1024]{1,0:T(8,128)(2,1)S(1)}, u32[]{:S(2)}, u32[]{:S(2)}) collective-permute-start(bf16[256,1024]{1,0:T(8,128)(2,1)S(1)} %copy-done.1), channel_id=1, source_target_pairs={{0,48},{16,0},{32,16},{48,32},{1,49},{17,1},{33,17},{49,33},{2,50}... | collective-permute-start | bytes 1572872 | tf_op jit(solution)/shard_map/ppermute | solution.py:356
  68.1 2.8 %collective-permute-start.8 = (bf16[256,1024]{1,0:T(8,128)(2,1)S(1)}, bf16[256,1024]{1,0:T(8,128)(2,1)S(1)}, u32[]{:S(2)}, u32[]{:S(2)}) collective-permute-start(bf16[256,1024]{1,0:T(8,128)(2,1)S(1)} %copy-done.1), channel_id=1, source_target_pairs={{0,16},{16,32},{32,48},{48,0},{1,17},{17,33},{33,49},{49,1},{2,18}... | collective-permute-start | bytes 1572872 | tf_op jit(solution)/shard_map/ppermute | solution.py:356
  70.8 1.9 %collective-permute-start.4 = (bf16[64,128]{1,0:T(8,128)(2,1)S(1)}, bf16[64,128]{1,0:T(8,128)(2,1)S(1)}, u32[]{:S(2)}, u32[]{:S(2)}) collective-permute-start(bf16[64,128]{1,0:T(8,128)(2,1)S(1)} %get-tuple-element.21), channel_id=1, source_target_pairs={{0,8},{8,0},{1,9},{9,1},{2,10},{10,2},{3,11},{11,3},{4,12},{12,4},... | collective-permute-start | bytes 49160 | tf_op jit(solution)/shard_map/ppermute | solution.py:30
  73.9 4.3 %collective-permute-start.7 = (bf16[2,64,128]{2,1,0:T(8,128)(2,1)S(1)}, bf16[2,64,128]{2,1,0:T(8,128)(2,1)S(1)}, u32[]{:S(2)}, u32[]{:S(2)}) collective-permute-start(bf16[2,64,128]{2,1,0:T(8,128)(2,1)S(1)} %pad_maximum_fusion.bc_0), channel_id=1, source_target_pairs={{0,48},{16,0},{32,16},{48,32},{1,49},{17,1},{33,17},{49,33},{2,50}... | collective-permute-start | bytes 98312 | tf_op jit(solution)/shard_map/ppermute | solution.py:43
  78.2 2.2 %collective-permute-start.6 = (bf16[2,64,128]{2,1,0:T(8,128)(2,1)S(1)}, bf16[2,64,128]{2,1,0:T(8,128)(2,1)S(1)}, u32[]{:S(2)}, u32[]{:S(2)}) collective-permute-start(bf16[2,64,128]{2,1,0:T(8,128)(2,1)S(1)} %pad_maximum_fusion.bc_0), channel_id=1, source_target_pairs={{0,32},{16,48},{32,0},{48,16},{1,33},{17,49},{33,1},{49,17},{2,34}... | collective-permute-start | bytes 98312 | tf_op jit(solution)/shard_map/ppermute | solution.py:43
  80.4 2.5 %collective-permute-start.5 = (bf16[2,64,128]{2,1,0:T(8,128)(2,1)S(1)}, bf16[2,64,128]{2,1,0:T(8,128)(2,1)S(1)}, u32[]{:S(2)}, u32[]{:S(2)}) collective-permute-start(bf16[2,64,128]{2,1,0:T(8,128)(2,1)S(1)} %pad_maximum_fusion.bc_0), channel_id=1, source_target_pairs={{0,16},{16,32},{32,48},{48,0},{1,17},{17,33},{33,49},{49,1},{2,18}... | collective-permute-start | bytes 98312 | tf_op jit(solution)/shard_map/ppermute | solution.py:43
  83.0 2.6 %collective-permute-done.6.bc_2 = bf16[2,64,128]{2,1,0:T(8,128)(2,1)S(1)} collective-permute-done((bf16[2,64,128]{2,1,0:T(8,128)(2,1)S(1)}, bf16[2,64,128]{2,1,0:T(8,128)(2,1)S(1)}, u32[]{:S(2)}, u32[]{:S(2)}) %collective-permute-start.6) | collective-permute-done | bytes 32800 | tf_op jit(solution)/shard_map/ppermute | solution.py:43
  92.6 8.9 %all-to-all-start.4 = ((bf16[32,2,16,256]{3,2,1,0:T(8,128)(2,1)}), bf16[32,2,16,256]{3,2,1,0:T(8,128)(2,1)S(1)}, u32[]{:S(2)}, u32[]{:S(2)}) async-start(bf16[32,2,16,256]{3,2,1,0:T(8,128)(2,1)} %bitcast.16), calls=%async_computation.4 | async-start | bytes 1048576 | tf_op jit(solution)/shard_map/all_to_all | solution.py:47
  101.5 4.7 %collective-permute-start.11 = (bf16[128,1024]{1,0:T(8,128)(2,1)S(1)}, bf16[128,1024]{1,0:T(8,128)(2,1)S(1)}, u32[]{:S(2)}, u32[]{:S(2)}) collective-permute-start(bf16[128,1024]{1,0:T(8,128)(2,1)S(1)} %slice.7), channel_id=1, source_target_pairs={{0,48},{16,0},{32,16},{48,32},{1,49},{17,1},{33,17},{49,33},{2,50}... | collective-permute-start | bytes 786440 | tf_op jit(solution)/shard_map/ppermute | solution.py:374
  106.2 1.9 %collective-permute-start.10 = (bf16[128,1024]{1,0:T(8,128)(2,1)S(1)}, bf16[128,1024]{1,0:T(8,128)(2,1)S(1)}, u32[]{:S(2)}, u32[]{:S(2)}) collective-permute-start(bf16[128,1024]{1,0:T(8,128)(2,1)S(1)} %slice.6), channel_id=1, source_target_pairs={{0,16},{16,32},{32,48},{48,0},{1,17},{17,33},{33,49},{49,1},{2,18}... | collective-permute-start | bytes 786440 | tf_op jit(solution)/shard_map/ppermute | solution.py:373
  108.2 6.5 %collective-permute-done.11.high_ref = bf16[128,1024]{1,0:T(8,128)(2,1)S(1)} collective-permute-done((bf16[128,1024]{1,0:T(8,128)(2,1)S(1)}, bf16[128,1024]{1,0:T(8,128)(2,1)S(1)}, u32[]{:S(2)}, u32[]{:S(2)}) %collective-permute-start.11) | collective-permute-done | bytes 262176 | tf_op jit(solution)/shard_map/ppermute | solution.py:374
  114.7 3.1 %collective-permute-done.10.low_ref = bf16[128,1024]{1,0:T(8,128)(2,1)S(1)} collective-permute-done((bf16[128,1024]{1,0:T(8,128)(2,1)S(1)}, bf16[128,1024]{1,0:T(8,128)(2,1)S(1)}, u32[]{:S(2)}, u32[]{:S(2)}) %collective-permute-start.10) | collective-permute-done | bytes 262176 | tf_op jit(solution)/shard_map/ppermute | solution.py:373
  118.9 1.9 %collective-permute-start.12 = (bf16[8,16,1024]{2,1,0:T(8,128)(2,1)S(1)}, bf16[8,16,1024]{2,1,0:T(8,128)(2,1)S(1)}, u32[]{:S(2)}, u32[]{:S(2)}) collective-permute-start(bf16[8,16,1024]{2,1,0:T(8,128)(2,1)S(1)} %shard_map.160), channel_id=1, source_target_pairs={{0,8},{8,0},{1,9},{9,1},{2,10},{10,2},{3,11},{11,3},{4,12},{12,4},... | collective-permute-start | bytes 786440 | tf_op jit(solution)/shard_map/ppermute | solution.py:30
  122.5 15.0 %all_to_all.31.p_ref = bf16[8,16,1024]{2,1,0:T(8,128)(2,1)S(1)} all-to-all(bf16[8,16,1024]{2,1,0:T(8,128)(2,1)S(1)} %shard_map.161), channel_id=1, replica_groups=mesh['z'=8,'x'=4,'core'=2,'y'=8] {'z'}, dimensions={0} | all-to-all | bytes 524288 | tf_op jit(solution)/shard_map/all_to_all | solution.py:47
  (63 shorter events, 18.3 us)
Async XLA Ops:
  0.0 30.4 %copy-start.2 = (bf16[1024,256]{1,0:T(8,128)(2,1)S(1)}, bf16[1024,256]{1,0:T(8,128)(2,1)}, u32[]{:S(2)}) copy-start(bf16[1024,256]{1,0:T(8,128)(2,1)} %refs_0_.1) | copy-start | bytes 1572868
  0.0 32.9 %copy-start.4 = (bf16[1024,64]{0,1:T(8,128)(2,1)S(1)}, bf16[1024,64]{0,1:T(8,128)(2,1)}, u32[]{:S(2)}) copy-start(bf16[1024,64]{0,1:T(8,128)(2,1)} %param.20) | copy-start | bytes 393220
  0.0 41.7 %copy-start.7 = (f32[1024]{0:T(1024)S(1)}, f32[1024]{0:T(1024)}, u32[]{:S(2)}) copy-start(f32[1024]{0:T(1024)} %param.17) | copy-start | bytes 12292
  0.0 50.3 %copy-start.8 = (bf16[1024,4]{0,1:T(4,128)(2,1)S(1)}, bf16[1024,4]{0,1:T(4,128)(2,1)}, u32[]{:S(2)}) copy-start(bf16[1024,4]{0,1:T(4,128)(2,1)} %param.21) | copy-start | bytes 24580
  24.1 17.6 %all-to-all-start.1 = ((bf16[4,8,16,1024]{3,2,1,0:T(8,128)(2,1)}), bf16[4,8,16,1024]{3,2,1,0:T(8,128)(2,1)S(1)}, u32[]{:S(2)}, u32[]{:S(2)}) async-start(bf16[4,8,16,1024]{3,2,1,0:T(8,128)(2,1)} %broadcast_in_dim.22), calls=%async_computation.1 | async-start | bytes 2097152 | tf_op jit(solution)/shard_map/all_to_all | solution.py:34
  28.4 25.2 %collective-permute-start.1 = (bf16[1024,256]{1,0:T(8,128)(2,1)S(1)}, bf16[1024,256]{1,0:T(8,128)(2,1)S(1)}, u32[]{:S(2)}, u32[]{:S(2)}) collective-permute-start(bf16[1024,256]{1,0:T(8,128)(2,1)S(1)} %copy-done.3), channel_id=1, source_target_pairs={{0,8},{8,0},{1,9},{9,1},{2,10},{10,2},{3,11},{11,3},{4,12},{12,4},... | collective-permute-start | bytes 1572872 | tf_op jit(solution)/shard_map/ppermute | solution.py:30
  30.5 23.2 %collective-permute-start = (bf16[1024,256]{1,0:T(8,128)(2,1)S(1)}, bf16[1024,256]{1,0:T(8,128)(2,1)}, u32[]{:S(2)}, u32[]{:S(2)}) collective-permute-start(bf16[1024,256]{1,0:T(8,128)(2,1)S(1)} %copy-done.2), channel_id=1, source_target_pairs={{0,8},{8,0},{1,9},{9,1},{2,10},{10,2},{3,11},{11,3},{4,12},{12,4},... | collective-permute-start | bytes 1572872 | tf_op jit(solution)/shard_map/ppermute | solution.py:30
  32.9 3.2 %collective-permute-start.3 = (bf16[64,1024]{1,0:T(8,128)(2,1)S(1)}, bf16[64,1024]{1,0:T(8,128)(2,1)S(1)}, u32[]{:S(2)}, u32[]{:S(2)}) collective-permute-start(bf16[64,1024]{1,0:T(8,128)(2,1)S(1)} %bitcast.21), channel_id=1, source_target_pairs={{0,8},{8,0},{1,9},{9,1},{2,10},{10,2},{3,11},{11,3},{4,12},{12,4},... | collective-permute-start | bytes 393224 | tf_op jit(solution)/shard_map/ppermute | solution.py:30
  43.4 13.8 %all-to-all-start.2 = ((bf16[16,32,128]{2,1,0:T(8,128)(2,1)}), bf16[16,32,128]{2,1,0:T(8,128)(2,1)S(1)}, u32[]{:S(2)}, u32[]{:S(2)}) async-start(bf16[16,32,128]{2,1,0:T(8,128)(2,1)} %bitcast.5), calls=%async_computation.2 | async-start | bytes 262144 | tf_op jit(solution)/shard_map/all_to_all | solution.py:47
  50.4 32.5 %copy-start.10 = (f32[4,256]{1,0:T(4,128)S(1)}, f32[4,256]{1,0:T(4,128)}, u32[]{:S(2)}) copy-start(f32[4,256]{1,0:T(4,128)} %param.22) | copy-start | bytes 12292
  50.4 32.5 %copy-start.11 = (f32[256]{0:T(256)S(1)}, f32[256]{0:T(256)}, u32[]{:S(2)}) copy-start(f32[256]{0:T(256)} %param.30) | copy-start | bytes 3076
  50.4 3.2 %collective-permute-start.2 = (bf16[4,1024]{1,0:T(4,128)(2,1)S(1)}, bf16[4,1024]{1,0:T(4,128)(2,1)S(1)}, u32[]{:S(2)}, u32[]{:S(2)}) collective-permute-start(bf16[4,1024]{1,0:T(4,128)(2,1)S(1)} %bitcast.28), channel_id=1, source_target_pairs={{0,8},{8,0},{1,9},{9,1},{2,10},{10,2},{3,11},{11,3},{4,12},{12,4},... | collective-permute-start | bytes 24584 | tf_op jit(solution)/shard_map/ppermute | solution.py:30
  57.2 33.7 %copy-start.5 = (bf16[24,3,256]{2,0,1:T(8,128)(2,1)S(1)}, bf16[24,3,256]{2,0,1:T(8,128)(2,1)}, u32[]{:S(2)}) copy-start(bf16[24,3,256]{2,0,1:T(8,128)(2,1)} %param.24) | copy-start | bytes 110596
  57.8 33.1 %all-to-all-start.3 = ((bf16[16,64,512]{2,1,0:T(8,128)(2,1)}), bf16[16,64,512]{2,1,0:T(8,128)(2,1)S(1)}, u32[]{:S(2)}, u32[]{:S(2)}) async-start(bf16[16,64,512]{2,1,0:T(8,128)(2,1)} %bitcast.10), calls=%async_computation.3 | async-start | bytes 2097152 | tf_op jit(solution)/shard_map/all_to_all | solution.py:47
  65.0 25.9 %collective-permute-start.9 = (bf16[256,1024]{1,0:T(8,128)(2,1)S(1)}, bf16[256,1024]{1,0:T(8,128)(2,1)S(1)}, u32[]{:S(2)}, u32[]{:S(2)}) collective-permute-start(bf16[256,1024]{1,0:T(8,128)(2,1)S(1)} %copy-done.1), channel_id=1, source_target_pairs={{0,48},{16,0},{32,16},{48,32},{1,49},{17,1},{33,17},{49,33},{2,50}... | collective-permute-start | bytes 1572872 | tf_op jit(solution)/shard_map/ppermute | solution.py:356
  68.1 22.8 %collective-permute-start.8 = (bf16[256,1024]{1,0:T(8,128)(2,1)S(1)}, bf16[256,1024]{1,0:T(8,128)(2,1)S(1)}, u32[]{:S(2)}, u32[]{:S(2)}) collective-permute-start(bf16[256,1024]{1,0:T(8,128)(2,1)S(1)} %copy-done.1), channel_id=1, source_target_pairs={{0,16},{16,32},{32,48},{48,0},{1,17},{17,33},{33,49},{49,1},{2,18}... | collective-permute-start | bytes 1572872 | tf_op jit(solution)/shard_map/ppermute | solution.py:356
  70.8 3.1 %collective-permute-start.4 = (bf16[64,128]{1,0:T(8,128)(2,1)S(1)}, bf16[64,128]{1,0:T(8,128)(2,1)S(1)}, u32[]{:S(2)}, u32[]{:S(2)}) collective-permute-start(bf16[64,128]{1,0:T(8,128)(2,1)S(1)} %get-tuple-element.21), channel_id=1, source_target_pairs={{0,8},{8,0},{1,9},{9,1},{2,10},{10,2},{3,11},{11,3},{4,12},{12,4},... | collective-permute-start | bytes 49160 | tf_op jit(solution)/shard_map/ppermute | solution.py:30
  73.9 9.0 %collective-permute-start.7 = (bf16[2,64,128]{2,1,0:T(8,128)(2,1)S(1)}, bf16[2,64,128]{2,1,0:T(8,128)(2,1)S(1)}, u32[]{:S(2)}, u32[]{:S(2)}) collective-permute-start(bf16[2,64,128]{2,1,0:T(8,128)(2,1)S(1)} %pad_maximum_fusion.bc_0), channel_id=1, source_target_pairs={{0,48},{16,0},{32,16},{48,32},{1,49},{17,1},{33,17},{49,33},{2,50}... | collective-permute-start | bytes 98312 | tf_op jit(solution)/shard_map/ppermute | solution.py:43
  78.2 7.4 %collective-permute-start.6 = (bf16[2,64,128]{2,1,0:T(8,128)(2,1)S(1)}, bf16[2,64,128]{2,1,0:T(8,128)(2,1)S(1)}, u32[]{:S(2)}, u32[]{:S(2)}) collective-permute-start(bf16[2,64,128]{2,1,0:T(8,128)(2,1)S(1)} %pad_maximum_fusion.bc_0), channel_id=1, source_target_pairs={{0,32},{16,48},{32,0},{48,16},{1,33},{17,49},{33,1},{49,17},{2,34}... | collective-permute-start | bytes 98312 | tf_op jit(solution)/shard_map/ppermute | solution.py:43
  80.4 7.0 %collective-permute-start.5 = (bf16[2,64,128]{2,1,0:T(8,128)(2,1)S(1)}, bf16[2,64,128]{2,1,0:T(8,128)(2,1)S(1)}, u32[]{:S(2)}, u32[]{:S(2)}) collective-permute-start(bf16[2,64,128]{2,1,0:T(8,128)(2,1)S(1)} %pad_maximum_fusion.bc_0), channel_id=1, source_target_pairs={{0,16},{16,32},{32,48},{48,0},{1,17},{17,33},{33,49},{49,1},{2,18}... | collective-permute-start | bytes 98312 | tf_op jit(solution)/shard_map/ppermute | solution.py:43
  92.6 25.2 %all-to-all-start.4 = ((bf16[32,2,16,256]{3,2,1,0:T(8,128)(2,1)}), bf16[32,2,16,256]{3,2,1,0:T(8,128)(2,1)S(1)}, u32[]{:S(2)}, u32[]{:S(2)}) async-start(bf16[32,2,16,256]{3,2,1,0:T(8,128)(2,1)} %bitcast.16), calls=%async_computation.4 | async-start | bytes 1048576 | tf_op jit(solution)/shard_map/all_to_all | solution.py:47
  101.5 13.1 %collective-permute-start.11 = (bf16[128,1024]{1,0:T(8,128)(2,1)S(1)}, bf16[128,1024]{1,0:T(8,128)(2,1)S(1)}, u32[]{:S(2)}, u32[]{:S(2)}) collective-permute-start(bf16[128,1024]{1,0:T(8,128)(2,1)S(1)} %slice.7), channel_id=1, source_target_pairs={{0,48},{16,0},{32,16},{48,32},{1,49},{17,1},{33,17},{49,33},{2,50}... | collective-permute-start | bytes 786440 | tf_op jit(solution)/shard_map/ppermute | solution.py:374
  106.2 11.6 %collective-permute-start.10 = (bf16[128,1024]{1,0:T(8,128)(2,1)S(1)}, bf16[128,1024]{1,0:T(8,128)(2,1)S(1)}, u32[]{:S(2)}, u32[]{:S(2)}) collective-permute-start(bf16[128,1024]{1,0:T(8,128)(2,1)S(1)} %slice.6), channel_id=1, source_target_pairs={{0,16},{16,32},{32,48},{48,0},{1,17},{17,33},{33,49},{49,1},{2,18}... | collective-permute-start | bytes 786440 | tf_op jit(solution)/shard_map/ppermute | solution.py:373
  118.9 3.4 %collective-permute-start.12 = (bf16[8,16,1024]{2,1,0:T(8,128)(2,1)S(1)}, bf16[8,16,1024]{2,1,0:T(8,128)(2,1)S(1)}, u32[]{:S(2)}, u32[]{:S(2)}) collective-permute-start(bf16[8,16,1024]{2,1,0:T(8,128)(2,1)S(1)} %shard_map.160), channel_id=1, source_target_pairs={{0,8},{8,0},{1,9},{9,1},{2,10},{10,2},{3,11},{11,3},{4,12},{12,4},... | collective-permute-start | bytes 786440 | tf_op jit(solution)/shard_map/ppermute | solution.py:30
  (8 other events, 169.9 us)

commit v5 on v4

--- a/solution.py
+++ b/solution.py
@@ -1,6 +1,8 @@
 import functools
 
 import jax
+import ml_dtypes
+import numpy as np
 import jax.numpy as jnp
 from jax import lax
 from jax.experimental import pallas as pl
@@ -75,7 +77,7 @@
 def small_kernel(pos_ref, g_ref, gain_ref, w_ref, w_other_ref, out_ref):
     raw = g_ref[...].reshape(NX * NZ * SLOT, -1).astype(F32)
     lhs = (raw * gain_ref[...]).astype(BF)
-    out = over(lhs, jnp.concatenate([w_ref[...], w_other_ref[...]], axis=0), 1)
+    out = over(lhs, jnp.concatenate([w_ref[:64], w_other_ref[:64]], axis=0), 1)
     ss = jnp.sum(raw * raw, axis=1, keepdims=True)
     hi = ss.astype(BF).astype(F32)
     lane = lax.broadcasted_iota(jnp.int32, out.shape, 1) % 64
@@ -98,7 +100,7 @@
     heads = [
         jnp.broadcast_to(ref[h : h + 1, :].astype(F32), (SLOT, D // NY))
         for ref in weights[4:]
-        for h in range(4)
+        for h in range(64, 68)
     ]
     sizes = over(lhs, jnp.concatenate(heads, axis=0).astype(BF), 1)
     lane = lax.broadcasted_iota(jnp.int32, sizes.shape, 1)
@@ -230,22 +232,23 @@
         out_ref[t * RB : t * RB + RB, 256:] = out
 
 
-def state_kernel(ready_ref, p_ref, params_ref, hist_ref, u_ref):
-    m = lax.broadcasted_iota(jnp.int32, (1, NC * NY * HALF), 1)
+def orders():
+    m = np.arange(NC * NY * HALF)[None]
+    i = np.arange(STEPS * RB)[:, None]
     x, j = m % HALF // SLOT, m % SLOT
     q = x * NC + m // (NY * HALF)
-    step = (j * 11) // 32
-    row = jnp.where(j < SLOT - 1, step * RB + q * OWN + j - step * OWN, -1)
-    i = lax.broadcasted_iota(jnp.int32, (STEPS * RB, 1), 0)
-    gather = jnp.where(row == i, 1.0, 0.0).astype(BF)
-    q = jnp.where(j == SLOT - 1, q, -1)
-    empty = jnp.where(q == i % RB // OWN, 1.0, 0.0).astype(BF)
+    row = np.where(j < SLOT - 1, j // OWN * RB + q * OWN + j % OWN, -1)
+    empty = (q == i % RB // OWN) & (j == SLOT - 1)
+    return jnp.asarray(np.concatenate([row == i, empty]).astype(ml_dtypes.bfloat16))
+
+
+def state_kernel(ready_ref, p_ref, params_ref, hist_ref, orders_ref, u_ref):
     taps, gain = params_ref[0:4], params_ref[4:5]
     a_log, bias, skip = params_ref[5:6], params_ref[6:7], params_ref[7:8]
     y0, pairs = ready_ref[:, :256], ready_ref[:, 256:]
     rstd = pairs[:, 127:]
     large = p_ref[...].reshape(NC * NY * HALF, 512)
-    sizes = jnp.dot(empty, large[:, :128], preferred_element_type=F32) * rstd
+    sizes = jnp.dot(orders_ref[STEPS * RB :], large[:, :128], preferred_element_type=F32) * rstd
     row = lax.broadcasted_iota(jnp.int32, sizes.shape, 0)
     lane = lax.broadcasted_iota(jnp.int32, sizes.shape, 1)
     slot = row // RB * OWN + row % RB % OWN
@@ -257,7 +260,7 @@
     dt = jnp.maximum(pre, 0.0) + jnp.log1p(jnp.exp(-jnp.abs(pre)))
     decay = jnp.exp(-dt * jnp.exp(a_log))
     order, collect = slot_from_step()
-    raw = jnp.dot(gather, large, preferred_element_type=F32) * rstd
+    raw = jnp.dot(orders_ref[: STEPS * RB], large, preferred_element_type=F32) * rstd
     raw = raw.astype(BF).astype(F32)
     gate = raw[:, 256:]
     gate = gate * jax.nn.sigmoid(gate)
@@ -334,11 +337,13 @@
     pos = jnp.stack([lax.axis_index("core"), lax.axis_index("x")]).astype(jnp.int32)
     tokens = jnp.pad(inputs.reshape(STEPS * OWN, -1), ((0, 1), (0, 0)))
     gathered = to_all(to_all(tokens, "z", NZ), "x", NX)
-    gain, w_bc, w_dt = pre_gain[None], w_bc.T, w_dt.T
+    gain = pre_gain[None]
+    w_small = jnp.concatenate([w_bc.T, w_dt.T, jnp.zeros((12, w_bc.shape[0]), BF)], axis=0)
+    w_small_other = swap_core(w_small)
     small = call(small_kernel, shape((NC, NY, HALF // 2, 128), BF), [SM] + [VM] * 4)(
-        pos, gathered, gain, w_bc, swap_core(w_bc)
-    )
-    weights = (w_x, w_z, swap_core(w_x), swap_core(w_z), w_dt, swap_core(w_dt))
+        pos, gathered, gain, w_small, w_small_other
+    )
+    weights = (w_x, w_z, swap_core(w_x), swap_core(w_z), w_small, w_small_other)
     large = call(large_kernel, shape((NC, NY, HALF, 512), BF), [SM] + [VM] * 8)(
         pos, gathered, gain, *weights
     )
@@ -365,8 +370,8 @@
         pos, *around_x(jnp.stack([bcc, swap_core(bcc)])), rstd, ssm_state.reshape(RB, 256, 256)
     )
     ready, left, right = lax.optimization_barrier((ready, left, right))
-    u = call(state_kernel, shape((NX, NY, NC, SLOT, 256), BF), [VM] * 4)(
-        ready, large, params, jnp.swapaxes(conv_x_state, 0, 1)
+    u = call(state_kernel, shape((NX, NY, NC, SLOT, 256), BF), [VM] * 5)(
+        ready, large, params, jnp.swapaxes(conv_x_state, 0, 1), orders()
     )
     u = exchange(u.reshape(NX * NY, NC, SLOT, 256), ("x", "y")).reshape(u.shape)
     half = w_out.shape[0] // 2

time: 140 us -> 138 us (0.986)
  the two profiles are of different devices: /device:TPU:56 before, /device:TPU:8 now
where the time goes in v5:
time: 138 us; the launch traced here: 137 us
  starting transfers between devices  56.6 us (41%)
  blocking collectives  37 us (27%)
  waiting for transfers between devices  26.3 us (19%)
  Pallas kernels  12.3 us (9%)
  local copies, waits for them, and re-layouts  4.27 us (3%)
    all_to_all x1, blocking collectives, to_all(): lax.all_to_all(jnp.broadcast_to(v[None], (count,) + v.shape), axes, split...  22 us
    all_to_all x3, starting transfers between devices, exchange(): return lax.all_to_all(v, axes, split_axis=0, concat_axis=0, tiled=True)  19.1 us
    all_to_all x1, blocking collectives, exchange(): return lax.all_to_all(v, axes, split_axis=0, concat_axis=0, tiled=True)  15 us
    ppermute x5, starting transfers between devices, swap_core(): return lax.ppermute(v, 'core', [(0, 1), (1, 0)])  10.1 us
    ppermute x3, starting transfers between devices, around_x(): return [v] + [lax.ppermute(v, 'x', way) for way in (NEXT, ACROSS, PREVIOUS)]  8.96 us
    all_to_all x3, waiting for transfers between devices, exchange(): return lax.all_to_all(v, axes, split_axis=0, concat_axis=0, tiled=True)  7.77 us
    ppermute x2, starting transfers between devices, per_device(): left, right = (lax.ppermute(w_out, 'x', way) for way in (NEXT, PREVIOUS))  7.05 us
    ppermute x1, waiting for transfers between devices, per_device(): low = lax.ppermute(left[:half], 'x', NEXT)  6.93 us
  transfers between devices with their start and end apart: 16, of which 11 were waited for; matrix products, arithmetic and copies ran while one was open for 0% of the time, Pallas kernels for 6%

profile of v5, /device:TPU:8, one launch (start us, length us, event | category | flops | bytes accessed | tf_op | source)
XLA Modules:
  0.0 137.0 jit_solution(5293217563443416280)
XLA Ops:
  1.0 22.0 %all_to_all.30 = bf16[8,16,1024]{2,1,0:T(8,128)(2,1)S(1)} all-to-all(bf16[8,16,1024]{2,1,0:T(8,128)(2,1)S(1)} %broadcast_in_dim.24), channel_id=1, replica_groups=mesh['z'=8,'x'=4,'core'=2,'y'=8] {'z'}, dimensions={0} | all-to-all | bytes 524288 | tf_op jit(solution)/shard_map/all_to_all | solution.py:36
  24.1 4.3 %all-to-all-start.1 = ((bf16[4,8,16,1024]{3,2,1,0:T(8,128)(2,1)}), bf16[4,8,16,1024]{3,2,1,0:T(8,128)(2,1)S(1)}, u32[]{:S(2)}, u32[]{:S(2)}) async-start(bf16[4,8,16,1024]{3,2,1,0:T(8,128)(2,1)} %broadcast_in_dim.25), calls=%async_computation.1 | async-start | bytes 2097152 | tf_op jit(solution)/shard_map/all_to_all | solution.py:36
  28.4 1.9 %collective-permute-start = (bf16[1024,256]{1,0:T(8,128)(2,1)S(1)}, bf16[1024,256]{1,0:T(8,128)(2,1)}, u32[]{:S(2)}, u32[]{:S(2)}) collective-permute-start(bf16[1024,256]{1,0:T(8,128)(2,1)S(1)} %copy-done.2), channel_id=1, source_target_pairs={{0,8},{8,0},{1,9},{9,1},{2,10},{10,2},{3,11},{11,3},{4,12},{12,4},... | collective-permute-start | bytes 1572872 | tf_op jit(solution)/shard_map/ppermute | solution.py:32
  30.3 2.4 %collective-permute-start.1 = (bf16[1024,256]{1,0:T(8,128)(2,1)S(1)}, bf16[1024,256]{1,0:T(8,128)(2,1)}, u32[]{:S(2)}, u32[]{:S(2)}) collective-permute-start(bf16[1024,256]{1,0:T(8,128)(2,1)S(1)} %copy-done.3), channel_id=1, source_target_pairs={{0,8},{8,0},{1,9},{9,1},{2,10},{10,2},{3,11},{11,3},{4,12},{12,4},... | collective-permute-start | bytes 1572872 | tf_op jit(solution)/shard_map/ppermute | solution.py:32
  32.9 1.9 %collective-permute-start.2 = (bf16[80,1024]{1,0:T(8,128)(2,1)S(1)}, bf16[80,1024]{1,0:T(8,128)(2,1)S(1)}, u32[]{:S(2)}, u32[]{:S(2)}) collective-permute-start(bf16[80,1024]{1,0:T(8,128)(2,1)S(1)} %maximum_maximum_fusion.refs_4_.w_ref), channel_id=1, source_target_pairs={{0,8},{8,0},{1,9},{9,1},{2,10},{10,2},{3,11},{11,3},{4,12},{12,4},... | collective-permute-start | bytes 491528 | tf_op jit(solution)/shard_map/ppermute | solution.py:32
  36.2 5.5 %all-to-all-done.1.g_ref = bf16[4,8,16,1024]{3,2,1,0:T(8,128)(2,1)S(1)} async-done(((bf16[4,8,16,1024]{3,2,1,0:T(8,128)(2,1)}), bf16[4,8,16,1024]{3,2,1,0:T(8,128)(2,1)S(1)}, u32[]{:S(2)}, u32[]{:S(2)}) %all-to-all-start.1) | async-done | bytes 1048608 | tf_op jit(solution)/shard_map/all_to_all | solution.py:36
  43.5 7.6 %all-to-all-start.2 = ((bf16[16,32,128]{2,1,0:T(8,128)(2,1)}), bf16[16,32,128]{2,1,0:T(8,128)(2,1)S(1)}, u32[]{:S(2)}, u32[]{:S(2)}) async-start(bf16[16,32,128]{2,1,0:T(8,128)(2,1)} %bitcast.5), calls=%async_computation.2 | async-start | bytes 262144 | tf_op jit(solution)/shard_map/all_to_all | solution.py:49
  51.1 3.8 %shard_map.163 = bf16[2,8,64,512]{3,2,1,0:T(8,128)(2,1)} custom-call(s32[2]{0:T(128)S(1)} %pad_add_fusion.pos_ref, bf16[4,8,16,1024]{3,2,1,0:T(8,128)(2,1)S(1)} %all-to-all-done.1.g_ref, f32[1,1024]{1,0:T(1,128)S(1)} %bitcast.25, bf16[1024,256]{1,0:T(8,128)(2,1)S(1)} %copy-done.2, bf16[1024,256]{1,0:T(8,128)(2,1)S(1)} %copy-done.3, ...), custom_call_target="tpu_custom_call" | custom-call | tf_op jit(solution)/shard_map/pallas_call | solution.py:347
  54.9 4.3 %all-to-all-done.2.p_ref = bf16[16,32,128]{2,1,0:T(8,128)(2,1)S(1)} async-done(((bf16[16,32,128]{2,1,0:T(8,128)(2,1)}), bf16[16,32,128]{2,1,0:T(8,128)(2,1)S(1)}, u32[]{:S(2)}, u32[]{:S(2)}) %all-to-all-start.2) | async-done | bytes 131104 | tf_op jit(solution)/shard_map/all_to_all | solution.py:49
  59.8 3.8 %all-to-all-start.3 = ((bf16[16,64,512]{2,1,0:T(8,128)(2,1)}), bf16[16,64,512]{2,1,0:T(8,128)(2,1)S(1)}, u32[]{:S(2)}, u32[]{:S(2)}) async-start(bf16[16,64,512]{2,1,0:T(8,128)(2,1)} %bitcast.10), calls=%async_computation.3 | async-start | bytes 2097152 | tf_op jit(solution)/shard_map/all_to_all | solution.py:49
  63.6 2.5 %collective-permute-start.7 = (bf16[256,1024]{1,0:T(8,128)(2,1)S(1)}, bf16[256,1024]{1,0:T(8,128)(2,1)S(1)}, u32[]{:S(2)}, u32[]{:S(2)}) collective-permute-start(bf16[256,1024]{1,0:T(8,128)(2,1)S(1)} %copy-done.1), channel_id=1, source_target_pairs={{0,16},{16,32},{32,48},{48,0},{1,17},{17,33},{33,49},{49,1},{2,18}... | collective-permute-start | bytes 1572872 | tf_op jit(solution)/shard_map/ppermute | solution.py:361
  66.1 4.6 %collective-permute-start.8 = (bf16[256,1024]{1,0:T(8,128)(2,1)S(1)}, bf16[256,1024]{1,0:T(8,128)(2,1)S(1)}, u32[]{:S(2)}, u32[]{:S(2)}) collective-permute-start(bf16[256,1024]{1,0:T(8,128)(2,1)S(1)} %copy-done.1), channel_id=1, source_target_pairs={{0,48},{16,0},{32,16},{48,32},{1,49},{17,1},{33,17},{49,33},{2,50}... | collective-permute-start | bytes 1572872 | tf_op jit(solution)/shard_map/ppermute | solution.py:361
  70.7 1.9 %collective-permute-start.3 = (bf16[64,128]{1,0:T(8,128)(2,1)S(1)}, bf16[64,128]{1,0:T(8,128)(2,1)S(1)}, u32[]{:S(2)}, u32[]{:S(2)}) collective-permute-start(bf16[64,128]{1,0:T(8,128)(2,1)S(1)} %get-tuple-element.21), channel_id=1, source_target_pairs={{0,8},{8,0},{1,9},{9,1},{2,10},{10,2},{3,11},{11,3},{4,12},{12,4},... | collective-permute-start | bytes 49160 | tf_op jit(solution)/shard_map/ppermute | solution.py:32
  73.8 1.9 %collective-permute-start.4 = (bf16[2,64,128]{2,1,0:T(8,128)(2,1)S(1)}, bf16[2,64,128]{2,1,0:T(8,128)(2,1)S(1)}, u32[]{:S(2)}, u32[]{:S(2)}) collective-permute-start(bf16[2,64,128]{2,1,0:T(8,128)(2,1)S(1)} %pad_maximum_fusion.bc_0), channel_id=1, source_target_pairs={{0,16},{16,32},{32,48},{48,0},{1,17},{17,33},{33,49},{49,1},{2,18}... | collective-permute-start | bytes 98312 | tf_op jit(solution)/shard_map/ppermute | solution.py:45
  75.7 3.4 %collective-permute-start.5 = (bf16[2,64,128]{2,1,0:T(8,128)(2,1)S(1)}, bf16[2,64,128]{2,1,0:T(8,128)(2,1)S(1)}, u32[]{:S(2)}, u32[]{:S(2)}) collective-permute-start(bf16[2,64,128]{2,1,0:T(8,128)(2,1)S(1)} %pad_maximum_fusion.bc_0), channel_id=1, source_target_pairs={{0,32},{16,48},{32,0},{48,16},{1,33},{17,49},{33,1},{49,17},{2,34}... | collective-permute-start | bytes 98312 | tf_op jit(solution)/shard_map/ppermute | solution.py:45
  79.1 3.7 %collective-permute-start.6 = (bf16[2,64,128]{2,1,0:T(8,128)(2,1)S(1)}, bf16[2,64,128]{2,1,0:T(8,128)(2,1)S(1)}, u32[]{:S(2)}, u32[]{:S(2)}) collective-permute-start(bf16[2,64,128]{2,1,0:T(8,128)(2,1)S(1)} %pad_maximum_fusion.bc_0), channel_id=1, source_target_pairs={{0,48},{16,0},{32,16},{48,32},{1,49},{17,1},{33,17},{49,33},{2,50}... | collective-permute-start | bytes 98312 | tf_op jit(solution)/shard_map/ppermute | solution.py:45
  83.0 2.5 %collective-permute-done.6.bc_3 = bf16[2,64,128]{2,1,0:T(8,128)(2,1)S(1)} collective-permute-done((bf16[2,64,128]{2,1,0:T(8,128)(2,1)S(1)}, bf16[2,64,128]{2,1,0:T(8,128)(2,1)S(1)}, u32[]{:S(2)}, u32[]{:S(2)}) %collective-permute-start.6) | collective-permute-done | bytes 32800 | tf_op jit(solution)/shard_map/ppermute | solution.py:45
  92.1 7.8 %all-to-all-start.4 = ((bf16[32,2,16,256]{3,2,1,0:T(8,128)(2,1)}), bf16[32,2,16,256]{3,2,1,0:T(8,128)(2,1)S(1)}, u32[]{:S(2)}, u32[]{:S(2)}) async-start(bf16[32,2,16,256]{3,2,1,0:T(8,128)(2,1)} %bitcast.16), calls=%async_computation.4 | async-start | bytes 1048576 | tf_op jit(solution)/shard_map/all_to_all | solution.py:49
  99.9 3.4 %collective-permute-start.9 = (bf16[128,1024]{1,0:T(8,128)(2,1)S(1)}, bf16[128,1024]{1,0:T(8,128)(2,1)S(1)}, u32[]{:S(2)}, u32[]{:S(2)}) collective-permute-start(bf16[128,1024]{1,0:T(8,128)(2,1)S(1)} %slice.6), channel_id=1, source_target_pairs={{0,16},{16,32},{32,48},{48,0},{1,17},{17,33},{33,49},{49,1},{2,18}... | collective-permute-start | bytes 786440 | tf_op jit(solution)/shard_map/ppermute | solution.py:378
  103.3 3.7 %collective-permute-start.10 = (bf16[128,1024]{1,0:T(8,128)(2,1)S(1)}, bf16[128,1024]{1,0:T(8,128)(2,1)S(1)}, u32[]{:S(2)}, u32[]{:S(2)}) collective-permute-start(bf16[128,1024]{1,0:T(8,128)(2,1)S(1)} %slice.7), channel_id=1, source_target_pairs={{0,48},{16,0},{32,16},{48,32},{1,49},{17,1},{33,17},{49,33},{2,50}... | collective-permute-start | bytes 786440 | tf_op jit(solution)/shard_map/ppermute | solution.py:379
  107.0 6.9 %collective-permute-done.9.low_ref = bf16[128,1024]{1,0:T(8,128)(2,1)S(1)} collective-permute-done((bf16[128,1024]{1,0:T(8,128)(2,1)S(1)}, bf16[128,1024]{1,0:T(8,128)(2,1)S(1)}, u32[]{:S(2)}, u32[]{:S(2)}) %collective-permute-start.9) | collective-permute-done | bytes 262176 | tf_op jit(solution)/shard_map/ppermute | solution.py:378
  114.7 2.0 %all-to-all-done.4 = bf16[32,2,16,256]{3,2,1,0:T(8,128)(2,1)S(1)} async-done(((bf16[32,2,16,256]{3,2,1,0:T(8,128)(2,1)}), bf16[32,2,16,256]{3,2,1,0:T(8,128)(2,1)S(1)}, u32[]{:S(2)}, u32[]{:S(2)}) %all-to-all-start.4) | async-done | bytes 524320 | tf_op jit(solution)/shard_map/all_to_all | solution.py:49
  117.8 1.9 %collective-permute-start.11 = (bf16[8,16,1024]{2,1,0:T(8,128)(2,1)S(1)}, bf16[8,16,1024]{2,1,0:T(8,128)(2,1)S(1)}, u32[]{:S(2)}, u32[]{:S(2)}) collective-permute-start(bf16[8,16,1024]{2,1,0:T(8,128)(2,1)S(1)} %shard_map.169), channel_id=1, source_target_pairs={{0,8},{8,0},{1,9},{9,1},{2,10},{10,2},{3,11},{11,3},{4,12},{12,4},... | collective-permute-start | bytes 786440 | tf_op jit(solution)/shard_map/ppermute | solution.py:32
  121.3 15.0 %all_to_all.31.p_ref = bf16[8,16,1024]{2,1,0:T(8,128)(2,1)S(1)} all-to-all(bf16[8,16,1024]{2,1,0:T(8,128)(2,1)S(1)} %shard_map.170), channel_id=1, replica_groups=mesh['z'=8,'x'=4,'core'=2,'y'=8] {'z'}, dimensions={0} | all-to-all | bytes 524288 | tf_op jit(solution)/shard_map/all_to_all | solution.py:49
  (66 shorter events, 18.1 us)
Async XLA Ops:
  0.0 30.3 %copy-start.3 = (bf16[1024,256]{1,0:T(8,128)(2,1)S(1)}, bf16[1024,256]{1,0:T(8,128)(2,1)}, u32[]{:S(2)}) copy-start(bf16[1024,256]{1,0:T(8,128)(2,1)} %refs_1_.1) | copy-start | bytes 1572868
  0.0 32.8 %copy-start.10 = (bf16[1024,4]{0,1:T(4,128)(2,1)S(1)}, bf16[1024,4]{0,1:T(4,128)(2,1)}, u32[]{:S(2)}) copy-start(bf16[1024,4]{0,1:T(4,128)(2,1)} %param.22) | copy-start | bytes 24580
  0.0 32.8 %copy-start.9 = (bf16[1024,64]{0,1:T(8,128)(2,1)S(1)}, bf16[1024,64]{0,1:T(8,128)(2,1)}, u32[]{:S(2)}) copy-start(bf16[1024,64]{0,1:T(8,128)(2,1)} %param.21) | copy-start | bytes 393220
  0.0 41.7 %copy-start.7 = (f32[1024]{0:T(1024)S(1)}, f32[1024]{0:T(1024)}, u32[]{:S(2)}) copy-start(f32[1024]{0:T(1024)} %param.18) | copy-start | bytes 12292
  24.1 17.6 %all-to-all-start.1 = ((bf16[4,8,16,1024]{3,2,1,0:T(8,128)(2,1)}), bf16[4,8,16,1024]{3,2,1,0:T(8,128)(2,1)S(1)}, u32[]{:S(2)}, u32[]{:S(2)}) async-start(bf16[4,8,16,1024]{3,2,1,0:T(8,128)(2,1)} %broadcast_in_dim.25), calls=%async_computation.1 | async-start | bytes 2097152 | tf_op jit(solution)/shard_map/all_to_all | solution.py:36
  28.4 22.7 %collective-permute-start = (bf16[1024,256]{1,0:T(8,128)(2,1)S(1)}, bf16[1024,256]{1,0:T(8,128)(2,1)}, u32[]{:S(2)}, u32[]{:S(2)}) collective-permute-start(bf16[1024,256]{1,0:T(8,128)(2,1)S(1)} %copy-done.2), channel_id=1, source_target_pairs={{0,8},{8,0},{1,9},{9,1},{2,10},{10,2},{3,11},{11,3},{4,12},{12,4},... | collective-permute-start | bytes 1572872 | tf_op jit(solution)/shard_map/ppermute | solution.py:32
  30.3 20.8 %collective-permute-start.1 = (bf16[1024,256]{1,0:T(8,128)(2,1)S(1)}, bf16[1024,256]{1,0:T(8,128)(2,1)}, u32[]{:S(2)}, u32[]{:S(2)}) collective-permute-start(bf16[1024,256]{1,0:T(8,128)(2,1)S(1)} %copy-done.3), channel_id=1, source_target_pairs={{0,8},{8,0},{1,9},{9,1},{2,10},{10,2},{3,11},{11,3},{4,12},{12,4},... | collective-permute-start | bytes 1572872 | tf_op jit(solution)/shard_map/ppermute | solution.py:32
  32.9 3.3 %collective-permute-start.2 = (bf16[80,1024]{1,0:T(8,128)(2,1)S(1)}, bf16[80,1024]{1,0:T(8,128)(2,1)S(1)}, u32[]{:S(2)}, u32[]{:S(2)}) collective-permute-start(bf16[80,1024]{1,0:T(8,128)(2,1)S(1)} %maximum_maximum_fusion.refs_4_.w_ref), channel_id=1, source_target_pairs={{0,8},{8,0},{1,9},{9,1},{2,10},{10,2},{3,11},{11,3},{4,12},{12,4},... | collective-permute-start | bytes 491528 | tf_op jit(solution)/shard_map/ppermute | solution.py:32
  43.5 15.8 %all-to-all-start.2 = ((bf16[16,32,128]{2,1,0:T(8,128)(2,1)}), bf16[16,32,128]{2,1,0:T(8,128)(2,1)S(1)}, u32[]{:S(2)}, u32[]{:S(2)}) async-start(bf16[16,32,128]{2,1,0:T(8,128)(2,1)} %bitcast.5), calls=%async_computation.2 | async-start | bytes 262144 | tf_op jit(solution)/shard_map/all_to_all | solution.py:49
  51.1 31.7 %copy-start.11 = (f32[4,256]{1,0:T(4,128)S(1)}, f32[4,256]{1,0:T(4,128)}, u32[]{:S(2)}) copy-start(f32[4,256]{1,0:T(4,128)} %param.23) | copy-start | bytes 12292
  51.1 31.7 %copy-start.12 = (f32[256]{0:T(256)S(1)}, f32[256]{0:T(256)}, u32[]{:S(2)}) copy-start(f32[256]{0:T(256)} %param.31) | copy-start | bytes 3076
  54.9 35.5 %copy-start.4 = (bf16[240,1024]{1,0:T(8,128)(2,1)S(1)}, bf16[240,1024]{1,0:T(8,128)(2,1)}, u32[]{:S(2)}) copy-start(bf16[240,1024]{1,0:T(8,128)(2,1)} %constant.17.clone.orders_ref) | copy-start | bytes 1474564
  54.9 35.5 %copy-start.5 = (bf16[24,3,256]{2,0,1:T(8,128)(2,1)S(1)}, bf16[24,3,256]{2,0,1:T(8,128)(2,1)}, u32[]{:S(2)}) copy-start(bf16[24,3,256]{2,0,1:T(8,128)(2,1)} %param.25) | copy-start | bytes 110596
  59.8 30.6 %all-to-all-start.3 = ((bf16[16,64,512]{2,1,0:T(8,128)(2,1)}), bf16[16,64,512]{2,1,0:T(8,128)(2,1)S(1)}, u32[]{:S(2)}, u32[]{:S(2)}) async-start(bf16[16,64,512]{2,1,0:T(8,128)(2,1)} %bitcast.10), calls=%async_computation.3 | async-start | bytes 2097152 | tf_op jit(solution)/shard_map/all_to_all | solution.py:49
  63.6 25.3 %collective-permute-start.7 = (bf16[256,1024]{1,0:T(8,128)(2,1)S(1)}, bf16[256,1024]{1,0:T(8,128)(2,1)S(1)}, u32[]{:S(2)}, u32[]{:S(2)}) collective-permute-start(bf16[256,1024]{1,0:T(8,128)(2,1)S(1)} %copy-done.1), channel_id=1, source_target_pairs={{0,16},{16,32},{32,48},{48,0},{1,17},{17,33},{33,49},{49,1},{2,18}... | collective-permute-start | bytes 1572872 | tf_op jit(solution)/shard_map/ppermute | solution.py:361
  66.1 22.9 %collective-permute-start.8 = (bf16[256,1024]{1,0:T(8,128)(2,1)S(1)}, bf16[256,1024]{1,0:T(8,128)(2,1)S(1)}, u32[]{:S(2)}, u32[]{:S(2)}) collective-permute-start(bf16[256,1024]{1,0:T(8,128)(2,1)S(1)} %copy-done.1), channel_id=1, source_target_pairs={{0,48},{16,0},{32,16},{48,32},{1,49},{17,1},{33,17},{49,33},{2,50}... | collective-permute-start | bytes 1572872 | tf_op jit(solution)/shard_map/ppermute | solution.py:361
  70.7 3.1 %collective-permute-start.3 = (bf16[64,128]{1,0:T(8,128)(2,1)S(1)}, bf16[64,128]{1,0:T(8,128)(2,1)S(1)}, u32[]{:S(2)}, u32[]{:S(2)}) collective-permute-start(bf16[64,128]{1,0:T(8,128)(2,1)S(1)} %get-tuple-element.21), channel_id=1, source_target_pairs={{0,8},{8,0},{1,9},{9,1},{2,10},{10,2},{3,11},{11,3},{4,12},{12,4},... | collective-permute-start | bytes 49160 | tf_op jit(solution)/shard_map/ppermute | solution.py:32
  73.8 9.0 %collective-permute-start.4 = (bf16[2,64,128]{2,1,0:T(8,128)(2,1)S(1)}, bf16[2,64,128]{2,1,0:T(8,128)(2,1)S(1)}, u32[]{:S(2)}, u32[]{:S(2)}) collective-permute-start(bf16[2,64,128]{2,1,0:T(8,128)(2,1)S(1)} %pad_maximum_fusion.bc_0), channel_id=1, source_target_pairs={{0,16},{16,32},{32,48},{48,0},{1,17},{17,33},{33,49},{49,1},{2,18}... | collective-permute-start | bytes 98312 | tf_op jit(solution)/shard_map/ppermute | solution.py:45
  75.7 7.3 %collective-permute-start.5 = (bf16[2,64,128]{2,1,0:T(8,128)(2,1)S(1)}, bf16[2,64,128]{2,1,0:T(8,128)(2,1)S(1)}, u32[]{:S(2)}, u32[]{:S(2)}) collective-permute-start(bf16[2,64,128]{2,1,0:T(8,128)(2,1)S(1)} %pad_maximum_fusion.bc_0), channel_id=1, source_target_pairs={{0,32},{16,48},{32,0},{48,16},{1,33},{17,49},{33,1},{49,17},{2,34}... | collective-permute-start | bytes 98312 | tf_op jit(solution)/shard_map/ppermute | solution.py:45
  79.1 6.4 %collective-permute-start.6 = (bf16[2,64,128]{2,1,0:T(8,128)(2,1)S(1)}, bf16[2,64,128]{2,1,0:T(8,128)(2,1)S(1)}, u32[]{:S(2)}, u32[]{:S(2)}) collective-permute-start(bf16[2,64,128]{2,1,0:T(8,128)(2,1)S(1)} %pad_maximum_fusion.bc_0), channel_id=1, source_target_pairs={{0,48},{16,0},{32,16},{48,32},{1,49},{17,1},{33,17},{49,33},{2,50}... | collective-permute-start | bytes 98312 | tf_op jit(solution)/shard_map/ppermute | solution.py:45
  92.1 24.6 %all-to-all-start.4 = ((bf16[32,2,16,256]{3,2,1,0:T(8,128)(2,1)}), bf16[32,2,16,256]{3,2,1,0:T(8,128)(2,1)S(1)}, u32[]{:S(2)}, u32[]{:S(2)}) async-start(bf16[32,2,16,256]{3,2,1,0:T(8,128)(2,1)} %bitcast.16), calls=%async_computation.4 | async-start | bytes 1048576 | tf_op jit(solution)/shard_map/all_to_all | solution.py:49
  99.9 14.0 %collective-permute-start.9 = (bf16[128,1024]{1,0:T(8,128)(2,1)S(1)}, bf16[128,1024]{1,0:T(8,128)(2,1)S(1)}, u32[]{:S(2)}, u32[]{:S(2)}) collective-permute-start(bf16[128,1024]{1,0:T(8,128)(2,1)S(1)} %slice.6), channel_id=1, source_target_pairs={{0,16},{16,32},{32,48},{48,0},{1,17},{17,33},{33,49},{49,1},{2,18}... | collective-permute-start | bytes 786440 | tf_op jit(solution)/shard_map/ppermute | solution.py:378
  103.3 11.4 %collective-permute-start.10 = (bf16[128,1024]{1,0:T(8,128)(2,1)S(1)}, bf16[128,1024]{1,0:T(8,128)(2,1)S(1)}, u32[]{:S(2)}, u32[]{:S(2)}) collective-permute-start(bf16[128,1024]{1,0:T(8,128)(2,1)S(1)} %slice.7), channel_id=1, source_target_pairs={{0,48},{16,0},{32,16},{48,32},{1,49},{17,1},{33,17},{49,33},{2,50}... | collective-permute-start | bytes 786440 | tf_op jit(solution)/shard_map/ppermute | solution.py:379
  117.8 3.4 %collective-permute-start.11 = (bf16[8,16,1024]{2,1,0:T(8,128)(2,1)S(1)}, bf16[8,16,1024]{2,1,0:T(8,128)(2,1)S(1)}, u32[]{:S(2)}, u32[]{:S(2)}) collective-permute-start(bf16[8,16,1024]{2,1,0:T(8,128)(2,1)S(1)} %shard_map.169), channel_id=1, source_target_pairs={{0,8},{8,0},{1,9},{9,1},{2,10},{10,2},{3,11},{11,3},{4,12},{12,4},... | collective-permute-start | bytes 786440 | tf_op jit(solution)/shard_map/ppermute | solution.py:32
  (8 other events, 142.7 us)

commit v6 on v5

--- a/solution.py
+++ b/solution.py
@@ -83,14 +83,14 @@
     lane = lax.broadcasted_iota(jnp.int32, out.shape, 1) % 64
     slot = lax.broadcasted_iota(jnp.int32, out.shape, 0) % SLOT
     ss = jnp.where(lane == slot, hi, jnp.where(lane == slot + SLOT, ss - hi, 0.0))
-    out = into_empty(ss, lane < 2 * SLOT, out).reshape(NX, NZ, SLOT, 128)
+    out = into_empty(ss, lane < 2 * SLOT, out).astype(BF).reshape(NX, NZ, SLOT, 128)
     for x in range(2):
         low, high = out[x], out[x + 2]
         rows = slice(x * SLOT, x * SLOT + SLOT)
         own = jnp.concatenate([low[:, :, :64], high[:, :, :64]], axis=2)
         other = jnp.concatenate([low[:, :, 64:], high[:, :, 64:]], axis=2)
-        out_ref[pos_ref[0], :, rows] = own.astype(BF)
-        out_ref[1 - pos_ref[0], :, rows] = other.astype(BF)
+        out_ref[pos_ref[0], :, rows] = own
+        out_ref[1 - pos_ref[0], :, rows] = other
 
 
 def large_kernel(pos_ref, g_ref, gain_ref, *refs):
@@ -336,7 +336,8 @@
     shape = jax.ShapeDtypeStruct
     pos = jnp.stack([lax.axis_index("core"), lax.axis_index("x")]).astype(jnp.int32)
     tokens = jnp.pad(inputs.reshape(STEPS * OWN, -1), ((0, 1), (0, 0)))
-    gathered = to_all(to_all(tokens, "z", NZ), "x", NX)
+    column = to_all(tokens, "z", NZ).reshape(NZ * SLOT, -1)
+    gathered = to_all(column, "x", NX)
     gain = pre_gain[None]
     w_small = jnp.concatenate([w_bc.T, w_dt.T, jnp.zeros((12, w_bc.shape[0]), BF)], axis=0)
     w_small_other = swap_core(w_small)
@@ -364,7 +365,7 @@
         carried_kernel,
         shape((STEPS * RB, 384), F32),
         [SM] + [VM] * 6,
-        scratch_shapes=[pltpu.VMEM((2, RB * 8, 128), F32)] * 2
+        scratch_shapes=[pltpu.VMEM((2, RB * 8 + 8, 128), F32)] * 2
         + [pltpu.VMEM((NX * NC, 64, 128), F32)],
     )(
         pos, *around_x(jnp.stack([bcc, swap_core(bcc)])), rstd, ssm_state.reshape(RB, 256, 256)
@@ -373,7 +374,7 @@
     u = call(state_kernel, shape((NX, NY, NC, SLOT, 256), BF), [VM] * 5)(
         ready, large, params, jnp.swapaxes(conv_x_state, 0, 1), orders()
     )
-    u = exchange(u.reshape(NX * NY, NC, SLOT, 256), ("x", "y")).reshape(u.shape)
+    u = exchange(u.reshape(NX * NY, NC * SLOT, 256), ("x", "y")).reshape(u.shape)
     half = w_out.shape[0] // 2
     low = lax.ppermute(left[:half], "x", NEXT)
     high = lax.ppermute(right[half:], "x", PREVIOUS)

time: 138 us -> 138 us (level)
  no operation moved by 1% of the time
where the time goes in v6:
time: 138 us; the launch traced here: 137 us
  starting transfers between devices  56.6 us (41%)
  blocking collectives  37 us (27%)
  waiting for transfers between devices  26.3 us (19%)
  Pallas kernels  12.3 us (9%)
  local copies, waits for them, and re-layouts  4.27 us (3%)
    all_to_all x1, blocking collectives, to_all(): lax.all_to_all(jnp.broadcast_to(v[None], (count,) + v.shape), axes, split...  22 us
    all_to_all x3, starting transfers between devices, exchange(): return lax.all_to_all(v, axes, split_axis=0, concat_axis=0, tiled=True)  19.1 us
    all_to_all x1, blocking collectives, exchange(): return lax.all_to_all(v, axes, split_axis=0, concat_axis=0, tiled=True)  15 us
    ppermute x5, starting transfers between devices, swap_core(): return lax.ppermute(v, 'core', [(0, 1), (1, 0)])  10.1 us
    ppermute x3, starting transfers between devices, around_x(): return [v] + [lax.ppermute(v, 'x', way) for way in (NEXT, ACROSS, PREVIOUS)]  8.96 us
    all_to_all x3, waiting for transfers between devices, exchange(): return lax.all_to_all(v, axes, split_axis=0, concat_axis=0, tiled=True)  7.78 us
    ppermute x2, starting transfers between devices, per_device(): left, right = (lax.ppermute(w_out, 'x', way) for way in (NEXT, PREVIOUS))  7.05 us
    ppermute x1, waiting for transfers between devices, per_device(): low = lax.ppermute(left[:half], 'x', NEXT)  6.92 us
  transfers between devices with their start and end apart: 16, of which 11 were waited for; matrix products, arithmetic and copies ran while one was open for 0% of the time, Pallas kernels for 6%

profile of v6, /device:TPU:8, one launch (start us, length us, event | category | flops | bytes accessed | tf_op | source)
XLA Modules:
  0.0 137.1 jit_solution(17976563655671721946)
XLA Ops:
  1.0 22.0 %all_to_all.30 = bf16[8,16,1024]{2,1,0:T(8,128)(2,1)S(1)} all-to-all(bf16[8,16,1024]{2,1,0:T(8,128)(2,1)S(1)} %broadcast_in_dim.25), channel_id=1, replica_groups=mesh['z'=8,'x'=4,'core'=2,'y'=8] {'z'}, dimensions={0} | all-to-all | bytes 524288 | tf_op jit(solution)/shard_map/all_to_all | solution.py:36
  24.1 4.3 %all-to-all-start.1 = ((bf16[4,128,1024]{2,1,0:T(8,128)(2,1)}), bf16[4,128,1024]{2,1,0:T(8,128)(2,1)S(1)}, u32[]{:S(2)}, u32[]{:S(2)}) async-start(bf16[4,128,1024]{2,1,0:T(8,128)(2,1)} %broadcast_in_dim.27), calls=%async_computation.1 | async-start | bytes 2097152 | tf_op jit(solution)/shard_map/all_to_all | solution.py:36
  28.4 1.9 %collective-permute-start = (bf16[1024,256]{1,0:T(8,128)(2,1)S(1)}, bf16[1024,256]{1,0:T(8,128)(2,1)}, u32[]{:S(2)}, u32[]{:S(2)}) collective-permute-start(bf16[1024,256]{1,0:T(8,128)(2,1)S(1)} %copy-done.2), channel_id=1, source_target_pairs={{0,8},{8,0},{1,9},{9,1},{2,10},{10,2},{3,11},{11,3},{4,12},{12,4},... | collective-permute-start | bytes 1572872 | tf_op jit(solution)/shard_map/ppermute | solution.py:32
  30.3 2.4 %collective-permute-start.1 = (bf16[1024,256]{1,0:T(8,128)(2,1)S(1)}, bf16[1024,256]{1,0:T(8,128)(2,1)}, u32[]{:S(2)}, u32[]{:S(2)}) collective-permute-start(bf16[1024,256]{1,0:T(8,128)(2,1)S(1)} %copy-done.3), channel_id=1, source_target_pairs={{0,8},{8,0},{1,9},{9,1},{2,10},{10,2},{3,11},{11,3},{4,12},{12,4},... | collective-permute-start | bytes 1572872 | tf_op jit(solution)/shard_map/ppermute | solution.py:32
  32.9 1.9 %collective-permute-start.2 = (bf16[80,1024]{1,0:T(8,128)(2,1)S(1)}, bf16[80,1024]{1,0:T(8,128)(2,1)S(1)}, u32[]{:S(2)}, u32[]{:S(2)}) collective-permute-start(bf16[80,1024]{1,0:T(8,128)(2,1)S(1)} %maximum_maximum_fusion.refs_4_.w_ref), channel_id=1, source_target_pairs={{0,8},{8,0},{1,9},{9,1},{2,10},{10,2},{3,11},{11,3},{4,12},{12,4},... | collective-permute-start | bytes 491528 | tf_op jit(solution)/shard_map/ppermute | solution.py:32
  36.2 5.5 %all-to-all-done.1.g_ref = bf16[4,128,1024]{2,1,0:T(8,128)(2,1)S(1)} async-done(((bf16[4,128,1024]{2,1,0:T(8,128)(2,1)}), bf16[4,128,1024]{2,1,0:T(8,128)(2,1)S(1)}, u32[]{:S(2)}, u32[]{:S(2)}) %all-to-all-start.1) | async-done | bytes 1048608 | tf_op jit(solution)/shard_map/all_to_all | solution.py:36
  43.5 7.6 %all-to-all-start.2 = ((bf16[16,32,128]{2,1,0:T(8,128)(2,1)}), bf16[16,32,128]{2,1,0:T(8,128)(2,1)S(1)}, u32[]{:S(2)}, u32[]{:S(2)}) async-start(bf16[16,32,128]{2,1,0:T(8,128)(2,1)} %bitcast.6), calls=%async_computation.2 | async-start | bytes 262144 | tf_op jit(solution)/shard_map/all_to_all | solution.py:49
  51.2 3.8 %shard_map.163 = bf16[2,8,64,512]{3,2,1,0:T(8,128)(2,1)} custom-call(s32[2]{0:T(128)S(1)} %pad_add_fusion.pos_ref, bf16[4,128,1024]{2,1,0:T(8,128)(2,1)S(1)} %all-to-all-done.1.g_ref, f32[1,1024]{1,0:T(1,128)S(1)} %bitcast.26, bf16[1024,256]{1,0:T(8,128)(2,1)S(1)} %copy-done.2, bf16[1024,256]{1,0:T(8,128)(2,1)S(1)} %copy-done.3, ...), custom_call_target="tpu_custom_call" | custom-call | tf_op jit(solution)/shard_map/pallas_call | solution.py:348
  55.0 4.3 %all-to-all-done.2.p_ref = bf16[16,32,128]{2,1,0:T(8,128)(2,1)S(1)} async-done(((bf16[16,32,128]{2,1,0:T(8,128)(2,1)}), bf16[16,32,128]{2,1,0:T(8,128)(2,1)S(1)}, u32[]{:S(2)}, u32[]{:S(2)}) %all-to-all-start.2) | async-done | bytes 131104 | tf_op jit(solution)/shard_map/all_to_all | solution.py:49
  59.8 3.8 %all-to-all-start.3 = ((bf16[16,64,512]{2,1,0:T(8,128)(2,1)}), bf16[16,64,512]{2,1,0:T(8,128)(2,1)S(1)}, u32[]{:S(2)}, u32[]{:S(2)}) async-start(bf16[16,64,512]{2,1,0:T(8,128)(2,1)} %bitcast.11), calls=%async_computation.3 | async-start | bytes 2097152 | tf_op jit(solution)/shard_map/all_to_all | solution.py:49
  63.7 2.5 %collective-permute-start.7 = (bf16[256,1024]{1,0:T(8,128)(2,1)S(1)}, bf16[256,1024]{1,0:T(8,128)(2,1)S(1)}, u32[]{:S(2)}, u32[]{:S(2)}) collective-permute-start(bf16[256,1024]{1,0:T(8,128)(2,1)S(1)} %copy-done.1), channel_id=1, source_target_pairs={{0,16},{16,32},{32,48},{48,0},{1,17},{17,33},{33,49},{49,1},{2,18}... | collective-permute-start | bytes 1572872 | tf_op jit(solution)/shard_map/ppermute | solution.py:362
  66.1 4.6 %collective-permute-start.8 = (bf16[256,1024]{1,0:T(8,128)(2,1)S(1)}, bf16[256,1024]{1,0:T(8,128)(2,1)S(1)}, u32[]{:S(2)}, u32[]{:S(2)}) collective-permute-start(bf16[256,1024]{1,0:T(8,128)(2,1)S(1)} %copy-done.1), channel_id=1, source_target_pairs={{0,48},{16,0},{32,16},{48,32},{1,49},{17,1},{33,17},{49,33},{2,50}... | collective-permute-start | bytes 1572872 | tf_op jit(solution)/shard_map/ppermute | solution.py:362
  70.7 1.9 %collective-permute-start.3 = (bf16[64,128]{1,0:T(8,128)(2,1)S(1)}, bf16[64,128]{1,0:T(8,128)(2,1)S(1)}, u32[]{:S(2)}, u32[]{:S(2)}) collective-permute-start(bf16[64,128]{1,0:T(8,128)(2,1)S(1)} %get-tuple-element.21), channel_id=1, source_target_pairs={{0,8},{8,0},{1,9},{9,1},{2,10},{10,2},{3,11},{11,3},{4,12},{12,4},... | collective-permute-start | bytes 49160 | tf_op jit(solution)/shard_map/ppermute | solution.py:32
  73.8 1.9 %collective-permute-start.4 = (bf16[2,64,128]{2,1,0:T(8,128)(2,1)S(1)}, bf16[2,64,128]{2,1,0:T(8,128)(2,1)S(1)}, u32[]{:S(2)}, u32[]{:S(2)}) collective-permute-start(bf16[2,64,128]{2,1,0:T(8,128)(2,1)S(1)} %pad_maximum_fusion.bc_0), channel_id=1, source_target_pairs={{0,16},{16,32},{32,48},{48,0},{1,17},{17,33},{33,49},{49,1},{2,18}... | collective-permute-start | bytes 98312 | tf_op jit(solution)/shard_map/ppermute | solution.py:45
  75.7 3.4 %collective-permute-start.5 = (bf16[2,64,128]{2,1,0:T(8,128)(2,1)S(1)}, bf16[2,64,128]{2,1,0:T(8,128)(2,1)S(1)}, u32[]{:S(2)}, u32[]{:S(2)}) collective-permute-start(bf16[2,64,128]{2,1,0:T(8,128)(2,1)S(1)} %pad_maximum_fusion.bc_0), channel_id=1, source_target_pairs={{0,32},{16,48},{32,0},{48,16},{1,33},{17,49},{33,1},{49,17},{2,34}... | collective-permute-start | bytes 98312 | tf_op jit(solution)/shard_map/ppermute | solution.py:45
  79.1 3.7 %collective-permute-start.6 = (bf16[2,64,128]{2,1,0:T(8,128)(2,1)S(1)}, bf16[2,64,128]{2,1,0:T(8,128)(2,1)S(1)}, u32[]{:S(2)}, u32[]{:S(2)}) collective-permute-start(bf16[2,64,128]{2,1,0:T(8,128)(2,1)S(1)} %pad_maximum_fusion.bc_0), channel_id=1, source_target_pairs={{0,48},{16,0},{32,16},{48,32},{1,49},{17,1},{33,17},{49,33},{2,50}... | collective-permute-start | bytes 98312 | tf_op jit(solution)/shard_map/ppermute | solution.py:45
  83.0 2.5 %collective-permute-done.6.bc_3 = bf16[2,64,128]{2,1,0:T(8,128)(2,1)S(1)} collective-permute-done((bf16[2,64,128]{2,1,0:T(8,128)(2,1)S(1)}, bf16[2,64,128]{2,1,0:T(8,128)(2,1)S(1)}, u32[]{:S(2)}, u32[]{:S(2)}) %collective-permute-start.6) | collective-permute-done | bytes 32800 | tf_op jit(solution)/shard_map/ppermute | solution.py:45
  92.1 7.8 %all-to-all-start.4 = ((bf16[32,32,256]{2,1,0:T(8,128)(2,1)}), bf16[32,32,256]{2,1,0:T(8,128)(2,1)S(1)}, u32[]{:S(2)}, u32[]{:S(2)}) async-start(bf16[32,32,256]{2,1,0:T(8,128)(2,1)} %bitcast.17), calls=%async_computation.4 | async-start | bytes 1048576 | tf_op jit(solution)/shard_map/all_to_all | solution.py:49
  99.9 3.4 %collective-permute-start.9 = (bf16[128,1024]{1,0:T(8,128)(2,1)S(1)}, bf16[128,1024]{1,0:T(8,128)(2,1)S(1)}, u32[]{:S(2)}, u32[]{:S(2)}) collective-permute-start(bf16[128,1024]{1,0:T(8,128)(2,1)S(1)} %slice.6), channel_id=1, source_target_pairs={{0,16},{16,32},{32,48},{48,0},{1,17},{17,33},{33,49},{49,1},{2,18}... | collective-permute-start | bytes 786440 | tf_op jit(solution)/shard_map/ppermute | solution.py:379
  103.4 3.7 %collective-permute-start.10 = (bf16[128,1024]{1,0:T(8,128)(2,1)S(1)}, bf16[128,1024]{1,0:T(8,128)(2,1)S(1)}, u32[]{:S(2)}, u32[]{:S(2)}) collective-permute-start(bf16[128,1024]{1,0:T(8,128)(2,1)S(1)} %slice.7), channel_id=1, source_target_pairs={{0,48},{16,0},{32,16},{48,32},{1,49},{17,1},{33,17},{49,33},{2,50}... | collective-permute-start | bytes 786440 | tf_op jit(solution)/shard_map/ppermute | solution.py:380
  107.0 6.9 %collective-permute-done.9.low_ref = bf16[128,1024]{1,0:T(8,128)(2,1)S(1)} collective-permute-done((bf16[128,1024]{1,0:T(8,128)(2,1)S(1)}, bf16[128,1024]{1,0:T(8,128)(2,1)S(1)}, u32[]{:S(2)}, u32[]{:S(2)}) %collective-permute-start.9) | collective-permute-done | bytes 262176 | tf_op jit(solution)/shard_map/ppermute | solution.py:379
  114.7 2.0 %all-to-all-done.4 = bf16[32,32,256]{2,1,0:T(8,128)(2,1)S(1)} async-done(((bf16[32,32,256]{2,1,0:T(8,128)(2,1)}), bf16[32,32,256]{2,1,0:T(8,128)(2,1)S(1)}, u32[]{:S(2)}, u32[]{:S(2)}) %all-to-all-start.4) | async-done | bytes 524320 | tf_op jit(solution)/shard_map/all_to_all | solution.py:49
  117.8 1.9 %collective-permute-start.11 = (bf16[8,16,1024]{2,1,0:T(8,128)(2,1)S(1)}, bf16[8,16,1024]{2,1,0:T(8,128)(2,1)S(1)}, u32[]{:S(2)}, u32[]{:S(2)}) collective-permute-start(bf16[8,16,1024]{2,1,0:T(8,128)(2,1)S(1)} %shard_map.169), channel_id=1, source_target_pairs={{0,8},{8,0},{1,9},{9,1},{2,10},{10,2},{3,11},{11,3},{4,12},{12,4},... | collective-permute-start | bytes 786440 | tf_op jit(solution)/shard_map/ppermute | solution.py:32
  121.4 15.0 %all_to_all.31.p_ref = bf16[8,16,1024]{2,1,0:T(8,128)(2,1)S(1)} all-to-all(bf16[8,16,1024]{2,1,0:T(8,128)(2,1)S(1)} %shard_map.170), channel_id=1, replica_groups=mesh['z'=8,'x'=4,'core'=2,'y'=8] {'z'}, dimensions={0} | all-to-all | bytes 524288 | tf_op jit(solution)/shard_map/all_to_all | solution.py:49
  (66 shorter events, 18.1 us)
Async XLA Ops:
  0.0 30.3 %copy-start.3 = (bf16[1024,256]{1,0:T(8,128)(2,1)S(1)}, bf16[1024,256]{1,0:T(8,128)(2,1)}, u32[]{:S(2)}) copy-start(bf16[1024,256]{1,0:T(8,128)(2,1)} %refs_1_.1) | copy-start | bytes 1572868
  0.0 32.8 %copy-start.10 = (bf16[1024,4]{0,1:T(4,128)(2,1)S(1)}, bf16[1024,4]{0,1:T(4,128)(2,1)}, u32[]{:S(2)}) copy-start(bf16[1024,4]{0,1:T(4,128)(2,1)} %param.22) | copy-start | bytes 24580
  0.0 32.8 %copy-start.9 = (bf16[1024,64]{0,1:T(8,128)(2,1)S(1)}, bf16[1024,64]{0,1:T(8,128)(2,1)}, u32[]{:S(2)}) copy-start(bf16[1024,64]{0,1:T(8,128)(2,1)} %param.21) | copy-start | bytes 393220
  0.0 41.7 %copy-start.7 = (f32[1024]{0:T(1024)S(1)}, f32[1024]{0:T(1024)}, u32[]{:S(2)}) copy-start(f32[1024]{0:T(1024)} %param.18) | copy-start | bytes 12292
  24.1 17.6 %all-to-all-start.1 = ((bf16[4,128,1024]{2,1,0:T(8,128)(2,1)}), bf16[4,128,1024]{2,1,0:T(8,128)(2,1)S(1)}, u32[]{:S(2)}, u32[]{:S(2)}) async-start(bf16[4,128,1024]{2,1,0:T(8,128)(2,1)} %broadcast_in_dim.27), calls=%async_computation.1 | async-start | bytes 2097152 | tf_op jit(solution)/shard_map/all_to_all | solution.py:36
  28.4 22.8 %collective-permute-start = (bf16[1024,256]{1,0:T(8,128)(2,1)S(1)}, bf16[1024,256]{1,0:T(8,128)(2,1)}, u32[]{:S(2)}, u32[]{:S(2)}) collective-permute-start(bf16[1024,256]{1,0:T(8,128)(2,1)S(1)} %copy-done.2), channel_id=1, source_target_pairs={{0,8},{8,0},{1,9},{9,1},{2,10},{10,2},{3,11},{11,3},{4,12},{12,4},... | collective-permute-start | bytes 1572872 | tf_op jit(solution)/shard_map/ppermute | solution.py:32
  30.3 20.9 %collective-permute-start.1 = (bf16[1024,256]{1,0:T(8,128)(2,1)S(1)}, bf16[1024,256]{1,0:T(8,128)(2,1)}, u32[]{:S(2)}, u32[]{:S(2)}) collective-permute-start(bf16[1024,256]{1,0:T(8,128)(2,1)S(1)} %copy-done.3), channel_id=1, source_target_pairs={{0,8},{8,0},{1,9},{9,1},{2,10},{10,2},{3,11},{11,3},{4,12},{12,4},... | collective-permute-start | bytes 1572872 | tf_op jit(solution)/shard_map/ppermute | solution.py:32
  32.9 3.3 %collective-permute-start.2 = (bf16[80,1024]{1,0:T(8,128)(2,1)S(1)}, bf16[80,1024]{1,0:T(8,128)(2,1)S(1)}, u32[]{:S(2)}, u32[]{:S(2)}) collective-permute-start(bf16[80,1024]{1,0:T(8,128)(2,1)S(1)} %maximum_maximum_fusion.refs_4_.w_ref), channel_id=1, source_target_pairs={{0,8},{8,0},{1,9},{9,1},{2,10},{10,2},{3,11},{11,3},{4,12},{12,4},... | collective-permute-start | bytes 491528 | tf_op jit(solution)/shard_map/ppermute | solution.py:32
  43.5 15.8 %all-to-all-start.2 = ((bf16[16,32,128]{2,1,0:T(8,128)(2,1)}), bf16[16,32,128]{2,1,0:T(8,128)(2,1)S(1)}, u32[]{:S(2)}, u32[]{:S(2)}) async-start(bf16[16,32,128]{2,1,0:T(8,128)(2,1)} %bitcast.6), calls=%async_computation.2 | async-start | bytes 262144 | tf_op jit(solution)/shard_map/all_to_all | solution.py:49
  51.1 31.7 %copy-start.11 = (f32[4,256]{1,0:T(4,128)S(1)}, f32[4,256]{1,0:T(4,128)}, u32[]{:S(2)}) copy-start(f32[4,256]{1,0:T(4,128)} %param.23) | copy-start | bytes 12292
  51.1 31.7 %copy-start.12 = (f32[256]{0:T(256)S(1)}, f32[256]{0:T(256)}, u32[]{:S(2)}) copy-start(f32[256]{0:T(256)} %param.31) | copy-start | bytes 3076
  55.0 35.5 %copy-start.4 = (bf16[240,1024]{1,0:T(8,128)(2,1)S(1)}, bf16[240,1024]{1,0:T(8,128)(2,1)}, u32[]{:S(2)}) copy-start(bf16[240,1024]{1,0:T(8,128)(2,1)} %constant.17.clone.orders_ref) | copy-start | bytes 1474564
  55.0 35.5 %copy-start.5 = (bf16[24,3,256]{2,0,1:T(8,128)(2,1)S(1)}, bf16[24,3,256]{2,0,1:T(8,128)(2,1)}, u32[]{:S(2)}) copy-start(bf16[24,3,256]{2,0,1:T(8,128)(2,1)} %param.25) | copy-start | bytes 110596
  59.8 30.6 %all-to-all-start.3 = ((bf16[16,64,512]{2,1,0:T(8,128)(2,1)}), bf16[16,64,512]{2,1,0:T(8,128)(2,1)S(1)}, u32[]{:S(2)}, u32[]{:S(2)}) async-start(bf16[16,64,512]{2,1,0:T(8,128)(2,1)} %bitcast.11), calls=%async_computation.3 | async-start | bytes 2097152 | tf_op jit(solution)/shard_map/all_to_all | solution.py:49
  63.7 25.3 %collective-permute-start.7 = (bf16[256,1024]{1,0:T(8,128)(2,1)S(1)}, bf16[256,1024]{1,0:T(8,128)(2,1)S(1)}, u32[]{:S(2)}, u32[]{:S(2)}) collective-permute-start(bf16[256,1024]{1,0:T(8,128)(2,1)S(1)} %copy-done.1), channel_id=1, source_target_pairs={{0,16},{16,32},{32,48},{48,0},{1,17},{17,33},{33,49},{49,1},{2,18}... | collective-permute-start | bytes 1572872 | tf_op jit(solution)/shard_map/ppermute | solution.py:362
  66.1 22.9 %collective-permute-start.8 = (bf16[256,1024]{1,0:T(8,128)(2,1)S(1)}, bf16[256,1024]{1,0:T(8,128)(2,1)S(1)}, u32[]{:S(2)}, u32[]{:S(2)}) collective-permute-start(bf16[256,1024]{1,0:T(8,128)(2,1)S(1)} %copy-done.1), channel_id=1, source_target_pairs={{0,48},{16,0},{32,16},{48,32},{1,49},{17,1},{33,17},{49,33},{2,50}... | collective-permute-start | bytes 1572872 | tf_op jit(solution)/shard_map/ppermute | solution.py:362
  70.7 3.1 %collective-permute-start.3 = (bf16[64,128]{1,0:T(8,128)(2,1)S(1)}, bf16[64,128]{1,0:T(8,128)(2,1)S(1)}, u32[]{:S(2)}, u32[]{:S(2)}) collective-permute-start(bf16[64,128]{1,0:T(8,128)(2,1)S(1)} %get-tuple-element.21), channel_id=1, source_target_pairs={{0,8},{8,0},{1,9},{9,1},{2,10},{10,2},{3,11},{11,3},{4,12},{12,4},... | collective-permute-start | bytes 49160 | tf_op jit(solution)/shard_map/ppermute | solution.py:32
  73.8 9.0 %collective-permute-start.4 = (bf16[2,64,128]{2,1,0:T(8,128)(2,1)S(1)}, bf16[2,64,128]{2,1,0:T(8,128)(2,1)S(1)}, u32[]{:S(2)}, u32[]{:S(2)}) collective-permute-start(bf16[2,64,128]{2,1,0:T(8,128)(2,1)S(1)} %pad_maximum_fusion.bc_0), channel_id=1, source_target_pairs={{0,16},{16,32},{32,48},{48,0},{1,17},{17,33},{33,49},{49,1},{2,18}... | collective-permute-start | bytes 98312 | tf_op jit(solution)/shard_map/ppermute | solution.py:45
  75.7 7.3 %collective-permute-start.5 = (bf16[2,64,128]{2,1,0:T(8,128)(2,1)S(1)}, bf16[2,64,128]{2,1,0:T(8,128)(2,1)S(1)}, u32[]{:S(2)}, u32[]{:S(2)}) collective-permute-start(bf16[2,64,128]{2,1,0:T(8,128)(2,1)S(1)} %pad_maximum_fusion.bc_0), channel_id=1, source_target_pairs={{0,32},{16,48},{32,0},{48,16},{1,33},{17,49},{33,1},{49,17},{2,34}... | collective-permute-start | bytes 98312 | tf_op jit(solution)/shard_map/ppermute | solution.py:45
  79.1 6.4 %collective-permute-start.6 = (bf16[2,64,128]{2,1,0:T(8,128)(2,1)S(1)}, bf16[2,64,128]{2,1,0:T(8,128)(2,1)S(1)}, u32[]{:S(2)}, u32[]{:S(2)}) collective-permute-start(bf16[2,64,128]{2,1,0:T(8,128)(2,1)S(1)} %pad_maximum_fusion.bc_0), channel_id=1, source_target_pairs={{0,48},{16,0},{32,16},{48,32},{1,49},{17,1},{33,17},{49,33},{2,50}... | collective-permute-start | bytes 98312 | tf_op jit(solution)/shard_map/ppermute | solution.py:45
  92.1 24.6 %all-to-all-start.4 = ((bf16[32,32,256]{2,1,0:T(8,128)(2,1)}), bf16[32,32,256]{2,1,0:T(8,128)(2,1)S(1)}, u32[]{:S(2)}, u32[]{:S(2)}) async-start(bf16[32,32,256]{2,1,0:T(8,128)(2,1)} %bitcast.17), calls=%async_computation.4 | async-start | bytes 1048576 | tf_op jit(solution)/shard_map/all_to_all | solution.py:49
  99.9 14.0 %collective-permute-start.9 = (bf16[128,1024]{1,0:T(8,128)(2,1)S(1)}, bf16[128,1024]{1,0:T(8,128)(2,1)S(1)}, u32[]{:S(2)}, u32[]{:S(2)}) collective-permute-start(bf16[128,1024]{1,0:T(8,128)(2,1)S(1)} %slice.6), channel_id=1, source_target_pairs={{0,16},{16,32},{32,48},{48,0},{1,17},{17,33},{33,49},{49,1},{2,18}... | collective-permute-start | bytes 786440 | tf_op jit(solution)/shard_map/ppermute | solution.py:379
  103.4 11.4 %collective-permute-start.10 = (bf16[128,1024]{1,0:T(8,128)(2,1)S(1)}, bf16[128,1024]{1,0:T(8,128)(2,1)S(1)}, u32[]{:S(2)}, u32[]{:S(2)}) collective-permute-start(bf16[128,1024]{1,0:T(8,128)(2,1)S(1)} %slice.7), channel_id=1, source_target_pairs={{0,48},{16,0},{32,16},{48,32},{1,49},{17,1},{33,17},{49,33},{2,50}... | collective-permute-start | bytes 786440 | tf_op jit(solution)/shard_map/ppermute | solution.py:380
  117.8 3.4 %collective-permute-start.11 = (bf16[8,16,1024]{2,1,0:T(8,128)(2,1)S(1)}, bf16[8,16,1024]{2,1,0:T(8,128)(2,1)S(1)}, u32[]{:S(2)}, u32[]{:S(2)}) collective-permute-start(bf16[8,16,1024]{2,1,0:T(8,128)(2,1)S(1)} %shard_map.169), channel_id=1, source_target_pairs={{0,8},{8,0},{1,9},{9,1},{2,10},{10,2},{3,11},{11,3},{4,12},{12,4},... | collective-permute-start | bytes 786440 | tf_op jit(solution)/shard_map/ppermute | solution.py:32
  (8 other events, 142.8 us)
